TPU v7x, 32 devices: a whole 2x2x4 slice. The times are simulated.
32 devices in a mesh: seq: 8 (over z, y), head: 4 (over x, core).
Axes of the slice: x: 2, y: 2, z: 4, core: 2. Of those that a mesh axis runs over, the one named last changes fastest.
Arguments:
- queries: bfloat16 [4096, 4096], P(('seq', 'head')), may hold values from -52 to 52
- keys: bfloat16 [4096, 4096], P(('seq', 'head')), may hold values from -4 to 4
- values: bfloat16 [4096, 4096], P(('seq', 'head')), may hold values from -32 to 32
- grad_out: bfloat16 [4096, 4096], P(('seq', 'head')), may hold values from -64 to 64
- rand_blocks: int32 [32, 64, 3], P('head', 'seq'), may hold values from 0 to 63, as said below
- global_ids: int32 [2], replicated, may hold values from 0 to 63
- drop_mask: int32 [32, 64, 8], P('head', 'seq'), may hold values 0 or 1
Outputs:
- attended: bfloat16 [4096, 4096], P('seq', 'head')
- grad_queries: bfloat16 [4096, 4096], P('seq', 'head')
- grad_keys: bfloat16 [4096, 4096], P('seq', 'head')
- grad_values: bfloat16 [4096, 4096], P('seq', 'head')
Inputs may be any that keep to these rules, and one draw needn't show every extreme that they name: `rand_blocks`: for every sequence shard s (query blocks s * 8 onward) and head group g (heads g * 8 onward), the 192 listed random blocks come from a g-dependent hot shard exactly 30 times, and from no shard more than 30 times; the rest spread evenly over the other shards; the hot shard is the same for all s of one head group.
All inputs are finite; a program needn't handle non-finite values. No bound on the sum of `drop_mask` on one device may be relied on, other than what follows from the above.
Results may differ from a plain program's by a relative error of at most 0.015.
Values may be sent and summed in bfloat16 or wider, within the bound.
No kernel may reach another device: no remote copies, remote signals or barrier semaphores. Data moves between devices by JAX's collectives and lax.ppermute only.
A program may use at most 128 MiB of HBM per device.

v0:
```python
import functools
import math

import jax
import jax.numpy as jnp
from jax import lax
from jax.experimental import pallas as pl
from jax.experimental.pallas import tpu as pltpu
from jax.sharding import PartitionSpec as P

HEAD_WIDTH = 128
BLOCK_TOKENS = 64
R = 3
G = 2
SLOTS = 3 + G + R
WIDE = SLOTS * BLOCK_TOKENS
UNROLL = 2
STRIP = 16
VMEM_LIMIT = 56 * 1024 * 1024

keep_prob = 0.9

vmem = pl.BlockSpec(memory_space=pltpu.VMEM)
smem = pl.BlockSpec(memory_space=pltpu.SMEM)


def copy_cost(size):
    return pl.CostEstimate(flops=0, bytes_accessed=4 * size, transcendentals=0)


def block_rows(number):
    start = number * BLOCK_TOKENS
    if not isinstance(number, int):
        start = pl.multiple_of(start, BLOCK_TOKENS)
    return pl.ds(start, BLOCK_TOKENS)


def pack_kernel(heads, table_rows, *refs):
    refs = list(refs)
    if table_rows:
        drop_ref, rand_ref, table = refs.pop(0), refs.pop(0), refs.pop()
    out_ref = refs.pop()
    begin = 0
    for ref in refs:
        rows = ref.shape[0]
        for m in range(heads):
            out_ref[m, 0, pl.ds(begin, rows), :] = ref[:, pl.ds(m * HEAD_WIDTH, HEAD_WIDTH)]
        begin += rows
    if table_rows:
        blocks = drop_ref.shape[1]
        table[...] = jnp.zeros_like(table)
        for m in range(heads):
            table[pl.ds(0, blocks), pl.ds(0, SLOTS)] = drop_ref[m].astype(jnp.float32)
            for r in range(R):
                table[pl.ds(blocks + r, 1), pl.ds(0, blocks)] = rand_ref[
                    r, pl.ds(m, 1), :
                ].astype(jnp.float32)
            out_ref[m, 0, pl.ds(begin, table_rows), :] = table[...].astype(jnp.bfloat16)


def pack(groups, heads, sources, tables=(), table_rows=0):
    specs = [pl.BlockSpec(t.shape, lambda g: (0, 0, 0)) for t in tables]
    for _, at, rows in sources:
        specs.append(
            pl.BlockSpec((rows, heads * HEAD_WIDTH), functools.partial(lambda at, g: (at, g), at))
        )
    total = sum(rows for _, _, rows in sources) + table_rows
    shape = (heads, groups, total, HEAD_WIDTH)
    packed = pl.pallas_call(
        functools.partial(pack_kernel, heads, table_rows),
        grid=(groups,),
        out_shape=jax.ShapeDtypeStruct(shape, jnp.bfloat16),
        in_specs=specs,
        out_specs=pl.BlockSpec((heads, 1, total, HEAD_WIDTH), lambda g: (0, g, 0, 0)),
        scratch_shapes=[pltpu.VMEM((table_rows, HEAD_WIDTH), jnp.float32)] if table_rows else [],
        compiler_params=pltpu.CompilerParams(vmem_limit_bytes=VMEM_LIMIT),
        cost_estimate=copy_cost(math.prod(shape)),
    )(*tables, *[array for array, _, _ in sources])
    return packed.reshape(heads * groups, total, HEAD_WIDTH)


def unpack_kernel(parts, member_ref, *refs):
    outs = refs[len(refs) - len(parts) :]
    heads = outs[0].shape[-1] // HEAD_WIDTH
    for k in range(heads):
        column = pl.multiple_of((member_ref[0] ^ k) * HEAD_WIDTH, HEAD_WIDTH)
        for begin, out in zip(parts, outs):
            runs, _, rows, _ = out.shape
            for i in range(runs):
                out[i, 0, :, pl.ds(column, HEAD_WIDTH)] = refs[k][pl.ds(begin + i * rows, rows), :]


def unpack(member, received, parts):
    heads = len(received)
    shapes, specs, olds, aliases, size = [], [], [], {}, 0
    for n, (_, rows, runs, pieces, piece, old) in enumerate(parts):
        shapes.append(
            jax.ShapeDtypeStruct((runs, pieces, rows, heads * HEAD_WIDTH), jnp.bfloat16)
        )
        specs.append(
            pl.BlockSpec(
                (runs, 1, rows, heads * HEAD_WIDTH),
                functools.partial(lambda piece, h: (0, piece, 0, 0), piece),
            )
        )
        size += rows * runs * heads * HEAD_WIDTH
        if old is not None:
            aliases[1 + heads + len(olds)] = n
            olds.append(old)
    return pl.pallas_call(
        functools.partial(unpack_kernel, tuple(part[0] for part in parts)),
        grid=(1,),
        out_shape=shapes,
        in_specs=[smem]
        + [pl.BlockSpec(received[0].shape, lambda h: (0, 0))] * heads
        + [pl.BlockSpec(memory_space=pl.ANY)] * len(olds),
        out_specs=specs,
        input_output_aliases=aliases,
        compiler_params=pltpu.CompilerParams(vmem_limit_bytes=VMEM_LIMIT),
        cost_estimate=copy_cost(size),
    )(member, *received, *olds)


def attention_kernel(
    last_block,
    device_blocks,
    per,
    piece,
    out_rows,
    source_rows,
    qd_rows,
    qd_begin,
    has_qd,
    has_start,
    joined,
    tokens,
    targets,
    ids_ref,
    starts_ref,
    first_ref,
    member_ref,
    drop_ref,
    kv_ref,
    *refs,
):
    refs = list(refs)
    qd_ref = refs.pop(0) if has_qd else kv_ref
    start_ref = refs.pop(0) if has_start else None
    out_refs = [refs.pop(0) for _ in range(targets)]
    acc, retain, waiting, near = refs
    scale = HEAD_WIDTH ** (-0.5)
    steps = targets * (out_rows // BLOCK_TOKENS)
    slot_of_lane = lax.broadcasted_iota(jnp.int32, (SLOTS, WIDE), 1) // BLOCK_TOKENS
    slot_row = lax.broadcasted_iota(jnp.int32, (SLOTS, WIDE), 0)
    expand = (slot_of_lane == slot_row).astype(jnp.float32)
    retain[...] = jnp.dot(
        drop_ref[...].astype(jnp.float32), expand, preferred_element_type=jnp.float32
    ) * (1.0 / keep_prob)
    acc[...] = start_ref[...] if has_start else jnp.zeros_like(acc)
    lane = lax.broadcasted_iota(jnp.int32, (1, WIDE), 1)
    nt = (((1,), (1,)), ((), ()))
    tn = (((0,), (0,)), ((), ()))
    out_steps = steps // targets

    def place(i):
        if per == 1:
            source, sub = i, 0
        else:
            source, sub = lax.div(i, per), lax.rem(i, per)
        return source, sub, source * device_blocks + piece * per + sub

    def load(i):
        source, sub, j = place(i)
        starts = [starts_ref[j * SLOTS + s] for s in range(SLOTS)]
        q, do = [
            qd_ref[
                pl.ds(
                    pl.multiple_of(
                        source * qd_rows + (n * per + sub) * BLOCK_TOKENS + qd_begin, 16
                    ),
                    BLOCK_TOKENS,
                ),
                :,
            ]
            for n in range(2)
        ]
        keys, vals = [
            jnp.concatenate(
                [kv_ref[pl.ds(pl.multiple_of(r + n * tokens, 16), BLOCK_TOKENS), :] for r in starts],
                axis=0,
            )
            for n in range(2)
        ]
        return q, do, keys, vals

    def score(i):
        q, do, keys, vals = load(i)
        logits = lax.dot_general(q, keys, nt, preferred_element_type=jnp.float32)
        raw = lax.dot_general(do, vals, nt, preferred_element_type=jnp.float32)
        return logits, raw

    def factor(i, u, logits, raw):
        j = place(i)[2]
        block_id = first_ref[0] + j
        absent = ((block_id == 0) & (lane < BLOCK_TOKENS)) | (
            (block_id == last_block) & (lane >= 2 * BLOCK_TOKENS) & (lane < 3 * BLOCK_TOKENS)
        )
        keep = retain[pl.ds(j, 1), :]
        for r in range(0, BLOCK_TOKENS, STRIP):
            part = jnp.where(absent, -jnp.inf, logits[r : r + STRIP])
            top = jnp.max(part, axis=-1, keepdims=True)
            expd = jnp.exp2((part - top) * (scale / math.log(2.0)))
            probs = expd * (1.0 / jnp.sum(expd, axis=-1, keepdims=True))
            kept = probs * keep
            weighted = kept * raw[r : r + STRIP]
            delta = jnp.sum(weighted, axis=-1, keepdims=True)
            waiting[u, pl.ds(r, STRIP), :] = (weighted - probs * delta).astype(jnp.bfloat16)
            waiting[u, pl.ds(BLOCK_TOKENS + r, STRIP), :] = kept.astype(jnp.bfloat16)

    def finish(i, u):
        j = place(i)[2]
        q, do, keys, vals = load(i)
        factors = waiting[u]
        dq = jnp.dot(factors[:BLOCK_TOKENS], keys, preferred_element_type=jnp.float32) * scale
        att = jnp.dot(factors[BLOCK_TOKENS:], vals, preferred_element_type=jnp.float32)
        none = jnp.zeros_like(q)
        pair = jnp.concatenate(
            [jnp.concatenate([q, none], axis=1), jnp.concatenate([none, do], axis=1)], axis=0
        )
        terms = lax.dot_general(factors, pair, tn, preferred_element_type=jnp.float32)
        for s in range(SLOTS):
            acc[block_rows(ids_ref[j * SLOTS + s]), :] += terms[
                s * BLOCK_TOKENS : (s + 1) * BLOCK_TOKENS
            ]
        target, pos = lax.div(i, out_steps), lax.rem(i, out_steps)
        near[target, block_rows(pos), :] = att.astype(jnp.bfloat16)
        near[target, block_rows(out_steps + pos), :] = dq.astype(jnp.bfloat16)

    def step(t, carry):
        scores = [score(t * UNROLL + u) for u in range(UNROLL)]
        for u in range(UNROLL):
            finish((t - 1) * UNROLL + u, u)
        for u in range(UNROLL):
            factor(t * UNROLL + u, u, *scores[u])
        return carry

    for u in range(UNROLL):
        factor(u, u, *score(u))
    lax.fori_loop(1, steps // UNROLL, step, 0)
    for u in range(UNROLL):
        finish(steps - UNROLL + u, u)
    for k, out_ref in enumerate(out_refs):
        target = member_ref[0] ^ k
        out_ref[pl.ds(0, 2 * out_rows), :] = near[target]
        if joined:
            rows = acc.shape[0] // targets
            part = pl.ds(pl.multiple_of(target * rows, rows), rows)
            out_ref[pl.ds(2 * out_rows, rows), :] = (acc[part, :HEAD_WIDTH] * scale).astype(
                jnp.bfloat16
            )
            out_ref[pl.ds(2 * out_rows + rows, rows), :] = acc[part, HEAD_WIDTH:].astype(
                jnp.bfloat16
            )


def attend(
    ids, starts, first_block, member, drop, kv, qd, qd_begin, start, piece, per, joined, device_blocks, total_blocks, tokens, targets
):
    team_blocks = drop.shape[0]
    source = kv if qd is None else qd
    steps = team_blocks * per // device_blocks
    length = total_blocks * BLOCK_TOKENS
    pairs = steps * BLOCK_TOKENS * WIDE
    accumulator = (length, 2 * HEAD_WIDTH)
    out_rows = steps * BLOCK_TOKENS // targets
    total_rows = 2 * out_rows + (2 * length // targets if joined else 0)
    out_shape = [jax.ShapeDtypeStruct((total_rows, HEAD_WIDTH), jnp.bfloat16)] * targets
    scratch = [
        pltpu.VMEM((team_blocks, WIDE), jnp.float32),
        pltpu.VMEM((UNROLL, 2 * BLOCK_TOKENS, WIDE), jnp.bfloat16),
        pltpu.VMEM((targets, 2 * out_rows, HEAD_WIDTH), jnp.bfloat16),
    ]
    if joined:
        scratch = [pltpu.VMEM(accumulator, jnp.float32)] + scratch
    else:
        out_shape.append(jax.ShapeDtypeStruct(accumulator, jnp.float32))
    flat = [t.reshape(-1, HEAD_WIDTH) for t in (kv, qd) if t is not None]
    operands = flat + ([] if start is None else [start])
    return pl.pallas_call(
        functools.partial(
            attention_kernel,
            total_blocks - 1,
            device_blocks,
            per,
            piece,
            out_rows,
            kv.shape[1],
            source.shape[1],
            qd_begin,
            qd is not None,
            start is not None,
            joined,
            tokens,
            targets,
        ),
        out_shape=out_shape,
        in_specs=[smem, smem, smem, smem, vmem] + [vmem] * len(operands),
        out_specs=[vmem] * len(out_shape),
        scratch_shapes=scratch,
        compiler_params=pltpu.CompilerParams(vmem_limit_bytes=VMEM_LIMIT),
        cost_estimate=pl.CostEstimate(
            flops=12 * pairs * HEAD_WIDTH,
            bytes_accessed=2 * (source.size + kv.size) + 8 * length * HEAD_WIDTH,
            transcendentals=pairs,
        ),
    )(ids, starts, first_block, member, drop, *operands)


def per_device(queries, keys, values, grad_out, rand_blocks, global_ids, drop_mask):
    shards = lax.axis_size("seq")
    groups = lax.axis_size("head")
    shard = lax.axis_index("seq")
    heads, shard_blocks, _ = rand_blocks.shape
    tokens = queries.shape[0]
    device_blocks = tokens // BLOCK_TOKENS
    shard_tokens = shard_blocks * BLOCK_TOKENS
    teams = shards // heads
    team, member = lax.div(shard, heads), lax.rem(shard, heads)
    team_blocks = heads * shard_blocks
    total_blocks = shards * shard_blocks
    first_block = team * team_blocks
    whole = teams == 1
    pieces = device_blocks if whole else 1
    per = device_blocks // pieces
    rows = tokens // pieces
    same_team_all = (
        None
        if whole
        else [
            [(t * heads + m) * groups + g for m in range(heads) for g in range(groups)]
            for t in range(teams)
        ]
    )
    same_head = [[t * heads + m for t in range(teams)] for m in range(heads)]

    def to_heads(packed):
        return lax.all_to_all(
            packed,
            ("seq", "head"),
            split_axis=0,
            concat_axis=0,
            tiled=True,
            axis_index_groups=same_team_all,
        )

    def to_shards(results):
        received = list(results)
        for k in reversed(range(1, heads)):
            pairs = [(s, s ^ k) for s in range(shards)]
            received[k] = lax.ppermute(results[k], "seq", pairs)
        return received

    table_rows = -(-(shard_blocks + R) // 16) * 16
    sources = [[(queries, c, rows), (grad_out, c, rows)] for c in range(pieces)]
    qd_begin = 2 * tokens
    table_begin = qd_begin + 2 * rows
    kv = to_heads(
        pack(
            groups,
            heads,
            [(keys, 0, tokens), (values, 0, tokens)] + sources[0],
            (drop_mask, rand_blocks.transpose(2, 0, 1)),
            table_rows,
        )
    )
    later = [to_heads(pack(groups, heads, each)) for each in sources[1:]]
    tables = lax.dynamic_index_in_dim(
        kv.reshape(heads, groups, -1, HEAD_WIDTH)[:, :, table_begin:],
        lax.axis_index("head"),
        axis=1,
        keepdims=False,
    ).astype(jnp.int32)
    drops = tables[:, :shard_blocks, :SLOTS].reshape(team_blocks, SLOTS)
    randoms = tables[:, shard_blocks : shard_blocks + R, :shard_blocks].transpose(0, 2, 1)
    randoms = randoms.reshape(team_blocks, R)
    qd = [None] + later
    if not whole:
        qd[0] = kv[:, qd_begin:table_begin]
        kv = lax.all_gather(kv[:, : 2 * tokens], "seq", axis=0, tiled=True, axis_index_groups=same_head)
    blocks = first_block + jnp.arange(team_blocks, dtype=jnp.int32)
    window = jnp.stack([blocks - 1, blocks, blocks + 1], axis=1)
    listed = jnp.concatenate(
        [window, jnp.broadcast_to(global_ids[None], (team_blocks, G)), randoms], axis=1
    )
    listed = jnp.clip(listed, 0, total_blocks - 1).reshape(-1)
    starts = listed // device_blocks * kv.shape[1] + listed % device_blocks * BLOCK_TOKENS
    near = []
    sums = None
    for c in range(pieces):
        results = attend(
            listed,
            starts,
            first_block.reshape(1),
            member.reshape(1),
            drops,
            kv,
            qd[c],
            qd_begin if qd[c] is None else 0,
            sums[0] if sums else None,
            c,
            per,
            whole and c == pieces - 1,
            device_blocks,
            total_blocks,
            tokens,
            heads,
        )
        near.append(to_shards(results[:heads]))
        sums = results[heads:]
    runs = shard_blocks // device_blocks
    att, dq = None, None
    for c in range(pieces):
        begin = shard_tokens // pieces
        parts = [(0, rows, runs, pieces, c, att), (begin, rows, runs, pieces, c, dq)]
        if c < pieces - 1:
            att, dq = unpack(member.reshape(1), near[c], parts)
        elif whole:
            grads = [(2 * begin + n * shard_tokens, shard_tokens, 1, 1, 0, None) for n in range(2)]
            att, dq, dk, dv = unpack(member.reshape(1), near[c], parts + grads)
        else:
            att, dq = unpack(member.reshape(1), near[c], parts)
            grads = lax.psum_scatter(
                sums[0], "seq", scatter_dimension=0, tiled=True, axis_index_groups=same_head
            ).reshape(heads, shard_tokens, 2, HEAD_WIDTH)
            grads = jnp.concatenate(
                [grads[:, :, 0] * HEAD_WIDTH ** (-0.5), grads[:, :, 1]], axis=1
            ).astype(jnp.bfloat16)
            grads = to_shards(
                [lax.dynamic_index_in_dim(grads, member ^ k, 0, keepdims=False) for k in range(heads)]
            )
            dk, dv = unpack(
                member.reshape(1), grads, [(n * shard_tokens, shard_tokens, 1, 1, 0, None) for n in range(2)]
            )
    return tuple(t.reshape(shard_tokens, heads * HEAD_WIDTH) for t in (att, dq, dk, dv))


def solution(mesh):
    return jax.shard_map(
        per_device,
        mesh=mesh,
        in_specs=(
            P(("seq", "head"), None),
            P(("seq", "head"), None),
            P(("seq", "head"), None),
            P(("seq", "head"), None),
            P("head", "seq", None),
            P(),
            P("head", "seq", None),
        ),
        out_specs=(P("seq", "head"), P("seq", "head"), P("seq", "head"), P("seq", "head")),
        check_vma=False,
    )
```

profile of v0, /device:TPU:9, one launch (start us, length us, event | category | flops | bytes accessed | tf_op | source)
XLA Modules:
  0.0 243.3 jit_solution(858225309618498884)
XLA Ops:
  0.6 4.5 %shard_map.102 = bf16[8,4,400,128]{3,2,1,0:T(8,128)(2,1)} custom-call(s32[8,8,8]{2,1,0:T(8,128)} %refs_0_.2, s32[3,8,8]{2,1,0:T(8,128)} %bitcast.28, bf16[128,4096]{1,0:T(8,128)(2,1)} %refs_2_.1, bf16[128,4096]{1,0:T(8,128)(2,1)} %refs_3_.1, bf16[128,4096]{1,0:T(8,128)(2,1)} %refs_0_.3, bf16[128,4096]{1,0:T(8,128)(2,1)} %refs_1_.1), custom_call_target="tpu_custom_call" | custom-call | bytes 6553600 | tf_op jit(solution)/shard_map/pallas_call | solution.py:69
  5.2 6.4 %all-to-all-start = ((bf16[32,400,128]{2,1,0:T(8,128)(2,1)}), bf16[32,400,128]{2,1,0:T(8,128)(2,1)S(1)}, u32[]{:S(2)}, u32[]{:S(2)}) async-start(bf16[32,400,128]{2,1,0:T(8,128)(2,1)} %bitcast.24), calls=%async_computation | async-start | bytes 6553600 | tf_op jit(solution)/shard_map/all_to_all | solution.py:347
  11.5 0.0 copy-start.22
  11.5 3.5 %shard_map.103 = bf16[8,4,128,128]{3,2,1,0:T(8,128)(2,1)} custom-call(bf16[128,4096]{1,0:T(8,128)(2,1)} %refs_0_.3, bf16[128,4096]{1,0:T(8,128)(2,1)} %refs_1_.1), custom_call_target="tpu_custom_call" | custom-call | bytes 2097152 | tf_op jit(solution)/shard_map/pallas_call | solution.py:69
  15.0 68.2 %all-to-all-done = bf16[32,400,128]{2,1,0:T(8,128)(2,1)S(1)} async-done(((bf16[32,400,128]{2,1,0:T(8,128)(2,1)}), bf16[32,400,128]{2,1,0:T(8,128)(2,1)S(1)}, u32[]{:S(2)}, u32[]{:S(2)}) %all-to-all-start) | async-done | bytes 3276832 | tf_op jit(solution)/shard_map/all_to_all | solution.py:347
  83.2 6.5 %all-to-all-start.1 = ((bf16[32,128,128]{2,1,0:T(8,128)(2,1)}), bf16[32,128,128]{2,1,0:T(8,128)(2,1)}, u32[]{:S(2)}, u32[]{:S(2)}) async-start(bf16[32,128,128]{2,1,0:T(8,128)(2,1)} %bitcast.25), calls=%async_computation.1 | async-start | bytes 2097152 | tf_op jit(solution)/shard_map/all_to_all | solution.py:347
  89.9 0.1 reshape.78
  90.0 0.0 copy-done.22
  90.0 0.1 broadcast_in_dim.2
  90.1 0.1 copy.17
  90.2 0.1 min.12.ids_ref
  90.3 0.6 fusion.1.starts_ref
  90.9 0.6 slice_bitcast_fusion.drop_ref
  91.5 14.3 %shard_map.104 = (bf16[512,128]{1,0:T(8,128)(2,1)}, bf16[512,128]{1,0:T(8,128)(2,1)}, bf16[512,128]{1,0:T(8,128)(2,1)}, bf16[512,128]{1,0:T(8,128)(2,1)}, bf16[5...) custom-call(s32[512]{0:T(512)} %copy-done.15, ...), custom_call_target="tpu_custom_call" | custom-call | flops 1610612736 | bytes 10747904 | tf_op jit(solution)/shard_map/pallas_call | solution.py:289
  105.8 1.2 collective-permute-start.7
  107.0 8.1 %all-to-all-done.1 = bf16[32,128,128]{2,1,0:T(8,128)(2,1)} async-done(((bf16[32,128,128]{2,1,0:T(8,128)(2,1)}), bf16[32,128,128]{2,1,0:T(8,128)(2,1)}, u32[]{:S(2)}, u32[]{:S(2)}) %all-to-all-start.1) | async-done | bytes 1048608 | tf_op jit(solution)/shard_map/all_to_all | solution.py:347
  115.1 15.6 %shard_map.105 = (bf16[1536,128]{1,0:T(8,128)(2,1)}, bf16[1536,128]{1,0:T(8,128)(2,1)}, bf16[1536,128]{1,0:T(8,128)(2,1)}, bf16[1536,128]{1,0:T(8,128)(2,1)}, bf...) custom-call(s32[512]{0:T(512)} %copy-done.15, ...), custom_call_target="tpu_custom_call" | custom-call | flops 1610612736 | bytes 8519680 | tf_op jit(solution)/shard_map/pallas_call | solution.py:289
  130.7 0.0 collective-permute-start
  130.7 1.5 collective-permute-start.1
  132.2 0.1 collective-permute-start.8
  132.2 1.3 collective-permute-start.9
  133.5 0.0 collective-permute-done.7.refs_1_
  133.5 2.0 collective-permute-start.10
  135.5 9.6 %collective-permute-done.8.refs_2_ = bf16[512,128]{1,0:T(8,128)(2,1)S(1)} collective-permute-done((bf16[512,128]{1,0:T(8,128)(2,1)S(1)}, bf16[512,128]{1,0:T(8,128)(2,1)S(1)}, u32[]{:S(2)}, u32[]{:S(2)}) %collective-permute-start.8) | collective-permute-done | bytes 131104 | tf_op jit(solution)/shard_map/ppermute | solution.py:360
  145.1 3.3 %collective-permute-start.11 = (bf16[512,128]{1,0:T(8,128)(2,1)S(1)}, bf16[512,128]{1,0:T(8,128)(2,1)S(1)}, u32[]{:S(2)}, u32[]{:S(2)}) collective-permute-start(bf16[512,128]{1,0:T(8,128)(2,1)S(1)} %copy-done.18), channel_id=1, source_target_pairs={{0,20},{4,16},{8,28},{12,24},{16,4},{20,0},{24,12},{28,8},{1,21},{... | collective-permute-start | bytes 393224 | tf_op jit(solution)/shard_map/ppermute | solution.py:360
  148.3 0.0 collective-permute-done.9.refs_3_
  148.4 1.1 collective-permute-start.12
  149.5 0.8 collective-permute-done.10.refs_4_
  150.2 1.5 collective-permute-start.13
  151.8 8.5 %collective-permute-done.11.refs_5_ = bf16[512,128]{1,0:T(8,128)(2,1)S(1)} collective-permute-done((bf16[512,128]{1,0:T(8,128)(2,1)S(1)}, bf16[512,128]{1,0:T(8,128)(2,1)S(1)}, u32[]{:S(2)}, u32[]{:S(2)}) %collective-permute-start.11) | collective-permute-done | bytes 131104 | tf_op jit(solution)/shard_map/ppermute | solution.py:360
  160.3 3.9 %collective-permute-start.2 = (bf16[1536,128]{1,0:T(8,128)(2,1)}, bf16[1536,128]{1,0:T(8,128)(2,1)S(1)}, u32[]{:S(2)}, u32[]{:S(2)}) collective-permute-start(bf16[1536,128]{1,0:T(8,128)(2,1)} %get-tuple-element.31), channel_id=1, source_target_pairs={{0,12},{4,8},{8,4},{12,0},{16,28},{20,24},{24,20},{28,16},{1,13},{... | collective-permute-start | bytes 1179656 | tf_op jit(solution)/shard_map/ppermute | solution.py:360
  164.2 0.7 collective-permute-done.12.refs_6_
  164.9 0.0 collective-permute-start.3
  164.9 6.5 %collective-permute-done.13.refs_7_ = bf16[512,128]{1,0:T(8,128)(2,1)S(1)} collective-permute-done((bf16[512,128]{1,0:T(8,128)(2,1)S(1)}, bf16[512,128]{1,0:T(8,128)(2,1)S(1)}, u32[]{:S(2)}, u32[]{:S(2)}) %collective-permute-start.13) | collective-permute-done | bytes 131104 | tf_op jit(solution)/shard_map/ppermute | solution.py:360
  171.4 0.0 collective-permute-start.4
  171.4 0.0 collective-permute-done.refs_1_
  171.4 0.5 collective-permute-start.5
  172.0 0.0 collective-permute-done.1.refs_2_
  172.0 0.0 collective-permute-start.6
  172.0 0.0 copy-done.14
  172.0 2.6 %shard_map.106 = (bf16[4,2,64,1024]{3,2,1,0:T(8,128)(2,1)}, bf16[4,2,64,1024]{3,2,1,0:T(8,128)(2,1)}) custom-call(s32[1]{0:T(128)} %bitcast.member_ref, bf16[512,128]{1,0:T(8,128)(2,1)} %get-tuple-element.36.refs_0_, bf16[512,128]{1,0:T(8,128)(2,1)} %copy-done.8, bf16[512,128]{1,0:T(8,128)(2,1)} %copy-done.9, bf16[512,128]{1,0:T(8,128)(2,1)} %copy-done.10, ...), custom_call_target="tpu_custom_call" | custom-call | bytes 2097152 | tf_op jit(solution)/shard_map/pallas_call | solution.py:110
  174.7 5.4 %collective-permute-done.2.refs_3_ = bf16[1536,128]{1,0:T(8,128)(2,1)S(1)} collective-permute-done((bf16[1536,128]{1,0:T(8,128)(2,1)}, bf16[1536,128]{1,0:T(8,128)(2,1)S(1)}, u32[]{:S(2)}, u32[]{:S(2)}) %collective-permute-start.2) | collective-permute-done | bytes 393248 | tf_op jit(solution)/shard_map/ppermute | solution.py:360
  180.0 4.2 %collective-permute-done.3.refs_4_ = bf16[1536,128]{1,0:T(8,128)(2,1)S(1)} collective-permute-done((bf16[1536,128]{1,0:T(8,128)(2,1)}, bf16[1536,128]{1,0:T(8,128)(2,1)S(1)}, u32[]{:S(2)}, u32[]{:S(2)}) %collective-permute-start.3) | collective-permute-done | bytes 393248 | tf_op jit(solution)/shard_map/ppermute | solution.py:360
  184.2 32.9 %collective-permute-done.4.refs_5_ = bf16[1536,128]{1,0:T(8,128)(2,1)S(1)} collective-permute-done((bf16[1536,128]{1,0:T(8,128)(2,1)}, bf16[1536,128]{1,0:T(8,128)(2,1)S(1)}, u32[]{:S(2)}, u32[]{:S(2)}) %collective-permute-start.4) | collective-permute-done | bytes 393248 | tf_op jit(solution)/shard_map/ppermute | solution.py:360
  217.1 10.3 %collective-permute-done.5.refs_6_ = bf16[1536,128]{1,0:T(8,128)(2,1)S(1)} collective-permute-done((bf16[1536,128]{1,0:T(8,128)(2,1)}, bf16[1536,128]{1,0:T(8,128)(2,1)S(1)}, u32[]{:S(2)}, u32[]{:S(2)}) %collective-permute-start.5) | collective-permute-done | bytes 393248 | tf_op jit(solution)/shard_map/ppermute | solution.py:360
  227.4 10.7 %collective-permute-done.6.refs_7_ = bf16[1536,128]{1,0:T(8,128)(2,1)S(1)} collective-permute-done((bf16[1536,128]{1,0:T(8,128)(2,1)}, bf16[1536,128]{1,0:T(8,128)(2,1)S(1)}, u32[]{:S(2)}, u32[]{:S(2)}) %collective-permute-start.6) | collective-permute-done | bytes 393248 | tf_op jit(solution)/shard_map/ppermute | solution.py:360
  238.2 0.7 copy-done.7
  238.9 4.4 %shard_map.107 = (bf16[4,2,64,1024]{3,2,1,0:T(8,128)(2,1)}, bf16[4,2,64,1024]{3,2,1,0:T(8,128)(2,1)}, bf16[1,1,512,1024]{3,2,1,0:T(8,128)(2,1)}, bf16[1,1,512,1024]{3,2,1,0:T(8,128)(2,1)}) custom-call(s32[1]{0:T(128)} %bitcast.member_ref, bf16[1536,128]{1,0:T(8,128)(2,1)} %get-tuple-element.28.refs_0_, ...), custom_call_target="tpu_custom_call", output_to_operand_aliasing={{0}: (9, {}), {1}: (10, {})} | custom-call | bytes 6291456 | tf_op jit(solution)/shard_map/pallas_call | solution.py:110
  (50 shorter events, 0.2 us)
Async XLA Ops:
  5.2 78.1 %all-to-all-start = ((bf16[32,400,128]{2,1,0:T(8,128)(2,1)}), bf16[32,400,128]{2,1,0:T(8,128)(2,1)S(1)}, u32[]{:S(2)}, u32[]{:S(2)}) async-start(bf16[32,400,128]{2,1,0:T(8,128)(2,1)} %bitcast.24), calls=%async_computation | async-start | bytes 6553600 | tf_op jit(solution)/shard_map/all_to_all | solution.py:347
  11.5 78.4 %copy-start.22 = (s32[2]{0:T(128)S(1)}, s32[2]{0:T(128)}, u32[]{:S(2)}) copy-start(s32[2]{0:T(128)} %param.12) | copy-start | bytes 28
  83.2 8.2 %copy-start = (bf16[32,400,128]{2,1,0:T(8,128)(2,1)}, bf16[32,400,128]{2,1,0:T(8,128)(2,1)S(1)}, u32[]{:S(2)}) copy-start(bf16[32,400,128]{2,1,0:T(8,128)(2,1)S(1)} %all-to-all-done) | copy-start | bytes 9830404
  83.2 31.9 %all-to-all-start.1 = ((bf16[32,128,128]{2,1,0:T(8,128)(2,1)}), bf16[32,128,128]{2,1,0:T(8,128)(2,1)}, u32[]{:S(2)}, u32[]{:S(2)}) async-start(bf16[32,128,128]{2,1,0:T(8,128)(2,1)} %bitcast.25), calls=%async_computation.1 | async-start | bytes 2097152 | tf_op jit(solution)/shard_map/all_to_all | solution.py:347
  90.3 1.2 copy-start.15
  105.8 27.7 %collective-permute-start.7 = (bf16[512,128]{1,0:T(8,128)(2,1)}, bf16[512,128]{1,0:T(8,128)(2,1)S(1)}, u32[]{:S(2)}, u32[]{:S(2)}) collective-permute-start(bf16[512,128]{1,0:T(8,128)(2,1)} %get-tuple-element.37), channel_id=1, source_target_pairs={{0,4},{4,0},{8,12},{12,8},{16,20},{20,16},{24,28},{28,24},{1,5},{5... | collective-permute-start | bytes 393224 | tf_op jit(solution)/shard_map/ppermute | solution.py:360
  115.1 17.1 %copy-start.21 = (bf16[512,128]{1,0:T(8,128)(2,1)S(1)}, bf16[512,128]{1,0:T(8,128)(2,1)}, u32[]{:S(2)}) copy-start(bf16[512,128]{1,0:T(8,128)(2,1)} %get-tuple-element.38) | copy-start | bytes 393220
  115.1 17.1 %copy-start.20 = (bf16[512,128]{1,0:T(8,128)(2,1)S(1)}, bf16[512,128]{1,0:T(8,128)(2,1)}, u32[]{:S(2)}) copy-start(bf16[512,128]{1,0:T(8,128)(2,1)} %get-tuple-element.39) | copy-start | bytes 393220
  115.1 18.4 %copy-start.19 = (bf16[512,128]{1,0:T(8,128)(2,1)S(1)}, bf16[512,128]{1,0:T(8,128)(2,1)}, u32[]{:S(2)}) copy-start(bf16[512,128]{1,0:T(8,128)(2,1)} %get-tuple-element.40) | copy-start | bytes 393220
  115.1 30.0 %copy-start.18 = (bf16[512,128]{1,0:T(8,128)(2,1)S(1)}, bf16[512,128]{1,0:T(8,128)(2,1)}, u32[]{:S(2)}) copy-start(bf16[512,128]{1,0:T(8,128)(2,1)} %get-tuple-element.41) | copy-start | bytes 393220
  115.1 33.2 %copy-start.17 = (bf16[512,128]{1,0:T(8,128)(2,1)S(1)}, bf16[512,128]{1,0:T(8,128)(2,1)}, u32[]{:S(2)}) copy-start(bf16[512,128]{1,0:T(8,128)(2,1)} %get-tuple-element.42) | copy-start | bytes 393220
  115.1 35.1 %copy-start.16 = (bf16[512,128]{1,0:T(8,128)(2,1)S(1)}, bf16[512,128]{1,0:T(8,128)(2,1)}, u32[]{:S(2)}) copy-start(bf16[512,128]{1,0:T(8,128)(2,1)} %get-tuple-element.43) | copy-start | bytes 393220
  130.7 40.7 %collective-permute-start = (bf16[1536,128]{1,0:T(8,128)(2,1)}, bf16[1536,128]{1,0:T(8,128)(2,1)S(1)}, u32[]{:S(2)}, u32[]{:S(2)}) collective-permute-start(bf16[1536,128]{1,0:T(8,128)(2,1)} %get-tuple-element.29), channel_id=1, source_target_pairs={{0,4},{4,0},{8,12},{12,8},{16,20},{20,16},{24,28},{28,24},{1,5},{5... | collective-permute-start | bytes 1179656 | tf_op jit(solution)/shard_map/ppermute | solution.py:360
  130.7 41.2 %collective-permute-start.1 = (bf16[1536,128]{1,0:T(8,128)(2,1)}, bf16[1536,128]{1,0:T(8,128)(2,1)S(1)}, u32[]{:S(2)}, u32[]{:S(2)}) collective-permute-start(bf16[1536,128]{1,0:T(8,128)(2,1)} %get-tuple-element.30), channel_id=1, source_target_pairs={{0,8},{4,12},{8,0},{12,4},{16,24},{20,28},{24,16},{28,20},{1,9},{5... | collective-permute-start | bytes 1179656 | tf_op jit(solution)/shard_map/ppermute | solution.py:360
  132.2 12.9 %collective-permute-start.8 = (bf16[512,128]{1,0:T(8,128)(2,1)S(1)}, bf16[512,128]{1,0:T(8,128)(2,1)S(1)}, u32[]{:S(2)}, u32[]{:S(2)}) collective-permute-start(bf16[512,128]{1,0:T(8,128)(2,1)S(1)} %copy-done.21), channel_id=1, source_target_pairs={{0,8},{4,12},{8,0},{12,4},{16,24},{20,28},{24,16},{28,20},{1,9},{5... | collective-permute-start | bytes 393224 | tf_op jit(solution)/shard_map/ppermute | solution.py:360
  132.2 16.1 %collective-permute-start.9 = (bf16[512,128]{1,0:T(8,128)(2,1)S(1)}, bf16[512,128]{1,0:T(8,128)(2,1)S(1)}, u32[]{:S(2)}, u32[]{:S(2)}) collective-permute-start(bf16[512,128]{1,0:T(8,128)(2,1)S(1)} %copy-done.20), channel_id=1, source_target_pairs={{0,12},{4,8},{8,4},{12,0},{16,28},{20,24},{24,20},{28,16},{1,13},{... | collective-permute-start | bytes 393224 | tf_op jit(solution)/shard_map/ppermute | solution.py:360
  133.5 38.5 %copy-start.8 = (bf16[512,128]{1,0:T(8,128)(2,1)}, bf16[512,128]{1,0:T(8,128)(2,1)S(1)}, u32[]{:S(2)}) copy-start(bf16[512,128]{1,0:T(8,128)(2,1)S(1)} %collective-permute-done.7.refs_1_) | copy-start | bytes 393220
  133.5 16.7 %collective-permute-start.10 = (bf16[512,128]{1,0:T(8,128)(2,1)S(1)}, bf16[512,128]{1,0:T(8,128)(2,1)S(1)}, u32[]{:S(2)}, u32[]{:S(2)}) collective-permute-start(bf16[512,128]{1,0:T(8,128)(2,1)S(1)} %copy-done.19), channel_id=1, source_target_pairs={{0,16},{4,20},{8,24},{12,28},{16,0},{20,4},{24,8},{28,12},{1,17},{... | collective-permute-start | bytes 393224 | tf_op jit(solution)/shard_map/ppermute | solution.py:360
  145.1 26.9 %copy-start.9 = (bf16[512,128]{1,0:T(8,128)(2,1)}, bf16[512,128]{1,0:T(8,128)(2,1)S(1)}, u32[]{:S(2)}) copy-start(bf16[512,128]{1,0:T(8,128)(2,1)S(1)} %collective-permute-done.8.refs_2_) | copy-start | bytes 393220
  145.1 15.2 %collective-permute-start.11 = (bf16[512,128]{1,0:T(8,128)(2,1)S(1)}, bf16[512,128]{1,0:T(8,128)(2,1)S(1)}, u32[]{:S(2)}, u32[]{:S(2)}) collective-permute-start(bf16[512,128]{1,0:T(8,128)(2,1)S(1)} %copy-done.18), channel_id=1, source_target_pairs={{0,20},{4,16},{8,28},{12,24},{16,4},{20,0},{24,12},{28,8},{1,21},{... | collective-permute-start | bytes 393224 | tf_op jit(solution)/shard_map/ppermute | solution.py:360
  148.3 23.6 %copy-start.10 = (bf16[512,128]{1,0:T(8,128)(2,1)}, bf16[512,128]{1,0:T(8,128)(2,1)S(1)}, u32[]{:S(2)}) copy-start(bf16[512,128]{1,0:T(8,128)(2,1)S(1)} %collective-permute-done.9.refs_3_) | copy-start | bytes 393220
  148.4 16.5 %collective-permute-start.12 = (bf16[512,128]{1,0:T(8,128)(2,1)S(1)}, bf16[512,128]{1,0:T(8,128)(2,1)S(1)}, u32[]{:S(2)}, u32[]{:S(2)}) collective-permute-start(bf16[512,128]{1,0:T(8,128)(2,1)S(1)} %copy-done.17), channel_id=1, source_target_pairs={{0,24},{4,28},{8,16},{12,20},{16,8},{20,12},{24,0},{28,4},{1,25},{... | collective-permute-start | bytes 393224 | tf_op jit(solution)/shard_map/ppermute | solution.py:360
  150.2 21.8 %copy-start.11 = (bf16[512,128]{1,0:T(8,128)(2,1)}, bf16[512,128]{1,0:T(8,128)(2,1)S(1)}, u32[]{:S(2)}) copy-start(bf16[512,128]{1,0:T(8,128)(2,1)S(1)} %collective-permute-done.10.refs_4_) | copy-start | bytes 393220
  150.2 21.1 %collective-permute-start.13 = (bf16[512,128]{1,0:T(8,128)(2,1)S(1)}, bf16[512,128]{1,0:T(8,128)(2,1)S(1)}, u32[]{:S(2)}, u32[]{:S(2)}) collective-permute-start(bf16[512,128]{1,0:T(8,128)(2,1)S(1)} %copy-done.16), channel_id=1, source_target_pairs={{0,28},{4,24},{8,20},{12,16},{16,12},{20,8},{24,4},{28,0},{1,29},{... | collective-permute-start | bytes 393224 | tf_op jit(solution)/shard_map/ppermute | solution.py:360
  160.3 11.7 %copy-start.12 = (bf16[512,128]{1,0:T(8,128)(2,1)}, bf16[512,128]{1,0:T(8,128)(2,1)S(1)}, u32[]{:S(2)}) copy-start(bf16[512,128]{1,0:T(8,128)(2,1)S(1)} %collective-permute-done.11.refs_5_) | copy-start | bytes 393220
  160.3 19.7 %collective-permute-start.2 = (bf16[1536,128]{1,0:T(8,128)(2,1)}, bf16[1536,128]{1,0:T(8,128)(2,1)S(1)}, u32[]{:S(2)}, u32[]{:S(2)}) collective-permute-start(bf16[1536,128]{1,0:T(8,128)(2,1)} %get-tuple-element.31), channel_id=1, source_target_pairs={{0,12},{4,8},{8,4},{12,0},{16,28},{20,24},{24,20},{28,16},{1,13},{... | collective-permute-start | bytes 1179656 | tf_op jit(solution)/shard_map/ppermute | solution.py:360
  164.9 7.1 %copy-start.13 = (bf16[512,128]{1,0:T(8,128)(2,1)}, bf16[512,128]{1,0:T(8,128)(2,1)S(1)}, u32[]{:S(2)}) copy-start(bf16[512,128]{1,0:T(8,128)(2,1)S(1)} %collective-permute-done.12.refs_6_) | copy-start | bytes 393220
  164.9 19.4 %collective-permute-start.3 = (bf16[1536,128]{1,0:T(8,128)(2,1)}, bf16[1536,128]{1,0:T(8,128)(2,1)S(1)}, u32[]{:S(2)}, u32[]{:S(2)}) collective-permute-start(bf16[1536,128]{1,0:T(8,128)(2,1)} %get-tuple-element.32), channel_id=1, source_target_pairs={{0,16},{4,20},{8,24},{12,28},{16,0},{20,4},{24,8},{28,12},{1,17},{... | collective-permute-start | bytes 1179656 | tf_op jit(solution)/shard_map/ppermute | solution.py:360
  171.4 0.6 copy-start.14
  171.4 45.8 %collective-permute-start.4 = (bf16[1536,128]{1,0:T(8,128)(2,1)}, bf16[1536,128]{1,0:T(8,128)(2,1)S(1)}, u32[]{:S(2)}, u32[]{:S(2)}) collective-permute-start(bf16[1536,128]{1,0:T(8,128)(2,1)} %get-tuple-element.33), channel_id=1, source_target_pairs={{0,20},{4,16},{8,28},{12,24},{16,4},{20,0},{24,12},{28,8},{1,21},{... | collective-permute-start | bytes 1179656 | tf_op jit(solution)/shard_map/ppermute | solution.py:360
  171.4 66.7 %copy-start.1 = (bf16[1536,128]{1,0:T(8,128)(2,1)}, bf16[1536,128]{1,0:T(8,128)(2,1)S(1)}, u32[]{:S(2)}) copy-start(bf16[1536,128]{1,0:T(8,128)(2,1)S(1)} %collective-permute-done.refs_1_) | copy-start | bytes 1179652
  171.4 56.0 %collective-permute-start.5 = (bf16[1536,128]{1,0:T(8,128)(2,1)}, bf16[1536,128]{1,0:T(8,128)(2,1)S(1)}, u32[]{:S(2)}, u32[]{:S(2)}) collective-permute-start(bf16[1536,128]{1,0:T(8,128)(2,1)} %get-tuple-element.34), channel_id=1, source_target_pairs={{0,24},{4,28},{8,16},{12,20},{16,8},{20,12},{24,0},{28,4},{1,25},{... | collective-permute-start | bytes 1179656 | tf_op jit(solution)/shard_map/ppermute | solution.py:360
  172.0 66.2 %copy-start.2 = (bf16[1536,128]{1,0:T(8,128)(2,1)}, bf16[1536,128]{1,0:T(8,128)(2,1)S(1)}, u32[]{:S(2)}) copy-start(bf16[1536,128]{1,0:T(8,128)(2,1)S(1)} %collective-permute-done.1.refs_2_) | copy-start | bytes 1179652
  172.0 66.2 %collective-permute-start.6 = (bf16[1536,128]{1,0:T(8,128)(2,1)}, bf16[1536,128]{1,0:T(8,128)(2,1)S(1)}, u32[]{:S(2)}, u32[]{:S(2)}) collective-permute-start(bf16[1536,128]{1,0:T(8,128)(2,1)} %get-tuple-element.35), channel_id=1, source_target_pairs={{0,28},{4,24},{8,20},{12,16},{16,12},{20,8},{24,4},{28,0},{1,29},{... | collective-permute-start | bytes 1179656 | tf_op jit(solution)/shard_map/ppermute | solution.py:360
  180.0 58.1 %copy-start.3 = (bf16[1536,128]{1,0:T(8,128)(2,1)}, bf16[1536,128]{1,0:T(8,128)(2,1)S(1)}, u32[]{:S(2)}) copy-start(bf16[1536,128]{1,0:T(8,128)(2,1)S(1)} %collective-permute-done.2.refs_3_) | copy-start | bytes 1179652
  184.2 53.9 %copy-start.4 = (bf16[1536,128]{1,0:T(8,128)(2,1)}, bf16[1536,128]{1,0:T(8,128)(2,1)S(1)}, u32[]{:S(2)}) copy-start(bf16[1536,128]{1,0:T(8,128)(2,1)S(1)} %collective-permute-done.3.refs_4_) | copy-start | bytes 1179652
  217.1 21.0 %copy-start.5 = (bf16[1536,128]{1,0:T(8,128)(2,1)}, bf16[1536,128]{1,0:T(8,128)(2,1)S(1)}, u32[]{:S(2)}) copy-start(bf16[1536,128]{1,0:T(8,128)(2,1)S(1)} %collective-permute-done.4.refs_5_) | copy-start | bytes 1179652
  227.4 10.8 %copy-start.6 = (bf16[1536,128]{1,0:T(8,128)(2,1)}, bf16[1536,128]{1,0:T(8,128)(2,1)S(1)}, u32[]{:S(2)}) copy-start(bf16[1536,128]{1,0:T(8,128)(2,1)S(1)} %collective-permute-done.5.refs_6_) | copy-start | bytes 1179652
  238.1 0.8 copy-start.7
where the time goes:
time: 244 us; the launch traced here: 243 us
  waiting for transfers between devices  166 us (68%)
  Pallas kernels  44.9 us (18%)
  starting transfers between devices  29.2 us (12%)
    ppermute x14, waiting for transfers between devices, to_shards(): received[k] = lax.ppermute(results[k], 'seq', pairs)  89.6 us
    all_to_all x2, waiting for transfers between devices, to_heads(): lax.all_to_all(packed, ('seq', 'head'), split_axis=0, concat_axis=0, tile...  76.3 us
    pallas_call x2, Pallas kernels, attend(): pl.pallas_call(functools.partial(attention_kernel, total_blocks - 1, devi...  29.9 us
    ppermute x14, starting transfers between devices, to_shards(): received[k] = lax.ppermute(results[k], 'seq', pairs)  16.3 us
    all_to_all x2, starting transfers between devices, to_heads(): lax.all_to_all(packed, ('seq', 'head'), split_axis=0, concat_axis=0, tile...  12.9 us
    pallas_call x2, Pallas kernels, pack(): pl.pallas_call(functools.partial(pack_kernel, heads, table_rows), grid=(g...  8.01 us
    pallas_call x2, Pallas kernels, unpack(): pl.pallas_call(functools.partial(unpack_kernel, tuple((part[0] for part i...  7.02 us
  transfers between devices with their start and end apart: 16, of which 12 were waited for; matrix products, arithmetic and copies ran while one was open for 1% of the time, Pallas kernels for 15%

commit v1 on v0

--- a/solution.py
+++ b/solution.py
@@ -119,6 +119,50 @@
         compiler_params=pltpu.CompilerParams(vmem_limit_bytes=VMEM_LIMIT),
         cost_estimate=copy_cost(size),
     )(member, *received, *olds)
+
+
+def unpack_all_kernel(begins, step_heads, piece_ref, *refs):
+    outs = refs[len(refs) - len(begins) :]
+    for begin, out in zip(begins, outs):
+        runs, _, rows, _ = out.shape
+        for m in range(step_heads):
+            for i in range(runs):
+                out[i, 0, :, pl.ds(m * HEAD_WIDTH, HEAD_WIDTH)] = piece_ref[
+                    m, pl.ds(begin + i * rows, rows), :
+                ]
+
+
+def unpack_all(received, parts):
+    heads, total, _ = received.shape
+    step_heads = 2 if heads % 2 == 0 else 1
+    width = step_heads * HEAD_WIDTH
+    shapes, out_specs, begins, olds, aliases = [], [], [], [], {}
+    size = 0
+    for n, (begin, rows, runs, pieces, piece, old) in enumerate(parts):
+        begins.append(begin)
+        shapes.append(
+            jax.ShapeDtypeStruct((runs, pieces, rows, heads * HEAD_WIDTH), jnp.bfloat16)
+        )
+        out_specs.append(
+            pl.BlockSpec(
+                (runs, 1, rows, width), functools.partial(lambda piece, h: (0, piece, 0, h), piece)
+            )
+        )
+        size += rows * runs * heads * HEAD_WIDTH
+        if old is not None:
+            aliases[1 + len(olds)] = n
+            olds.append(old)
+    return pl.pallas_call(
+        functools.partial(unpack_all_kernel, begins, step_heads),
+        grid=(heads // step_heads,),
+        out_shape=shapes,
+        in_specs=[pl.BlockSpec((step_heads, total, HEAD_WIDTH), lambda h: (h, 0, 0))]
+        + [pl.BlockSpec(memory_space=pl.ANY)] * len(olds),
+        out_specs=out_specs,
+        input_output_aliases=aliases,
+        compiler_params=pltpu.CompilerParams(vmem_limit_bytes=VMEM_LIMIT),
+        cost_estimate=copy_cost(size),
+    )(received, *olds)
 
 
 def attention_kernel(
@@ -146,7 +190,7 @@
     refs = list(refs)
     qd_ref = refs.pop(0) if has_qd else kv_ref
     start_ref = refs.pop(0) if has_start else None
-    out_refs = [refs.pop(0) for _ in range(targets)]
+    out_refs = [refs.pop(0) for _ in range(1 if joined else targets)]
     acc, retain, waiting, near = refs
     scale = HEAD_WIDTH ** (-0.5)
     steps = targets * (out_rows // BLOCK_TOKENS)
@@ -249,18 +293,20 @@
     lax.fori_loop(1, steps // UNROLL, step, 0)
     for u in range(UNROLL):
         finish(steps - UNROLL + u, u)
-    for k, out_ref in enumerate(out_refs):
-        target = member_ref[0] ^ k
-        out_ref[pl.ds(0, 2 * out_rows), :] = near[target]
-        if joined:
-            rows = acc.shape[0] // targets
-            part = pl.ds(pl.multiple_of(target * rows, rows), rows)
-            out_ref[pl.ds(2 * out_rows, rows), :] = (acc[part, :HEAD_WIDTH] * scale).astype(
-                jnp.bfloat16
-            )
-            out_ref[pl.ds(2 * out_rows + rows, rows), :] = acc[part, HEAD_WIDTH:].astype(
-                jnp.bfloat16
-            )
+    if joined:
+        rows = acc.shape[0] // targets
+        for target in range(targets):
+            part = pl.ds(target * rows, rows)
+            out_refs[0][target, pl.ds(0, 2 * out_rows), :] = near[target]
+            out_refs[0][target, pl.ds(2 * out_rows, rows), :] = (
+                acc[part, :HEAD_WIDTH] * scale
+            ).astype(jnp.bfloat16)
+            out_refs[0][target, pl.ds(2 * out_rows + rows, rows), :] = acc[
+                part, HEAD_WIDTH:
+            ].astype(jnp.bfloat16)
+    else:
+        for k, out_ref in enumerate(out_refs):
+            out_ref[...] = near[member_ref[0] ^ k]
 
 
 def attend(
@@ -273,8 +319,14 @@
     pairs = steps * BLOCK_TOKENS * WIDE
     accumulator = (length, 2 * HEAD_WIDTH)
     out_rows = steps * BLOCK_TOKENS // targets
-    total_rows = 2 * out_rows + (2 * length // targets if joined else 0)
-    out_shape = [jax.ShapeDtypeStruct((total_rows, HEAD_WIDTH), jnp.bfloat16)] * targets
+    if joined:
+        out_shape = [
+            jax.ShapeDtypeStruct(
+                (targets, 2 * out_rows + 2 * length // targets, HEAD_WIDTH), jnp.bfloat16
+            )
+        ]
+    else:
+        out_shape = [jax.ShapeDtypeStruct((2 * out_rows, HEAD_WIDTH), jnp.bfloat16)] * targets
     scratch = [
         pltpu.VMEM((team_blocks, WIDE), jnp.float32),
         pltpu.VMEM((UNROLL, 2 * BLOCK_TOKENS, WIDE), jnp.bfloat16),
@@ -309,7 +361,7 @@
         scratch_shapes=scratch,
         compiler_params=pltpu.CompilerParams(vmem_limit_bytes=VMEM_LIMIT),
         cost_estimate=pl.CostEstimate(
-            flops=12 * pairs * HEAD_WIDTH,
+            flops=128 * pairs * HEAD_WIDTH,
             bytes_accessed=2 * (source.size + kv.size) + 8 * length * HEAD_WIDTH,
             transcendentals=pairs,
         ),
@@ -394,53 +446,64 @@
     )
     listed = jnp.clip(listed, 0, total_blocks - 1).reshape(-1)
     starts = listed // device_blocks * kv.shape[1] + listed % device_blocks * BLOCK_TOKENS
-    near = []
-    sums = None
+    pieces_out = []
+    sums = []
     for c in range(pieces):
-        results = attend(
-            listed,
-            starts,
-            first_block.reshape(1),
+        pieces_out.append(
+            attend(
+                listed,
+                starts,
+                first_block.reshape(1),
+                member.reshape(1),
+                drops,
+                kv,
+                qd[c],
+                qd_begin if qd[c] is None else 0,
+                sums[0] if sums else None,
+                c,
+                per,
+                whole and c == pieces - 1,
+                device_blocks,
+                total_blocks,
+                tokens,
+                heads,
+            )
+        )
+        sums = pieces_out[c][heads:]
+    runs = shard_blocks // device_blocks
+    begin = shard_tokens // pieces
+    near = [to_shards(out[:heads]) for out in pieces_out if len(out) > 1]
+    att, dq = None, None
+    if whole:
+        rest = pieces_out[-1][0]
+        if near:
+            rest, *near[-1][heads // 2 :] = lax.optimization_barrier(
+                (rest, *near[-1][heads // 2 :])
+            )
+        rest = lax.all_to_all(rest, "seq", split_axis=0, concat_axis=0, tiled=True)
+    for c in range(len(near)):
+        parts = [(0, rows, runs, pieces, c, att), (begin, rows, runs, pieces, c, dq)]
+        att, dq = unpack(member.reshape(1), near[c], parts)
+    if whole:
+        c = pieces - 1
+        parts = [(0, rows, runs, pieces, c, att), (begin, rows, runs, pieces, c, dq)]
+        grads = [(2 * begin + n * shard_tokens, shard_tokens, 1, 1, 0, None) for n in range(2)]
+        att, dq, dk, dv = unpack_all(rest, parts + grads)
+    else:
+        grads = lax.psum_scatter(
+            sums[0], "seq", scatter_dimension=0, tiled=True, axis_index_groups=same_head
+        ).reshape(heads, shard_tokens, 2, HEAD_WIDTH)
+        grads = jnp.concatenate(
+            [grads[:, :, 0] * HEAD_WIDTH ** (-0.5), grads[:, :, 1]], axis=1
+        ).astype(jnp.bfloat16)
+        grads = to_shards(
+            [lax.dynamic_index_in_dim(grads, member ^ k, 0, keepdims=False) for k in range(heads)]
+        )
+        dk, dv = unpack(
             member.reshape(1),
-            drops,
-            kv,
-            qd[c],
-            qd_begin if qd[c] is None else 0,
-            sums[0] if sums else None,
-            c,
-            per,
-            whole and c == pieces - 1,
-            device_blocks,
-            total_blocks,
-            tokens,
-            heads,
-        )
-        near.append(to_shards(results[:heads]))
-        sums = results[heads:]
-    runs = shard_blocks // device_blocks
-    att, dq = None, None
-    for c in range(pieces):
-        begin = shard_tokens // pieces
-        parts = [(0, rows, runs, pieces, c, att), (begin, rows, runs, pieces, c, dq)]
-        if c < pieces - 1:
-            att, dq = unpack(member.reshape(1), near[c], parts)
-        elif whole:
-            grads = [(2 * begin + n * shard_tokens, shard_tokens, 1, 1, 0, None) for n in range(2)]
-            att, dq, dk, dv = unpack(member.reshape(1), near[c], parts + grads)
-        else:
-            att, dq = unpack(member.reshape(1), near[c], parts)
-            grads = lax.psum_scatter(
-                sums[0], "seq", scatter_dimension=0, tiled=True, axis_index_groups=same_head
-            ).reshape(heads, shard_tokens, 2, HEAD_WIDTH)
-            grads = jnp.concatenate(
-                [grads[:, :, 0] * HEAD_WIDTH ** (-0.5), grads[:, :, 1]], axis=1
-            ).astype(jnp.bfloat16)
-            grads = to_shards(
-                [lax.dynamic_index_in_dim(grads, member ^ k, 0, keepdims=False) for k in range(heads)]
-            )
-            dk, dv = unpack(
-                member.reshape(1), grads, [(n * shard_tokens, shard_tokens, 1, 1, 0, None) for n in range(2)]
-            )
+            grads,
+            [(n * shard_tokens, shard_tokens, 1, 1, 0, None) for n in range(2)],
+        )
     return tuple(t.reshape(shard_tokens, heads * HEAD_WIDTH) for t in (att, dq, dk, dv))
 
 

time: 244 us -> 227 us (0.930)
  the two profiles are of different devices: /device:TPU:9 before, /device:TPU:0 now
where the time goes in v1:
time: 227 us; the launch traced here: 226 us
  waiting for transfers between devices  149 us (66%)
  Pallas kernels  45.1 us (20%)
  starting transfers between devices  26.2 us (12%)
  local copies, waits for them, and re-layouts  3.97 us (2%)
    all_to_all x2, waiting for transfers between devices, to_heads(): lax.all_to_all(packed, ('seq', 'head'), split_axis=0, concat_axis=0, tile...  85.1 us
    ppermute x7, waiting for transfers between devices, to_shards(): received[k] = lax.ppermute(results[k], 'seq', pairs)  53.7 us
    pallas_call x2, Pallas kernels, attend(): pl.pallas_call(functools.partial(attention_kernel, total_blocks - 1, devi...  30.3 us
    all_to_all x2, starting transfers between devices, to_heads(): lax.all_to_all(packed, ('seq', 'head'), split_axis=0, concat_axis=0, tile...  11.4 us
    ppermute x7, starting transfers between devices, to_shards(): received[k] = lax.ppermute(results[k], 'seq', pairs)  11.2 us
    all_to_all x1, waiting for transfers between devices, per_device(): rest = lax.all_to_all(rest, 'seq', split_axis=0, concat_axis=0, tiled=True)  10.1 us
    pallas_call x2, Pallas kernels, pack(): pl.pallas_call(functools.partial(pack_kernel, heads, table_rows), grid=(g...  7.95 us
  transfers between devices with their start and end apart: 10, of which 6 were waited for; matrix products, arithmetic and copies ran while one was open for 1% of the time, Pallas kernels for 16%

profile of v1, /device:TPU:0, one launch (start us, length us, event | category | flops | bytes accessed | tf_op | source)
XLA Modules:
  0.0 225.5 jit_solution(10731894887826103459)
XLA Ops:
  0.6 4.5 %shard_map.102 = bf16[8,4,400,128]{3,2,1,0:T(8,128)(2,1)} custom-call(s32[8,8,8]{2,1,0:T(8,128)} %refs_0_.2, s32[3,8,8]{2,1,0:T(8,128)} %bitcast.28, bf16[128,4096]{1,0:T(8,128)(2,1)} %refs_2_.1, bf16[128,4096]{1,0:T(8,128)(2,1)} %refs_3_.1, bf16[128,4096]{1,0:T(8,128)(2,1)} %refs_0_.3, bf16[128,4096]{1,0:T(8,128)(2,1)} %refs_1_.1), custom_call_target="tpu_custom_call" | custom-call | bytes 6553600 | tf_op jit(solution)/shard_map/pallas_call | solution.py:69
  5.1 7.3 %all-to-all-start = ((bf16[32,400,128]{2,1,0:T(8,128)(2,1)}), bf16[32,400,128]{2,1,0:T(8,128)(2,1)S(1)}, u32[]{:S(2)}, u32[]{:S(2)}) async-start(bf16[32,400,128]{2,1,0:T(8,128)(2,1)} %bitcast.21), calls=%async_computation | async-start | bytes 6553600 | tf_op jit(solution)/shard_map/all_to_all | solution.py:399
  12.4 0.0 copy-start.10
  12.4 3.5 %shard_map.103 = bf16[8,4,128,128]{3,2,1,0:T(8,128)(2,1)} custom-call(bf16[128,4096]{1,0:T(8,128)(2,1)} %refs_0_.3, bf16[128,4096]{1,0:T(8,128)(2,1)} %refs_1_.1), custom_call_target="tpu_custom_call" | custom-call | bytes 2097152 | tf_op jit(solution)/shard_map/pallas_call | solution.py:69
  15.9 70.8 %all-to-all-done = bf16[32,400,128]{2,1,0:T(8,128)(2,1)S(1)} async-done(((bf16[32,400,128]{2,1,0:T(8,128)(2,1)}), bf16[32,400,128]{2,1,0:T(8,128)(2,1)S(1)}, u32[]{:S(2)}, u32[]{:S(2)}) %all-to-all-start) | async-done | bytes 3276832 | tf_op jit(solution)/shard_map/all_to_all | solution.py:399
  86.7 4.1 %all-to-all-start.1 = ((bf16[32,128,128]{2,1,0:T(8,128)(2,1)}), bf16[32,128,128]{2,1,0:T(8,128)(2,1)}, u32[]{:S(2)}, u32[]{:S(2)}) async-start(bf16[32,128,128]{2,1,0:T(8,128)(2,1)} %bitcast.22), calls=%async_computation.1 | async-start | bytes 2097152 | tf_op jit(solution)/shard_map/all_to_all | solution.py:399
  90.8 0.1 reshape.76
  90.9 0.0 copy-done.10
  90.9 0.1 broadcast_in_dim.2
  91.0 0.1 copy.17
  91.1 0.1 min.12.ids_ref
  91.2 0.0 copy-start.9
  91.2 0.6 fusion.1.starts_ref
  91.7 0.6 slice_bitcast_fusion.drop_ref
  92.3 0.0 copy-done.1
  92.4 0.0 copy-done.9
  92.4 14.3 %shard_map.104 = (bf16[512,128]{1,0:T(8,128)(2,1)}, bf16[512,128]{1,0:T(8,128)(2,1)}, bf16[512,128]{1,0:T(8,128)(2,1)}, bf16[512,128]{1,0:T(8,128)(2,1)}, bf16[5...) custom-call(s32[512]{0:T(512)} %copy-done.9, ...), custom_call_target="tpu_custom_call" | custom-call | flops 17179869184 | bytes 10747904 | tf_op jit(solution)/shard_map/pallas_call | solution.py:341
  106.7 2.6 %collective-permute-start = (bf16[512,128]{1,0:T(8,128)(2,1)}, bf16[512,128]{1,0:T(8,128)(2,1)S(1)}, u32[]{:S(2)}, u32[]{:S(2)}) collective-permute-start(bf16[512,128]{1,0:T(8,128)(2,1)} %get-tuple-element.25), channel_id=1, source_target_pairs={{0,16},{4,20},{8,24},{12,28},{16,0},{20,4},{24,8},{28,12},{1,17},{... | collective-permute-start | bytes 393224 | tf_op jit(solution)/shard_map/ppermute | solution.py:412
  109.3 1.4 collective-permute-start.1
  110.7 3.4 %collective-permute-start.2 = (bf16[512,128]{1,0:T(8,128)(2,1)}, bf16[512,128]{1,0:T(8,128)(2,1)S(1)}, u32[]{:S(2)}, u32[]{:S(2)}) collective-permute-start(bf16[512,128]{1,0:T(8,128)(2,1)} %get-tuple-element.27), channel_id=1, source_target_pairs={{0,24},{4,28},{8,16},{12,20},{16,8},{20,12},{24,0},{28,4},{1,25},{... | collective-permute-start | bytes 393224 | tf_op jit(solution)/shard_map/ppermute | solution.py:412
  114.1 0.2 collective-permute-start.3
  114.3 14.3 %all-to-all-done.1 = bf16[32,128,128]{2,1,0:T(8,128)(2,1)} async-done(((bf16[32,128,128]{2,1,0:T(8,128)(2,1)}), bf16[32,128,128]{2,1,0:T(8,128)(2,1)}, u32[]{:S(2)}, u32[]{:S(2)}) %all-to-all-start.1) | async-done | bytes 1048608 | tf_op jit(solution)/shard_map/all_to_all | solution.py:399
  128.7 16.0 %shard_map.105 = bf16[8,1536,128]{2,1,0:T(8,128)(2,1)} custom-call(s32[512]{0:T(512)} %copy-done.9, s32[512]{0:T(512)} %fusion.1.starts_ref, s32[1]{0:T(128)} %bitcast.5.first_ref, s32[1]{0:T(128)} %bitcast.6.member_ref, s32[64,8]{1,0:T(8,128)} %slice_bitcast_fusion.drop_ref, bf16[12800,128]{1,0:T(8,128)(2,1)} %bitcast.25, ...), custom_call_target="tpu_custom_call" | custom-call | flops 17179869184 | bytes 8519680 | tf_op jit(solution)/shard_map/pallas_call | solution.py:341
  144.6 0.0 collective-permute-done.refs_4_
  144.6 0.0 collective-permute-done.1.refs_5_
  144.6 0.0 copy-start.3
  144.6 0.0 collective-permute-done.2.refs_6_
  144.7 0.0 copy-start.4
  144.7 0.0 collective-permute-done.3.refs_7_
  144.7 0.0 copy-start.5
  144.7 0.7 copy-done.5
  145.4 3.6 %all-to-all-start.2 = ((bf16[8,1536,128]{2,1,0:T(8,128)(2,1)}), bf16[8,1536,128]{2,1,0:T(8,128)(2,1)S(1)}, u32[]{:S(2)}, u32[]{:S(2)}) async-start(bf16[8,1536,128]{2,1,0:T(8,128)(2,1)} %shard_map.105), calls=%async_computation.2 | async-start | bytes 6291456 | tf_op jit(solution)/shard_map/all_to_all | solution.py:483
  149.1 1.9 collective-permute-start.4
  151.0 1.5 collective-permute-start.5
  152.5 0.2 collective-permute-start.6
  152.6 25.6 %collective-permute-done.4.refs_1_ = bf16[512,128]{1,0:T(8,128)(2,1)S(1)} collective-permute-done((bf16[512,128]{1,0:T(8,128)(2,1)}, bf16[512,128]{1,0:T(8,128)(2,1)S(1)}, u32[]{:S(2)}, u32[]{:S(2)}) %collective-permute-start.4) | collective-permute-done | bytes 131104 | tf_op jit(solution)/shard_map/ppermute | solution.py:412
  178.2 26.6 %collective-permute-done.5.refs_2_ = bf16[512,128]{1,0:T(8,128)(2,1)S(1)} collective-permute-done((bf16[512,128]{1,0:T(8,128)(2,1)}, bf16[512,128]{1,0:T(8,128)(2,1)S(1)}, u32[]{:S(2)}, u32[]{:S(2)}) %collective-permute-start.5) | collective-permute-done | bytes 131104 | tf_op jit(solution)/shard_map/ppermute | solution.py:412
  204.8 1.4 collective-permute-done.6.refs_3_
  206.3 0.0 copy-done.2
  206.3 0.0 copy-done.3
  206.3 0.0 copy-done.4
  206.3 0.0 copy-done.6
  206.3 0.0 copy-done.7
  206.3 0.6 copy-done.8
  206.9 2.6 %shard_map.106 = (bf16[4,2,64,1024]{3,2,1,0:T(8,128)(2,1)}, bf16[4,2,64,1024]{3,2,1,0:T(8,128)(2,1)}) custom-call(s32[1]{0:T(128)} %bitcast.6.member_ref, bf16[512,128]{1,0:T(8,128)(2,1)} %get-tuple-element.30.refs_0_, bf16[512,128]{1,0:T(8,128)(2,1)} %copy-done.6, bf16[512,128]{1,0:T(8,128)(2,1)} %copy-done.7, bf16[512,128]{1,0:T(8,128)(2,1)} %copy-done.8, ...), custom_call_target="tpu_custom_call" | custom-call | bytes 2097152 | tf_op jit(solution)/shard_map/pallas_call | solution.py:110
  209.5 10.1 %all-to-all-done.2.piece_ref = bf16[8,1536,128]{2,1,0:T(8,128)(2,1)S(1)} async-done(((bf16[8,1536,128]{2,1,0:T(8,128)(2,1)}), bf16[8,1536,128]{2,1,0:T(8,128)(2,1)S(1)}, u32[]{:S(2)}, u32[]{:S(2)}) %all-to-all-start.2) | async-done | bytes 3145760 | tf_op jit(solution)/shard_map/all_to_all | solution.py:483
  219.5 1.6 copy-done
  221.2 4.3 %shard_map.107 = (bf16[4,2,64,1024]{3,2,1,0:T(8,128)(2,1)}, bf16[4,2,64,1024]{3,2,1,0:T(8,128)(2,1)}, bf16[1,1,512,1024]{3,2,1,0:T(8,128)(2,1)}, bf16[1,1,512,1024]{3,2,1,0:T(8,128)(2,1)}) custom-call(bf16[8,1536,128]{2,1,0:T(8,128)(2,1)} %copy-done, ...), custom_call_target="tpu_custom_call", output_to_operand_aliasing={{0}: (1, {}), {1}: (2, {})} | custom-call | bytes 6291456 | tf_op jit(solution)/shard_map/pallas_call | solution.py:155
  (14 shorter events, 0.1 us)
Async XLA Ops:
  5.1 81.6 %all-to-all-start = ((bf16[32,400,128]{2,1,0:T(8,128)(2,1)}), bf16[32,400,128]{2,1,0:T(8,128)(2,1)S(1)}, u32[]{:S(2)}, u32[]{:S(2)}) async-start(bf16[32,400,128]{2,1,0:T(8,128)(2,1)} %bitcast.21), calls=%async_computation | async-start | bytes 6553600 | tf_op jit(solution)/shard_map/all_to_all | solution.py:399
  12.4 78.5 %copy-start.10 = (s32[2]{0:T(128)S(1)}, s32[2]{0:T(128)}, u32[]{:S(2)}) copy-start(s32[2]{0:T(128)} %param.12) | copy-start | bytes 28
  86.7 5.7 %copy-start.1 = (bf16[32,400,128]{2,1,0:T(8,128)(2,1)}, bf16[32,400,128]{2,1,0:T(8,128)(2,1)S(1)}, u32[]{:S(2)}) copy-start(bf16[32,400,128]{2,1,0:T(8,128)(2,1)S(1)} %all-to-all-done) | copy-start | bytes 9830404
  86.7 42.0 %all-to-all-start.1 = ((bf16[32,128,128]{2,1,0:T(8,128)(2,1)}), bf16[32,128,128]{2,1,0:T(8,128)(2,1)}, u32[]{:S(2)}, u32[]{:S(2)}) async-start(bf16[32,128,128]{2,1,0:T(8,128)(2,1)} %bitcast.22), calls=%async_computation.1 | async-start | bytes 2097152 | tf_op jit(solution)/shard_map/all_to_all | solution.py:399
  91.2 1.2 copy-start.9
  106.7 37.9 %collective-permute-start = (bf16[512,128]{1,0:T(8,128)(2,1)}, bf16[512,128]{1,0:T(8,128)(2,1)S(1)}, u32[]{:S(2)}, u32[]{:S(2)}) collective-permute-start(bf16[512,128]{1,0:T(8,128)(2,1)} %get-tuple-element.25), channel_id=1, source_target_pairs={{0,16},{4,20},{8,24},{12,28},{16,0},{20,4},{24,8},{28,12},{1,17},{... | collective-permute-start | bytes 393224 | tf_op jit(solution)/shard_map/ppermute | solution.py:412
  109.3 35.3 %collective-permute-start.1 = (bf16[512,128]{1,0:T(8,128)(2,1)}, bf16[512,128]{1,0:T(8,128)(2,1)S(1)}, u32[]{:S(2)}, u32[]{:S(2)}) collective-permute-start(bf16[512,128]{1,0:T(8,128)(2,1)} %get-tuple-element.26), channel_id=1, source_target_pairs={{0,20},{4,16},{8,28},{12,24},{16,4},{20,0},{24,12},{28,8},{1,21},{... | collective-permute-start | bytes 393224 | tf_op jit(solution)/shard_map/ppermute | solution.py:412
  110.7 33.9 %collective-permute-start.2 = (bf16[512,128]{1,0:T(8,128)(2,1)}, bf16[512,128]{1,0:T(8,128)(2,1)S(1)}, u32[]{:S(2)}, u32[]{:S(2)}) collective-permute-start(bf16[512,128]{1,0:T(8,128)(2,1)} %get-tuple-element.27), channel_id=1, source_target_pairs={{0,24},{4,28},{8,16},{12,20},{16,8},{20,12},{24,0},{28,4},{1,25},{... | collective-permute-start | bytes 393224 | tf_op jit(solution)/shard_map/ppermute | solution.py:412
  114.1 30.6 %collective-permute-start.3 = (bf16[512,128]{1,0:T(8,128)(2,1)}, bf16[512,128]{1,0:T(8,128)(2,1)S(1)}, u32[]{:S(2)}, u32[]{:S(2)}) collective-permute-start(bf16[512,128]{1,0:T(8,128)(2,1)} %get-tuple-element.28), channel_id=1, source_target_pairs={{0,28},{4,24},{8,20},{12,16},{16,12},{20,8},{24,4},{28,0},{1,29},{... | collective-permute-start | bytes 393224 | tf_op jit(solution)/shard_map/ppermute | solution.py:412
  144.6 61.6 %copy-start.2 = (bf16[512,128]{1,0:T(8,128)(2,1)}, bf16[512,128]{1,0:T(8,128)(2,1)S(1)}, u32[]{:S(2)}) copy-start(bf16[512,128]{1,0:T(8,128)(2,1)S(1)} %collective-permute-done.refs_4_) | copy-start | bytes 393220
  144.6 61.6 %copy-start.3 = (bf16[512,128]{1,0:T(8,128)(2,1)}, bf16[512,128]{1,0:T(8,128)(2,1)S(1)}, u32[]{:S(2)}) copy-start(bf16[512,128]{1,0:T(8,128)(2,1)S(1)} %collective-permute-done.1.refs_5_) | copy-start | bytes 393220
  144.7 61.6 %copy-start.4 = (bf16[512,128]{1,0:T(8,128)(2,1)}, bf16[512,128]{1,0:T(8,128)(2,1)S(1)}, u32[]{:S(2)}) copy-start(bf16[512,128]{1,0:T(8,128)(2,1)S(1)} %collective-permute-done.2.refs_6_) | copy-start | bytes 393220
  144.7 0.7 copy-start.5
  145.4 74.1 %all-to-all-start.2 = ((bf16[8,1536,128]{2,1,0:T(8,128)(2,1)}), bf16[8,1536,128]{2,1,0:T(8,128)(2,1)S(1)}, u32[]{:S(2)}, u32[]{:S(2)}) async-start(bf16[8,1536,128]{2,1,0:T(8,128)(2,1)} %shard_map.105), calls=%async_computation.2 | async-start | bytes 6291456 | tf_op jit(solution)/shard_map/all_to_all | solution.py:483
  149.1 29.2 %collective-permute-start.4 = (bf16[512,128]{1,0:T(8,128)(2,1)}, bf16[512,128]{1,0:T(8,128)(2,1)S(1)}, u32[]{:S(2)}, u32[]{:S(2)}) collective-permute-start(bf16[512,128]{1,0:T(8,128)(2,1)} %get-tuple-element.31), channel_id=1, source_target_pairs={{0,4},{4,0},{8,12},{12,8},{16,20},{20,16},{24,28},{28,24},{1,5},{5... | collective-permute-start | bytes 393224 | tf_op jit(solution)/shard_map/ppermute | solution.py:412
  151.0 53.9 %collective-permute-start.5 = (bf16[512,128]{1,0:T(8,128)(2,1)}, bf16[512,128]{1,0:T(8,128)(2,1)S(1)}, u32[]{:S(2)}, u32[]{:S(2)}) collective-permute-start(bf16[512,128]{1,0:T(8,128)(2,1)} %get-tuple-element.32), channel_id=1, source_target_pairs={{0,8},{4,12},{8,0},{12,4},{16,24},{20,28},{24,16},{28,20},{1,9},{5... | collective-permute-start | bytes 393224 | tf_op jit(solution)/shard_map/ppermute | solution.py:412
  152.5 53.8 %collective-permute-start.6 = (bf16[512,128]{1,0:T(8,128)(2,1)}, bf16[512,128]{1,0:T(8,128)(2,1)S(1)}, u32[]{:S(2)}, u32[]{:S(2)}) collective-permute-start(bf16[512,128]{1,0:T(8,128)(2,1)} %get-tuple-element.33), channel_id=1, source_target_pairs={{0,12},{4,8},{8,4},{12,0},{16,28},{20,24},{24,20},{28,16},{1,13},{... | collective-permute-start | bytes 393224 | tf_op jit(solution)/shard_map/ppermute | solution.py:412
  178.2 28.1 %copy-start.6 = (bf16[512,128]{1,0:T(8,128)(2,1)}, bf16[512,128]{1,0:T(8,128)(2,1)S(1)}, u32[]{:S(2)}) copy-start(bf16[512,128]{1,0:T(8,128)(2,1)S(1)} %collective-permute-done.4.refs_1_) | copy-start | bytes 393220
  204.8 1.5 copy-start.7
  206.3 0.6 copy-start.8
  219.5 1.6 copy-start

commit v2 on v1

--- a/solution.py
+++ b/solution.py
@@ -191,7 +191,8 @@
     qd_ref = refs.pop(0) if has_qd else kv_ref
     start_ref = refs.pop(0) if has_start else None
     out_refs = [refs.pop(0) for _ in range(1 if joined else targets)]
-    acc, retain, waiting, near = refs
+    acc, retain, waiting, near = refs[:4]
+    earlier, sem = refs[4:] if has_start else (None, None)
     scale = HEAD_WIDTH ** (-0.5)
     steps = targets * (out_rows // BLOCK_TOKENS)
     slot_of_lane = lax.broadcasted_iota(jnp.int32, (SLOTS, WIDE), 1) // BLOCK_TOKENS
@@ -200,7 +201,10 @@
     retain[...] = jnp.dot(
         drop_ref[...].astype(jnp.float32), expand, preferred_element_type=jnp.float32
     ) * (1.0 / keep_prob)
-    acc[...] = start_ref[...] if has_start else jnp.zeros_like(acc)
+    acc[...] = jnp.zeros_like(acc)
+    if has_start:
+        fetch = pltpu.make_async_copy(start_ref, earlier, sem)
+        fetch.start()
     lane = lax.broadcasted_iota(jnp.int32, (1, WIDE), 1)
     nt = (((1,), (1,)), ((), ()))
     tn = (((0,), (0,)), ((), ()))
@@ -293,6 +297,9 @@
     lax.fori_loop(1, steps // UNROLL, step, 0)
     for u in range(UNROLL):
         finish(steps - UNROLL + u, u)
+    if has_start:
+        fetch.wait()
+        acc[...] += earlier[...]
     if joined:
         rows = acc.shape[0] // targets
         for target in range(targets):
@@ -336,8 +343,11 @@
         scratch = [pltpu.VMEM(accumulator, jnp.float32)] + scratch
     else:
         out_shape.append(jax.ShapeDtypeStruct(accumulator, jnp.float32))
+    if start is not None:
+        scratch += [pltpu.VMEM(accumulator, jnp.float32), pltpu.SemaphoreType.DMA]
     flat = [t.reshape(-1, HEAD_WIDTH) for t in (kv, qd) if t is not None]
     operands = flat + ([] if start is None else [start])
+    operand_specs = [vmem] * len(flat) + [pl.BlockSpec(memory_space=pl.ANY)] * (start is not None)
     return pl.pallas_call(
         functools.partial(
             attention_kernel,
@@ -356,7 +366,7 @@
             targets,
         ),
         out_shape=out_shape,
-        in_specs=[smem, smem, smem, smem, vmem] + [vmem] * len(operands),
+        in_specs=[smem, smem, smem, smem, vmem] + operand_specs,
         out_specs=[vmem] * len(out_shape),
         scratch_shapes=scratch,
         compiler_params=pltpu.CompilerParams(vmem_limit_bytes=VMEM_LIMIT),
@@ -447,6 +457,7 @@
     listed = jnp.clip(listed, 0, total_blocks - 1).reshape(-1)
     starts = listed // device_blocks * kv.shape[1] + listed % device_blocks * BLOCK_TOKENS
     pieces_out = []
+    held = []
     sums = []
     for c in range(pieces):
         pieces_out.append(
@@ -470,9 +481,18 @@
             )
         )
         sums = pieces_out[c][heads:]
+        if c + 1 < pieces:
+            qd[c + 1], *results = lax.optimization_barrier((qd[c + 1], *pieces_out[c][1:heads]))
+            held.append(results)
     runs = shard_blocks // device_blocks
     begin = shard_tokens // pieces
-    near = [to_shards(out[:heads]) for out in pieces_out if len(out) > 1]
+    near = []
+    for c, out in enumerate(pieces_out):
+        if len(out) > 1:
+            results = out[:heads]
+            if c + 1 < pieces:
+                results = [results[0], *held[c]]
+            near.append(to_shards(results))
     att, dq = None, None
     if whole:
         rest = pieces_out[-1][0]

time: 227 us -> 223 us (0.982)
  waiting for transfers between devices: 149 us -> 145 us
  starting transfers between devices: 26.2 us -> 28.6 us
    all_to_all x2, waiting for transfers between devices: 85.1 us -> 81 us  [to_heads(): lax.all_to_all(packed, ('seq', 'head'), split_axis=0, concat_axis=0, tile...]
    all_to_all x1, starting transfers between devices: 3.65 us -> 6.06 us  [per_device(): rest = lax.all_to_all(rest, 'seq', split_axis=0, concat_axis=0, tiled=True)]
where the time goes in v2:
time: 223 us; the launch traced here: 222 us
  waiting for transfers between devices  145 us (65%)
  Pallas kernels  44.1 us (20%)
  starting transfers between devices  28.6 us (13%)
  local copies, waits for them, and re-layouts  3.25 us (1%)
    all_to_all x2, waiting for transfers between devices, to_heads(): lax.all_to_all(packed, ('seq', 'head'), split_axis=0, concat_axis=0, tile...  81 us
    ppermute x7, waiting for transfers between devices, to_shards(): received[k] = lax.ppermute(results[k], 'seq', pairs)  53.5 us
    pallas_call x2, Pallas kernels, attend(): pl.pallas_call(functools.partial(attention_kernel, total_blocks - 1, devi...  29.3 us
    all_to_all x2, starting transfers between devices, to_heads(): lax.all_to_all(packed, ('seq', 'head'), split_axis=0, concat_axis=0, tile...  11.4 us
    ppermute x7, starting transfers between devices, to_shards(): received[k] = lax.ppermute(results[k], 'seq', pairs)  11.2 us
    all_to_all x1, waiting for transfers between devices, per_device(): rest = lax.all_to_all(rest, 'seq', split_axis=0, concat_axis=0, tiled=True)  10.2 us
    pallas_call x2, Pallas kernels, pack(): pl.pallas_call(functools.partial(pack_kernel, heads, table_rows), grid=(g...  7.91 us
    all_to_all x1, starting transfers between devices, per_device(): rest = lax.all_to_all(rest, 'seq', split_axis=0, concat_axis=0, tiled=True)  6.06 us
  transfers between devices with their start and end apart: 10, of which 6 were waited for; matrix products, arithmetic and copies ran while one was open for 1% of the time, Pallas kernels for 16%

profile of v2, /device:TPU:0, one launch (start us, length us, event | category | flops | bytes accessed | tf_op | source)
XLA Modules:
  0.0 222.0 jit_solution(12663006208822952817)
XLA Ops:
  0.6 4.4 %shard_map.102 = bf16[8,4,400,128]{3,2,1,0:T(8,128)(2,1)} custom-call(s32[8,8,8]{2,1,0:T(8,128)} %refs_0_.2, s32[3,8,8]{2,1,0:T(8,128)} %bitcast.28, bf16[128,4096]{1,0:T(8,128)(2,1)} %refs_2_.1, bf16[128,4096]{1,0:T(8,128)(2,1)} %refs_3_.1, bf16[128,4096]{1,0:T(8,128)(2,1)} %refs_0_.3, bf16[128,4096]{1,0:T(8,128)(2,1)} %refs_1_.1), custom_call_target="tpu_custom_call" | custom-call | bytes 6553600 | tf_op jit(solution)/shard_map/pallas_call | solution.py:69
  5.1 7.3 %all-to-all-start = ((bf16[32,400,128]{2,1,0:T(8,128)(2,1)}), bf16[32,400,128]{2,1,0:T(8,128)(2,1)S(1)}, u32[]{:S(2)}, u32[]{:S(2)}) async-start(bf16[32,400,128]{2,1,0:T(8,128)(2,1)} %bitcast.21), calls=%async_computation | async-start | bytes 6553600 | tf_op jit(solution)/shard_map/all_to_all | solution.py:409
  12.4 0.0 copy-start.9
  12.4 3.5 %shard_map.103 = bf16[8,4,128,128]{3,2,1,0:T(8,128)(2,1)} custom-call(bf16[128,4096]{1,0:T(8,128)(2,1)} %refs_0_.3, bf16[128,4096]{1,0:T(8,128)(2,1)} %refs_1_.1), custom_call_target="tpu_custom_call" | custom-call | bytes 2097152 | tf_op jit(solution)/shard_map/pallas_call | solution.py:69
  15.9 70.8 %all-to-all-done = bf16[32,400,128]{2,1,0:T(8,128)(2,1)S(1)} async-done(((bf16[32,400,128]{2,1,0:T(8,128)(2,1)}), bf16[32,400,128]{2,1,0:T(8,128)(2,1)S(1)}, u32[]{:S(2)}, u32[]{:S(2)}) %all-to-all-start) | async-done | bytes 3276832 | tf_op jit(solution)/shard_map/all_to_all | solution.py:409
  86.6 0.0 copy-start.1
  86.6 4.1 %all-to-all-start.1 = ((bf16[32,128,128]{2,1,0:T(8,128)(2,1)}), bf16[32,128,128]{2,1,0:T(8,128)(2,1)}, u32[]{:S(2)}, u32[]{:S(2)}) async-start(bf16[32,128,128]{2,1,0:T(8,128)(2,1)} %bitcast.22), calls=%async_computation.1 | async-start | bytes 2097152 | tf_op jit(solution)/shard_map/all_to_all | solution.py:409
  90.8 0.1 reshape.76
  90.9 0.0 copy-done.9
  90.9 0.1 broadcast_in_dim.2
  91.0 0.1 copy.17
  91.1 0.1 min.12.ids_ref
  91.1 0.0 copy-start.8
  91.2 0.6 fusion.1.starts_ref
  91.7 0.6 slice_bitcast_fusion.drop_ref
  92.3 0.0 copy-done.1
  92.3 0.0 copy-done.8
  92.3 14.3 %shard_map.104 = (bf16[512,128]{1,0:T(8,128)(2,1)}, bf16[512,128]{1,0:T(8,128)(2,1)}, bf16[512,128]{1,0:T(8,128)(2,1)}, bf16[512,128]{1,0:T(8,128)(2,1)}, bf16[5...) custom-call(s32[512]{0:T(512)} %copy-done.8, ...), custom_call_target="tpu_custom_call" | custom-call | flops 17179869184 | bytes 10747904 | tf_op jit(solution)/shard_map/pallas_call | solution.py:351
  106.6 10.3 %all-to-all-done.1 = bf16[32,128,128]{2,1,0:T(8,128)(2,1)} async-done(((bf16[32,128,128]{2,1,0:T(8,128)(2,1)}), bf16[32,128,128]{2,1,0:T(8,128)(2,1)}, u32[]{:S(2)}, u32[]{:S(2)}) %all-to-all-start.1) | async-done | bytes 1048608 | tf_op jit(solution)/shard_map/all_to_all | solution.py:409
  116.9 0.8 collective-permute-start
  117.7 3.1 %collective-permute-start.1 = (bf16[512,128]{1,0:T(8,128)(2,1)}, bf16[512,128]{1,0:T(8,128)(2,1)S(1)}, u32[]{:S(2)}, u32[]{:S(2)}) collective-permute-start(bf16[512,128]{1,0:T(8,128)(2,1)} %get-tuple-element.42), channel_id=1, source_target_pairs={{0,20},{4,16},{8,28},{12,24},{16,4},{20,0},{24,12},{28,8},{1,21},{... | collective-permute-start | bytes 393224 | tf_op jit(solution)/shard_map/ppermute | solution.py:422
  120.8 1.5 collective-permute-start.2
  122.3 2.3 %collective-permute-start.3 = (bf16[512,128]{1,0:T(8,128)(2,1)}, bf16[512,128]{1,0:T(8,128)(2,1)}, u32[]{:S(2)}, u32[]{:S(2)}) collective-permute-start(bf16[512,128]{1,0:T(8,128)(2,1)} %get-tuple-element.44), channel_id=1, source_target_pairs={{0,28},{4,24},{8,20},{12,16},{16,12},{20,8},{24,4},{28,0},{1,29},{... | collective-permute-start | bytes 393224 | tf_op jit(solution)/shard_map/ppermute | solution.py:422
  124.6 15.0 %shard_map.105 = bf16[8,1536,128]{2,1,0:T(8,128)(2,1)} custom-call(s32[512]{0:T(512)} %copy-done.8, s32[512]{0:T(512)} %fusion.1.starts_ref, s32[1]{0:T(128)} %bitcast.5.first_ref, s32[1]{0:T(128)} %bitcast.6.member_ref, s32[64,8]{1,0:T(8,128)} %slice_bitcast_fusion.drop_ref, bf16[12800,128]{1,0:T(8,128)(2,1)} %bitcast.25, ...), custom_call_target="tpu_custom_call" | custom-call | flops 17179869184 | bytes 8519680 | tf_op jit(solution)/shard_map/pallas_call | solution.py:351
  139.6 0.0 collective-permute-done.refs_4_
  139.6 0.0 copy-start.2
  139.6 0.0 collective-permute-done.1.refs_5_
  139.6 0.0 copy-start.3
  139.6 0.0 collective-permute-done.2.refs_6_
  139.6 0.0 copy-start.4
  139.6 0.0 collective-permute-done.3.refs_7_
  139.7 6.1 %all-to-all-start.2 = ((bf16[8,1536,128]{2,1,0:T(8,128)(2,1)}), bf16[8,1536,128]{2,1,0:T(8,128)(2,1)S(1)}, u32[]{:S(2)}, u32[]{:S(2)}) async-start(bf16[8,1536,128]{2,1,0:T(8,128)(2,1)} %shard_map.105), calls=%async_computation.2 | async-start | bytes 6291456 | tf_op jit(solution)/shard_map/all_to_all | solution.py:503
  145.7 2.0 collective-permute-start.4
  147.7 1.5 collective-permute-start.5
  149.2 0.0 collective-permute-start.6
  149.2 25.6 %collective-permute-done.4.refs_1_ = bf16[512,128]{1,0:T(8,128)(2,1)S(1)} collective-permute-done((bf16[512,128]{1,0:T(8,128)(2,1)}, bf16[512,128]{1,0:T(8,128)(2,1)S(1)}, u32[]{:S(2)}, u32[]{:S(2)}) %collective-permute-start.4) | collective-permute-done | bytes 131104 | tf_op jit(solution)/shard_map/ppermute | solution.py:422
  174.8 26.5 %collective-permute-done.5.refs_2_ = bf16[512,128]{1,0:T(8,128)(2,1)S(1)} collective-permute-done((bf16[512,128]{1,0:T(8,128)(2,1)}, bf16[512,128]{1,0:T(8,128)(2,1)S(1)}, u32[]{:S(2)}, u32[]{:S(2)}) %collective-permute-start.5) | collective-permute-done | bytes 131104 | tf_op jit(solution)/shard_map/ppermute | solution.py:422
  201.3 1.4 collective-permute-done.6.refs_3_
  202.7 0.0 copy-done.2
  202.7 0.0 copy-done.3
  202.7 0.0 copy-done.4
  202.7 0.0 copy-done.5
  202.7 0.0 copy-done.6
  202.7 0.6 copy-done.7
  203.3 2.6 %shard_map.106 = (bf16[4,2,64,1024]{3,2,1,0:T(8,128)(2,1)}, bf16[4,2,64,1024]{3,2,1,0:T(8,128)(2,1)}) custom-call(s32[1]{0:T(128)} %bitcast.6.member_ref, bf16[512,128]{1,0:T(8,128)(2,1)} %get-tuple-element.46.refs_0_, bf16[512,128]{1,0:T(8,128)(2,1)} %copy-done.5, bf16[512,128]{1,0:T(8,128)(2,1)} %copy-done.6, bf16[512,128]{1,0:T(8,128)(2,1)} %copy-done.7, ...), custom_call_target="tpu_custom_call" | custom-call | bytes 2097152 | tf_op jit(solution)/shard_map/pallas_call | solution.py:110
  205.9 10.2 %all-to-all-done.2.piece_ref = bf16[8,1536,128]{2,1,0:T(8,128)(2,1)S(1)} async-done(((bf16[8,1536,128]{2,1,0:T(8,128)(2,1)}), bf16[8,1536,128]{2,1,0:T(8,128)(2,1)S(1)}, u32[]{:S(2)}, u32[]{:S(2)}) %all-to-all-start.2) | async-done | bytes 3145760 | tf_op jit(solution)/shard_map/all_to_all | solution.py:503
  216.0 1.6 copy-done
  217.7 4.3 %shard_map.107 = (bf16[4,2,64,1024]{3,2,1,0:T(8,128)(2,1)}, bf16[4,2,64,1024]{3,2,1,0:T(8,128)(2,1)}, bf16[1,1,512,1024]{3,2,1,0:T(8,128)(2,1)}, bf16[1,1,512,1024]{3,2,1,0:T(8,128)(2,1)}) custom-call(bf16[8,1536,128]{2,1,0:T(8,128)(2,1)} %copy-done, ...), custom_call_target="tpu_custom_call", output_to_operand_aliasing={{0}: (1, {}), {1}: (2, {})} | custom-call | bytes 6291456 | tf_op jit(solution)/shard_map/pallas_call | solution.py:155
  (12 shorter events, 0.1 us)
Async XLA Ops:
  5.1 81.6 %all-to-all-start = ((bf16[32,400,128]{2,1,0:T(8,128)(2,1)}), bf16[32,400,128]{2,1,0:T(8,128)(2,1)S(1)}, u32[]{:S(2)}, u32[]{:S(2)}) async-start(bf16[32,400,128]{2,1,0:T(8,128)(2,1)} %bitcast.21), calls=%async_computation | async-start | bytes 6553600 | tf_op jit(solution)/shard_map/all_to_all | solution.py:409
  12.4 78.5 %copy-start.9 = (s32[2]{0:T(128)S(1)}, s32[2]{0:T(128)}, u32[]{:S(2)}) copy-start(s32[2]{0:T(128)} %param.12) | copy-start | bytes 28
  86.6 5.7 %copy-start.1 = (bf16[32,400,128]{2,1,0:T(8,128)(2,1)}, bf16[32,400,128]{2,1,0:T(8,128)(2,1)S(1)}, u32[]{:S(2)}) copy-start(bf16[32,400,128]{2,1,0:T(8,128)(2,1)S(1)} %all-to-all-done) | copy-start | bytes 9830404
  86.6 30.3 %all-to-all-start.1 = ((bf16[32,128,128]{2,1,0:T(8,128)(2,1)}), bf16[32,128,128]{2,1,0:T(8,128)(2,1)}, u32[]{:S(2)}, u32[]{:S(2)}) async-start(bf16[32,128,128]{2,1,0:T(8,128)(2,1)} %bitcast.22), calls=%async_computation.1 | async-start | bytes 2097152 | tf_op jit(solution)/shard_map/all_to_all | solution.py:409
  91.1 1.2 copy-start.8
  116.9 22.7 %collective-permute-start = (bf16[512,128]{1,0:T(8,128)(2,1)}, bf16[512,128]{1,0:T(8,128)(2,1)S(1)}, u32[]{:S(2)}, u32[]{:S(2)}) collective-permute-start(bf16[512,128]{1,0:T(8,128)(2,1)} %get-tuple-element.41), channel_id=1, source_target_pairs={{0,16},{4,20},{8,24},{12,28},{16,0},{20,4},{24,8},{28,12},{1,17},{... | collective-permute-start | bytes 393224 | tf_op jit(solution)/shard_map/ppermute | solution.py:422
  117.7 21.9 %collective-permute-start.1 = (bf16[512,128]{1,0:T(8,128)(2,1)}, bf16[512,128]{1,0:T(8,128)(2,1)S(1)}, u32[]{:S(2)}, u32[]{:S(2)}) collective-permute-start(bf16[512,128]{1,0:T(8,128)(2,1)} %get-tuple-element.42), channel_id=1, source_target_pairs={{0,20},{4,16},{8,28},{12,24},{16,4},{20,0},{24,12},{28,8},{1,21},{... | collective-permute-start | bytes 393224 | tf_op jit(solution)/shard_map/ppermute | solution.py:422
  120.8 18.9 %collective-permute-start.2 = (bf16[512,128]{1,0:T(8,128)(2,1)}, bf16[512,128]{1,0:T(8,128)(2,1)S(1)}, u32[]{:S(2)}, u32[]{:S(2)}) collective-permute-start(bf16[512,128]{1,0:T(8,128)(2,1)} %get-tuple-element.43), channel_id=1, source_target_pairs={{0,24},{4,28},{8,16},{12,20},{16,8},{20,12},{24,0},{28,4},{1,25},{... | collective-permute-start | bytes 393224 | tf_op jit(solution)/shard_map/ppermute | solution.py:422
  122.3 17.4 %collective-permute-start.3 = (bf16[512,128]{1,0:T(8,128)(2,1)}, bf16[512,128]{1,0:T(8,128)(2,1)}, u32[]{:S(2)}, u32[]{:S(2)}) collective-permute-start(bf16[512,128]{1,0:T(8,128)(2,1)} %get-tuple-element.44), channel_id=1, source_target_pairs={{0,28},{4,24},{8,20},{12,16},{16,12},{20,8},{24,4},{28,0},{1,29},{... | collective-permute-start | bytes 393224 | tf_op jit(solution)/shard_map/ppermute | solution.py:422
  139.6 63.1 %copy-start.2 = (bf16[512,128]{1,0:T(8,128)(2,1)}, bf16[512,128]{1,0:T(8,128)(2,1)S(1)}, u32[]{:S(2)}) copy-start(bf16[512,128]{1,0:T(8,128)(2,1)S(1)} %collective-permute-done.refs_4_) | copy-start | bytes 393220
  139.6 63.1 %copy-start.3 = (bf16[512,128]{1,0:T(8,128)(2,1)}, bf16[512,128]{1,0:T(8,128)(2,1)S(1)}, u32[]{:S(2)}) copy-start(bf16[512,128]{1,0:T(8,128)(2,1)S(1)} %collective-permute-done.1.refs_5_) | copy-start | bytes 393220
  139.6 63.1 %copy-start.4 = (bf16[512,128]{1,0:T(8,128)(2,1)}, bf16[512,128]{1,0:T(8,128)(2,1)S(1)}, u32[]{:S(2)}) copy-start(bf16[512,128]{1,0:T(8,128)(2,1)S(1)} %collective-permute-done.2.refs_6_) | copy-start | bytes 393220
  139.7 76.4 %all-to-all-start.2 = ((bf16[8,1536,128]{2,1,0:T(8,128)(2,1)}), bf16[8,1536,128]{2,1,0:T(8,128)(2,1)S(1)}, u32[]{:S(2)}, u32[]{:S(2)}) async-start(bf16[8,1536,128]{2,1,0:T(8,128)(2,1)} %shard_map.105), calls=%async_computation.2 | async-start | bytes 6291456 | tf_op jit(solution)/shard_map/all_to_all | solution.py:503
  145.7 29.1 %collective-permute-start.4 = (bf16[512,128]{1,0:T(8,128)(2,1)}, bf16[512,128]{1,0:T(8,128)(2,1)S(1)}, u32[]{:S(2)}, u32[]{:S(2)}) collective-permute-start(bf16[512,128]{1,0:T(8,128)(2,1)} %get-tuple-element.47), channel_id=1, source_target_pairs={{0,4},{4,0},{8,12},{12,8},{16,20},{20,16},{24,28},{28,24},{1,5},{5... | collective-permute-start | bytes 393224 | tf_op jit(solution)/shard_map/ppermute | solution.py:422
  147.7 53.5 %collective-permute-start.5 = (bf16[512,128]{1,0:T(8,128)(2,1)}, bf16[512,128]{1,0:T(8,128)(2,1)S(1)}, u32[]{:S(2)}, u32[]{:S(2)}) collective-permute-start(bf16[512,128]{1,0:T(8,128)(2,1)} %get-tuple-element.48), channel_id=1, source_target_pairs={{0,8},{4,12},{8,0},{12,4},{16,24},{20,28},{24,16},{28,20},{1,9},{5... | collective-permute-start | bytes 393224 | tf_op jit(solution)/shard_map/ppermute | solution.py:422
  149.2 53.5 %collective-permute-start.6 = (bf16[512,128]{1,0:T(8,128)(2,1)}, bf16[512,128]{1,0:T(8,128)(2,1)S(1)}, u32[]{:S(2)}, u32[]{:S(2)}) collective-permute-start(bf16[512,128]{1,0:T(8,128)(2,1)} %get-tuple-element.49), channel_id=1, source_target_pairs={{0,12},{4,8},{8,4},{12,0},{16,28},{20,24},{24,20},{28,16},{1,13},{... | collective-permute-start | bytes 393224 | tf_op jit(solution)/shard_map/ppermute | solution.py:422
  174.8 27.9 %copy-start.5 = (bf16[512,128]{1,0:T(8,128)(2,1)}, bf16[512,128]{1,0:T(8,128)(2,1)S(1)}, u32[]{:S(2)}) copy-start(bf16[512,128]{1,0:T(8,128)(2,1)S(1)} %collective-permute-done.4.refs_1_) | copy-start | bytes 393220
  201.3 1.4 copy-start.6
  202.7 0.6 copy-start.7
  216.0 1.6 copy-start

commit v3 on v2

--- a/solution.py
+++ b/solution.py
@@ -16,12 +16,16 @@
 WIDE = SLOTS * BLOCK_TOKENS
 UNROLL = 2
 STRIP = 16
-VMEM_LIMIT = 56 * 1024 * 1024
+VMEM_LIMIT = 16 * 1024 * 1024
 
 keep_prob = 0.9
 
 vmem = pl.BlockSpec(memory_space=pltpu.VMEM)
 smem = pl.BlockSpec(memory_space=pltpu.SMEM)
+
+
+def in_vmem(array):
+    return pltpu.with_memory_space_constraint(array, pltpu.VMEM)
 
 
 def copy_cost(size):
@@ -69,25 +73,26 @@
     packed = pl.pallas_call(
         functools.partial(pack_kernel, heads, table_rows),
         grid=(groups,),
-        out_shape=jax.ShapeDtypeStruct(shape, jnp.bfloat16),
+        out_shape=pltpu.VMEM(shape, jnp.bfloat16),
         in_specs=specs,
         out_specs=pl.BlockSpec((heads, 1, total, HEAD_WIDTH), lambda g: (0, g, 0, 0)),
         scratch_shapes=[pltpu.VMEM((table_rows, HEAD_WIDTH), jnp.float32)] if table_rows else [],
         compiler_params=pltpu.CompilerParams(vmem_limit_bytes=VMEM_LIMIT),
         cost_estimate=copy_cost(math.prod(shape)),
-    )(*tables, *[array for array, _, _ in sources])
+    )(*tables, *[pltpu.with_memory_space_constraint(a, pltpu.HBM) for a, _, _ in sources])
     return packed.reshape(heads * groups, total, HEAD_WIDTH)
 
 
 def unpack_kernel(parts, member_ref, *refs):
     outs = refs[len(refs) - len(parts) :]
     heads = outs[0].shape[-1] // HEAD_WIDTH
-    for k in range(heads):
+    for n in range(heads):
+        k = (heads - n) % heads
         column = pl.multiple_of((member_ref[0] ^ k) * HEAD_WIDTH, HEAD_WIDTH)
         for begin, out in zip(parts, outs):
             runs, _, rows, _ = out.shape
             for i in range(runs):
-                out[i, 0, :, pl.ds(column, HEAD_WIDTH)] = refs[k][pl.ds(begin + i * rows, rows), :]
+                out[i, 0, :, pl.ds(column, HEAD_WIDTH)] = refs[n][pl.ds(begin + i * rows, rows), :]
 
 
 def unpack(member, received, parts):
@@ -118,7 +123,7 @@
         input_output_aliases=aliases,
         compiler_params=pltpu.CompilerParams(vmem_limit_bytes=VMEM_LIMIT),
         cost_estimate=copy_cost(size),
-    )(member, *received, *olds)
+    )(member, received[0], *received[:0:-1], *olds)
 
 
 def unpack_all_kernel(begins, step_heads, piece_ref, *refs):
@@ -162,7 +167,7 @@
         input_output_aliases=aliases,
         compiler_params=pltpu.CompilerParams(vmem_limit_bytes=VMEM_LIMIT),
         cost_estimate=copy_cost(size),
-    )(received, *olds)
+    )(in_vmem(received), *olds)
 
 
 def attention_kernel(
@@ -328,9 +333,7 @@
     out_rows = steps * BLOCK_TOKENS // targets
     if joined:
         out_shape = [
-            jax.ShapeDtypeStruct(
-                (targets, 2 * out_rows + 2 * length // targets, HEAD_WIDTH), jnp.bfloat16
-            )
+            pltpu.VMEM((targets, 2 * out_rows + 2 * length // targets, HEAD_WIDTH), jnp.bfloat16)
         ]
     else:
         out_shape = [jax.ShapeDtypeStruct((2 * out_rows, HEAD_WIDTH), jnp.bfloat16)] * targets
@@ -345,7 +348,9 @@
         out_shape.append(jax.ShapeDtypeStruct(accumulator, jnp.float32))
     if start is not None:
         scratch += [pltpu.VMEM(accumulator, jnp.float32), pltpu.SemaphoreType.DMA]
-    flat = [t.reshape(-1, HEAD_WIDTH) for t in (kv, qd) if t is not None]
+    sums_bytes = 8 * length * HEAD_WIDTH
+    limit = VMEM_LIMIT + 2 * (kv.size + source.size) + (2 if start is not None else 1) * sums_bytes
+    flat = [in_vmem(t.reshape(-1, HEAD_WIDTH)) for t in (kv, qd) if t is not None]
     operands = flat + ([] if start is None else [start])
     operand_specs = [vmem] * len(flat) + [pl.BlockSpec(memory_space=pl.ANY)] * (start is not None)
     return pl.pallas_call(
@@ -369,7 +374,7 @@
         in_specs=[smem, smem, smem, smem, vmem] + operand_specs,
         out_specs=[vmem] * len(out_shape),
         scratch_shapes=scratch,
-        compiler_params=pltpu.CompilerParams(vmem_limit_bytes=VMEM_LIMIT),
+        compiler_params=pltpu.CompilerParams(vmem_limit_bytes=limit),
         cost_estimate=pl.CostEstimate(
             flops=128 * pairs * HEAD_WIDTH,
             bytes_accessed=2 * (source.size + kv.size) + 8 * length * HEAD_WIDTH,
@@ -497,9 +502,7 @@
     if whole:
         rest = pieces_out[-1][0]
         if near:
-            rest, *near[-1][heads // 2 :] = lax.optimization_barrier(
-                (rest, *near[-1][heads // 2 :])
-            )
+            rest, near[-1][heads // 2] = lax.optimization_barrier((rest, near[-1][heads // 2]))
         rest = lax.all_to_all(rest, "seq", split_axis=0, concat_axis=0, tiled=True)
     for c in range(len(near)):
         parts = [(0, rows, runs, pieces, c, att), (begin, rows, runs, pieces, c, dq)]

time: 223 us -> 236 us (1.058)
  waiting for transfers between devices: 145 us -> 159 us
  local copies, waits for them, and re-layouts: 3.25 us -> 13.5 us
  Pallas kernels: 44.1 us -> 34.8 us
    ppermute x7, waiting for transfers between devices: 53.5 us -> 80.2 us  [to_shards(): received[k] = lax.ppermute(results[k], 'seq', pairs)]
    unnamed x20 -> x30, local copies, waits for them, and re-layouts: 2.27 us -> 13.2 us
    all_to_all x1, waiting for transfers between devices: 10.2 us -> 0.01 us  [per_device(): rest = lax.all_to_all(rest, 'seq', split_axis=0, concat_axis=0, tiled=True)]
    pallas_call x2, Pallas kernels: 29.3 us -> 23.3 us  [attend(): pl.pallas_call(functools.partial(attention_kernel, total_blocks - 1, devi...]
    all_to_all x2, waiting for transfers between devices: 81 us -> 78.6 us  [to_heads(): lax.all_to_all(packed, ('seq', 'head'), split_axis=0, concat_axis=0, tile...]
  transfers between devices with their start and end apart: 10 -> 10, of which waited for: 6 -> 5; matrix products, arithmetic and copies ran while one was open for 1% -> 0% of each run, Pallas kernels for 16% -> 12%
where the time goes in v3:
time: 236 us; the launch traced here: 235 us
  waiting for transfers between devices  159 us (67%)
  Pallas kernels  34.8 us (15%)
  starting transfers between devices  27 us (11%)
  local copies, waits for them, and re-layouts  13.5 us (6%)
    ppermute x7, waiting for transfers between devices, to_shards(): received[k] = lax.ppermute(results[k], 'seq', pairs)  80.2 us
    all_to_all x2, waiting for transfers between devices, to_heads(): lax.all_to_all(packed, ('seq', 'head'), split_axis=0, concat_axis=0, tile...  78.6 us
    pallas_call x2, Pallas kernels, attend(): pl.pallas_call(functools.partial(attention_kernel, total_blocks - 1, devi...  23.3 us
    unnamed x30, local copies, waits for them, and re-layouts  13.2 us
    all_to_all x2, starting transfers between devices, to_heads(): lax.all_to_all(packed, ('seq', 'head'), split_axis=0, concat_axis=0, tile...  11.4 us
    ppermute x7, starting transfers between devices, to_shards(): received[k] = lax.ppermute(results[k], 'seq', pairs)  11.3 us
    pallas_call x2, Pallas kernels, pack(): pl.pallas_call(functools.partial(pack_kernel, heads, table_rows), grid=(g...  7.96 us
  transfers between devices with their start and end apart: 10, of which 5 were waited for; matrix products, arithmetic and copies ran while one was open for 0% of the time, Pallas kernels for 12%

profile of v3, /device:TPU:0, one launch (start us, length us, event | category | flops | bytes accessed | tf_op | source)
XLA Modules:
  0.0 235.0 jit_solution(11015905960750596279)
XLA Ops:
  0.6 0.0 copy-start.1
  0.6 0.7 copy-done.1
  1.4 0.7 copy-done.4
  2.1 4.5 %shard_map.102 = bf16[8,4,400,128]{3,2,1,0:T(8,128)(2,1)} custom-call(s32[8,8,8]{2,1,0:T(8,128)S(1)} %copy-done.1, s32[3,8,8]{2,1,0:T(8,128)S(1)} %bitcast.24, bf16[128,4096]{1,0:T(8,128)(2,1)} %refs_2_.1, bf16[128,4096]{1,0:T(8,128)(2,1)} %refs_3_.1, bf16[128,4096]{1,0:T(8,128)(2,1)} %refs_0_.3, bf16[128,4096]{1,0:T(8,128)(2,1)} %refs_1_.1), custom_call_target="tpu_custom_call" | custom-call | bytes 6553600 | tf_op jit(solution)/shard_map/pallas_call | solution.py:73
  6.6 7.3 %all-to-all-start = ((bf16[32,400,128]{2,1,0:T(8,128)(2,1)}), bf16[32,400,128]{2,1,0:T(8,128)(2,1)S(1)}, u32[]{:S(2)}, u32[]{:S(2)}) async-start(bf16[32,400,128]{2,1,0:T(8,128)(2,1)} %bitcast.1), calls=%async_computation | async-start | bytes 6553600 | tf_op jit(solution)/shard_map/all_to_all | solution.py:414
  13.9 0.0 copy-start.14
  13.9 3.5 %shard_map.103 = bf16[8,4,128,128]{3,2,1,0:T(8,128)(2,1)} custom-call(bf16[128,4096]{1,0:T(8,128)(2,1)} %refs_0_.3, bf16[128,4096]{1,0:T(8,128)(2,1)} %refs_1_.1), custom_call_target="tpu_custom_call" | custom-call | bytes 2097152 | tf_op jit(solution)/shard_map/pallas_call | solution.py:73
  17.4 70.8 %all-to-all-done = bf16[32,400,128]{2,1,0:T(8,128)(2,1)S(1)} async-done(((bf16[32,400,128]{2,1,0:T(8,128)(2,1)}), bf16[32,400,128]{2,1,0:T(8,128)(2,1)S(1)}, u32[]{:S(2)}, u32[]{:S(2)}) %all-to-all-start) | async-done | bytes 3276832 | tf_op jit(solution)/shard_map/all_to_all | solution.py:414
  88.1 4.1 %all-to-all-start.1 = ((bf16[32,128,128]{2,1,0:T(8,128)(2,1)}), bf16[32,128,128]{2,1,0:T(8,128)(2,1)}, u32[]{:S(2)}, u32[]{:S(2)}) async-start(bf16[32,128,128]{2,1,0:T(8,128)(2,1)} %bitcast.10), calls=%async_computation.1 | async-start | bytes 2097152 | tf_op jit(solution)/shard_map/all_to_all | solution.py:414
  92.3 0.1 reshape.76
  92.4 0.0 copy-done.14
  92.4 0.1 broadcast_in_dim.2
  92.5 0.1 copy.17
  92.6 0.1 min.12.ids_ref
  92.7 10.8 %shard_map.104 = (bf16[512,128]{1,0:T(8,128)(2,1)S(1)}, bf16[512,128]{1,0:T(8,128)(2,1)S(1)}, bf16[512,128]{1,0:T(8,128)(2,1)S(1)}, bf16[512,128]{1,0:T(8,128)(2...) custom-call(s32[512]{0:T(512)S(1)} %min.12.ids_ref, ...), custom_call_target="tpu_custom_call" | custom-call | flops 17179869184 | bytes 10747904 | tf_op jit(solution)/shard_map/pallas_call | solution.py:356
  103.5 0.0 copy-start.2
  103.5 0.6 copy-done.2
  104.1 0.7 copy-done.5
  104.7 0.7 copy-done.6
  105.4 0.7 copy-done.7
  106.1 0.7 copy-done.8
  106.7 0.7 copy-done.9
  107.4 0.7 copy-done.10
  108.0 0.6 copy-done.11
  108.7 2.0 copy-done.12
  110.6 7.8 %all-to-all-done.1 = bf16[32,128,128]{2,1,0:T(8,128)(2,1)} async-done(((bf16[32,128,128]{2,1,0:T(8,128)(2,1)}), bf16[32,128,128]{2,1,0:T(8,128)(2,1)}, u32[]{:S(2)}, u32[]{:S(2)}) %all-to-all-start.1) | async-done | bytes 1048608 | tf_op jit(solution)/shard_map/all_to_all | solution.py:414
  118.4 0.8 collective-permute-start
  119.2 0.8 copy-done.3
  120.0 2.2 copy-done.13
  122.1 12.5 %shard_map.105 = bf16[8,1536,128]{2,1,0:T(8,128)(2,1)S(1)} custom-call(s32[512]{0:T(512)S(1)} %min.12.ids_ref, s32[512]{0:T(512)S(1)} %fusion.1.starts_ref, s32[1]{0:T(128)} %bitcast.5.first_ref, s32[1]{0:T(128)} %bitcast.6.member_ref, s32[64,8]{1,0:T(8,128)S(1)} %copy-done.3, bf16[12800,128]{1,0:T(8,128)(2,1)S(1)} %bitcast.23, ...), custom_call_target="tpu_custom_call" | custom-call | flops 17179869184 | bytes 8519680 | tf_op jit(solution)/shard_map/pallas_call | solution.py:356
  134.7 1.6 copy-done
  136.3 0.0 collective-permute-done.refs_4_
  136.3 4.3 %all-to-all-start.2 = ((bf16[8,1536,128]{2,1,0:T(8,128)(2,1)}), bf16[8,1536,128]{2,1,0:T(8,128)(2,1)S(1)}, u32[]{:S(2)}, u32[]{:S(2)}) async-start(bf16[8,1536,128]{2,1,0:T(8,128)(2,1)} %copy-done), calls=%async_computation.2 | async-start | bytes 6291456 | tf_op jit(solution)/shard_map/all_to_all | solution.py:506
  140.6 4.7 %collective-permute-start.1 = (bf16[512,128]{1,0:T(8,128)(2,1)}, bf16[512,128]{1,0:T(8,128)(2,1)S(1)}, u32[]{:S(2)}, u32[]{:S(2)}) collective-permute-start(bf16[512,128]{1,0:T(8,128)(2,1)} %copy-done.10), channel_id=1, source_target_pairs={{0,28},{4,24},{8,20},{12,16},{16,12},{20,8},{24,4},{28,0},{1,29},{... | collective-permute-start | bytes 393224 | tf_op jit(solution)/shard_map/ppermute | solution.py:427
  145.4 0.6 collective-permute-start.2
  145.9 0.6 collective-permute-start.3
  146.5 4.2 %collective-permute-start.4 = (bf16[512,128]{1,0:T(8,128)(2,1)}, bf16[512,128]{1,0:T(8,128)(2,1)S(1)}, u32[]{:S(2)}, u32[]{:S(2)}) collective-permute-start(bf16[512,128]{1,0:T(8,128)(2,1)} %copy-done.7), channel_id=1, source_target_pairs={{0,12},{4,8},{8,4},{12,0},{16,28},{20,24},{24,20},{28,16},{1,13},{... | collective-permute-start | bytes 393224 | tf_op jit(solution)/shard_map/ppermute | solution.py:427
  150.7 0.0 collective-permute-start.5
  150.7 50.0 %collective-permute-done.1.refs_1_ = bf16[512,128]{1,0:T(8,128)(2,1)S(1)} collective-permute-done((bf16[512,128]{1,0:T(8,128)(2,1)}, bf16[512,128]{1,0:T(8,128)(2,1)S(1)}, u32[]{:S(2)}, u32[]{:S(2)}) %collective-permute-start.1) | collective-permute-done | bytes 131104 | tf_op jit(solution)/shard_map/ppermute | solution.py:427
  200.7 0.6 collective-permute-start.6
  201.2 1.3 collective-permute-done.2.refs_2_
  202.6 28.8 %collective-permute-done.3.refs_3_ = bf16[512,128]{1,0:T(8,128)(2,1)S(1)} collective-permute-done((bf16[512,128]{1,0:T(8,128)(2,1)}, bf16[512,128]{1,0:T(8,128)(2,1)S(1)}, u32[]{:S(2)}, u32[]{:S(2)}) %collective-permute-start.3) | collective-permute-done | bytes 131104 | tf_op jit(solution)/shard_map/ppermute | solution.py:427
  231.4 0.0 collective-permute-done.4.refs_5_
  231.4 0.0 collective-permute-done.5.refs_6_
  231.4 0.0 collective-permute-done.6.refs_7_
  231.4 1.3 shard_map.106
  232.7 0.0 all-to-all-done.2.piece_ref
  232.7 2.3 shard_map.107
  (22 shorter events, 0.1 us)
Async XLA Ops:
  0.6 0.8 copy-start.1
  1.4 0.7 copy-start.4
  6.6 81.6 %all-to-all-start = ((bf16[32,400,128]{2,1,0:T(8,128)(2,1)}), bf16[32,400,128]{2,1,0:T(8,128)(2,1)S(1)}, u32[]{:S(2)}, u32[]{:S(2)}) async-start(bf16[32,400,128]{2,1,0:T(8,128)(2,1)} %bitcast.1), calls=%async_computation | async-start | bytes 6553600 | tf_op jit(solution)/shard_map/all_to_all | solution.py:414
  13.9 78.5 %copy-start.14 = (s32[2]{0:T(128)S(1)}, s32[2]{0:T(128)}, u32[]{:S(2)}) copy-start(s32[2]{0:T(128)} %param.12) | copy-start | bytes 28
  88.1 30.3 %all-to-all-start.1 = ((bf16[32,128,128]{2,1,0:T(8,128)(2,1)}), bf16[32,128,128]{2,1,0:T(8,128)(2,1)}, u32[]{:S(2)}, u32[]{:S(2)}) async-start(bf16[32,128,128]{2,1,0:T(8,128)(2,1)} %bitcast.10), calls=%async_computation.1 | async-start | bytes 2097152 | tf_op jit(solution)/shard_map/all_to_all | solution.py:414
  103.5 0.6 copy-start.2
  104.1 0.7 copy-start.5
  104.7 0.7 copy-start.6
  105.4 0.7 copy-start.7
  106.0 0.7 copy-start.8
  106.7 0.7 copy-start.9
  107.4 0.7 copy-start.10
  108.0 0.7 copy-start.11
  108.7 2.0 copy-start.12
  118.4 17.9 %collective-permute-start = (bf16[512,128]{1,0:T(8,128)(2,1)}, bf16[512,128]{1,0:T(8,128)(2,1)S(1)}, u32[]{:S(2)}, u32[]{:S(2)}) collective-permute-start(bf16[512,128]{1,0:T(8,128)(2,1)} %copy-done.11), channel_id=1, source_target_pairs={{0,16},{4,20},{8,24},{12,28},{16,0},{20,4},{24,8},{28,12},{1,17},{... | collective-permute-start | bytes 393224 | tf_op jit(solution)/shard_map/ppermute | solution.py:427
  119.2 0.8 copy-start.3
  119.9 2.2 copy-start.13
  134.6 1.6 copy-start
  136.3 96.4 %all-to-all-start.2 = ((bf16[8,1536,128]{2,1,0:T(8,128)(2,1)}), bf16[8,1536,128]{2,1,0:T(8,128)(2,1)S(1)}, u32[]{:S(2)}, u32[]{:S(2)}) async-start(bf16[8,1536,128]{2,1,0:T(8,128)(2,1)} %copy-done), calls=%async_computation.2 | async-start | bytes 6291456 | tf_op jit(solution)/shard_map/all_to_all | solution.py:506
  140.6 60.0 %collective-permute-start.1 = (bf16[512,128]{1,0:T(8,128)(2,1)}, bf16[512,128]{1,0:T(8,128)(2,1)S(1)}, u32[]{:S(2)}, u32[]{:S(2)}) collective-permute-start(bf16[512,128]{1,0:T(8,128)(2,1)} %copy-done.10), channel_id=1, source_target_pairs={{0,28},{4,24},{8,20},{12,16},{16,12},{20,8},{24,4},{28,0},{1,29},{... | collective-permute-start | bytes 393224 | tf_op jit(solution)/shard_map/ppermute | solution.py:427
  145.4 57.2 %collective-permute-start.2 = (bf16[512,128]{1,0:T(8,128)(2,1)}, bf16[512,128]{1,0:T(8,128)(2,1)S(1)}, u32[]{:S(2)}, u32[]{:S(2)}) collective-permute-start(bf16[512,128]{1,0:T(8,128)(2,1)} %copy-done.9), channel_id=1, source_target_pairs={{0,24},{4,28},{8,16},{12,20},{16,8},{20,12},{24,0},{28,4},{1,25},{... | collective-permute-start | bytes 393224 | tf_op jit(solution)/shard_map/ppermute | solution.py:427
  145.9 85.5 %collective-permute-start.3 = (bf16[512,128]{1,0:T(8,128)(2,1)}, bf16[512,128]{1,0:T(8,128)(2,1)S(1)}, u32[]{:S(2)}, u32[]{:S(2)}) collective-permute-start(bf16[512,128]{1,0:T(8,128)(2,1)} %copy-done.8), channel_id=1, source_target_pairs={{0,20},{4,16},{8,28},{12,24},{16,4},{20,0},{24,12},{28,8},{1,21},{... | collective-permute-start | bytes 393224 | tf_op jit(solution)/shard_map/ppermute | solution.py:427
  146.5 84.9 %collective-permute-start.4 = (bf16[512,128]{1,0:T(8,128)(2,1)}, bf16[512,128]{1,0:T(8,128)(2,1)S(1)}, u32[]{:S(2)}, u32[]{:S(2)}) collective-permute-start(bf16[512,128]{1,0:T(8,128)(2,1)} %copy-done.7), channel_id=1, source_target_pairs={{0,12},{4,8},{8,4},{12,0},{16,28},{20,24},{24,20},{28,16},{1,13},{... | collective-permute-start | bytes 393224 | tf_op jit(solution)/shard_map/ppermute | solution.py:427
  150.7 80.8 %collective-permute-start.5 = (bf16[512,128]{1,0:T(8,128)(2,1)}, bf16[512,128]{1,0:T(8,128)(2,1)S(1)}, u32[]{:S(2)}, u32[]{:S(2)}) collective-permute-start(bf16[512,128]{1,0:T(8,128)(2,1)} %copy-done.6), channel_id=1, source_target_pairs={{0,8},{4,12},{8,0},{12,4},{16,24},{20,28},{24,16},{28,20},{1,9},{5... | collective-permute-start | bytes 393224 | tf_op jit(solution)/shard_map/ppermute | solution.py:427
  200.7 30.8 %collective-permute-start.6 = (bf16[512,128]{1,0:T(8,128)(2,1)}, bf16[512,128]{1,0:T(8,128)(2,1)S(1)}, u32[]{:S(2)}, u32[]{:S(2)}) collective-permute-start(bf16[512,128]{1,0:T(8,128)(2,1)} %copy-done.5), channel_id=1, source_target_pairs={{0,4},{4,0},{8,12},{12,8},{16,20},{20,16},{24,28},{28,24},{1,5},{5... | collective-permute-start | bytes 393224 | tf_op jit(solution)/shard_map/ppermute | solution.py:427

commit v4 on v3

--- a/solution.py
+++ b/solution.py
@@ -28,6 +28,10 @@
     return pltpu.with_memory_space_constraint(array, pltpu.VMEM)
 
 
+def in_hbm(array):
+    return pltpu.with_memory_space_constraint(array, pltpu.HBM)
+
+
 def copy_cost(size):
     return pl.CostEstimate(flops=0, bytes_accessed=4 * size, transcendentals=0)
 
@@ -39,17 +43,28 @@
     return pl.ds(start, BLOCK_TOKENS)
 
 
-def pack_kernel(heads, table_rows, *refs):
+def pack_kernel(heads, groups, sources, table_rows, *refs):
     refs = list(refs)
     if table_rows:
         drop_ref, rand_ref, table = refs.pop(0), refs.pop(0), refs.pop()
-    out_ref = refs.pop()
-    begin = 0
-    for ref in refs:
-        rows = ref.shape[0]
-        for m in range(heads):
-            out_ref[m, 0, pl.ds(begin, rows), :] = ref[:, pl.ds(m * HEAD_WIDTH, HEAD_WIDTH)]
-        begin += rows
+    count = len(sources)
+    arrays, out_ref = refs[:count], refs[count]
+    wholes, packed, in_sems, out_sems = refs[count + 1 : -3], refs[-3], refs[-2], refs[-1]
+    width = heads * HEAD_WIDTH
+    loads = []
+    for g in range(groups):
+        for n, (at, rows) in enumerate(sources):
+            columns = pl.ds(g * width, width)
+            loads.append(
+                pltpu.make_async_copy(
+                    arrays[n].at[pl.ds(at * rows, rows), columns],
+                    wholes[n].at[:, columns],
+                    in_sems.at[g, n],
+                )
+            )
+    for load in loads:
+        load.start()
+    begin = sum(rows for _, rows in sources)
     if table_rows:
         blocks = drop_ref.shape[1]
         table[...] = jnp.zeros_like(table)
@@ -59,27 +74,52 @@
                 table[pl.ds(blocks + r, 1), pl.ds(0, blocks)] = rand_ref[
                     r, pl.ds(m, 1), :
                 ].astype(jnp.float32)
-            out_ref[m, 0, pl.ds(begin, table_rows), :] = table[...].astype(jnp.bfloat16)
+            rounded = table[...].astype(jnp.bfloat16)
+            for g in range(groups):
+                packed[m, g, pl.ds(begin, table_rows), :] = rounded
+    stores = []
+    for g in range(groups):
+        for n in range(count):
+            loads[g * count + n].wait()
+        for m in range(heads):
+            begin = 0
+            for n, (_, rows) in enumerate(sources):
+                packed[m, g, pl.ds(begin, rows), :] = wholes[n][
+                    :, pl.ds((g * heads + m) * HEAD_WIDTH, HEAD_WIDTH)
+                ]
+                begin += rows
+            stores.append(
+                pltpu.make_async_copy(packed.at[m, g], out_ref.at[m, g], out_sems.at[g, m])
+            )
+            stores[-1].start()
+    for store in stores:
+        store.wait()
 
 
 def pack(groups, heads, sources, tables=(), table_rows=0):
-    specs = [pl.BlockSpec(t.shape, lambda g: (0, 0, 0)) for t in tables]
-    for _, at, rows in sources:
-        specs.append(
-            pl.BlockSpec((rows, heads * HEAD_WIDTH), functools.partial(lambda at, g: (at, g), at))
-        )
     total = sum(rows for _, _, rows in sources) + table_rows
     shape = (heads, groups, total, HEAD_WIDTH)
+    scratch = [
+        pltpu.VMEM((rows, groups * heads * HEAD_WIDTH), jnp.bfloat16) for _, _, rows in sources
+    ] + [
+        pltpu.VMEM(shape, jnp.bfloat16),
+        pltpu.SemaphoreType.DMA((groups, len(sources))),
+        pltpu.SemaphoreType.DMA((groups, heads)),
+    ]
+    if table_rows:
+        scratch.append(pltpu.VMEM((table_rows, HEAD_WIDTH), jnp.float32))
+    anywhere = pl.BlockSpec(memory_space=pl.ANY)
     packed = pl.pallas_call(
-        functools.partial(pack_kernel, heads, table_rows),
-        grid=(groups,),
-        out_shape=pltpu.VMEM(shape, jnp.bfloat16),
-        in_specs=specs,
-        out_specs=pl.BlockSpec((heads, 1, total, HEAD_WIDTH), lambda g: (0, g, 0, 0)),
-        scratch_shapes=[pltpu.VMEM((table_rows, HEAD_WIDTH), jnp.float32)] if table_rows else [],
+        functools.partial(
+            pack_kernel, heads, groups, tuple((at, rows) for _, at, rows in sources), table_rows
+        ),
+        out_shape=pltpu.HBM(shape, jnp.bfloat16),
+        in_specs=[vmem] * len(tables) + [anywhere] * len(sources),
+        out_specs=anywhere,
+        scratch_shapes=scratch,
         compiler_params=pltpu.CompilerParams(vmem_limit_bytes=VMEM_LIMIT),
         cost_estimate=copy_cost(math.prod(shape)),
-    )(*tables, *[pltpu.with_memory_space_constraint(a, pltpu.HBM) for a, _, _ in sources])
+    )(*[in_hbm(t) for t in tables], *[in_hbm(a) for a, _, _ in sources])
     return packed.reshape(heads * groups, total, HEAD_WIDTH)
 
 
@@ -197,7 +237,7 @@
     start_ref = refs.pop(0) if has_start else None
     out_refs = [refs.pop(0) for _ in range(1 if joined else targets)]
     acc, retain, waiting, near = refs[:4]
-    earlier, sem = refs[4:] if has_start else (None, None)
+    done, sems = refs[4:] if joined else (None, None)
     scale = HEAD_WIDTH ** (-0.5)
     steps = targets * (out_rows // BLOCK_TOKENS)
     slot_of_lane = lax.broadcasted_iota(jnp.int32, (SLOTS, WIDE), 1) // BLOCK_TOKENS
@@ -207,9 +247,6 @@
         drop_ref[...].astype(jnp.float32), expand, preferred_element_type=jnp.float32
     ) * (1.0 / keep_prob)
     acc[...] = jnp.zeros_like(acc)
-    if has_start:
-        fetch = pltpu.make_async_copy(start_ref, earlier, sem)
-        fetch.start()
     lane = lax.broadcasted_iota(jnp.int32, (1, WIDE), 1)
     nt = (((1,), (1,)), ((), ()))
     tn = (((0,), (0,)), ((), ()))
@@ -302,27 +339,34 @@
     lax.fori_loop(1, steps // UNROLL, step, 0)
     for u in range(UNROLL):
         finish(steps - UNROLL + u, u)
-    if has_start:
-        fetch.wait()
-        acc[...] += earlier[...]
     if joined:
         rows = acc.shape[0] // targets
+        stores = []
         for target in range(targets):
             part = pl.ds(target * rows, rows)
-            out_refs[0][target, pl.ds(0, 2 * out_rows), :] = near[target]
-            out_refs[0][target, pl.ds(2 * out_rows, rows), :] = (
-                acc[part, :HEAD_WIDTH] * scale
-            ).astype(jnp.bfloat16)
-            out_refs[0][target, pl.ds(2 * out_rows + rows, rows), :] = acc[
-                part, HEAD_WIDTH:
-            ].astype(jnp.bfloat16)
+            sums = acc[part, :]
+            if has_start:
+                sums += start_ref[part, :]
+            done[target, pl.ds(0, 2 * out_rows), :] = near[target]
+            done[target, pl.ds(2 * out_rows, rows), :] = (sums[:, :HEAD_WIDTH] * scale).astype(
+                jnp.bfloat16
+            )
+            done[target, pl.ds(2 * out_rows + rows, rows), :] = sums[:, HEAD_WIDTH:].astype(
+                jnp.bfloat16
+            )
+            stores.append(
+                pltpu.make_async_copy(done.at[target], out_refs[0].at[target], sems.at[target])
+            )
+            stores[-1].start()
+        for store in stores:
+            store.wait()
     else:
         for k, out_ref in enumerate(out_refs):
             out_ref[...] = near[member_ref[0] ^ k]
 
 
 def attend(
-    ids, starts, first_block, member, drop, kv, qd, qd_begin, start, piece, per, joined, device_blocks, total_blocks, tokens, targets
+    ids, starts, first_block, member, drop, kv, qd, qd_begin, start, piece, per, joined, device_blocks, total_blocks, tokens, targets, keep_sums
 ):
     team_blocks = drop.shape[0]
     source = kv if qd is None else qd
@@ -333,10 +377,10 @@
     out_rows = steps * BLOCK_TOKENS // targets
     if joined:
         out_shape = [
-            pltpu.VMEM((targets, 2 * out_rows + 2 * length // targets, HEAD_WIDTH), jnp.bfloat16)
+            pltpu.HBM((targets, 2 * out_rows + 2 * length // targets, HEAD_WIDTH), jnp.bfloat16)
         ]
     else:
-        out_shape = [jax.ShapeDtypeStruct((2 * out_rows, HEAD_WIDTH), jnp.bfloat16)] * targets
+        out_shape = [pltpu.HBM((2 * out_rows, HEAD_WIDTH), jnp.bfloat16)] * targets
     scratch = [
         pltpu.VMEM((team_blocks, WIDE), jnp.float32),
         pltpu.VMEM((UNROLL, 2 * BLOCK_TOKENS, WIDE), jnp.bfloat16),
@@ -345,14 +389,16 @@
     if joined:
         scratch = [pltpu.VMEM(accumulator, jnp.float32)] + scratch
     else:
-        out_shape.append(jax.ShapeDtypeStruct(accumulator, jnp.float32))
-    if start is not None:
-        scratch += [pltpu.VMEM(accumulator, jnp.float32), pltpu.SemaphoreType.DMA]
+        out_shape.append((pltpu.VMEM if keep_sums else pltpu.HBM)(accumulator, jnp.float32))
+    if joined:
+        scratch += [
+            pltpu.VMEM(out_shape[0].shape, jnp.bfloat16),
+            pltpu.SemaphoreType.DMA((targets,)),
+        ]
     sums_bytes = 8 * length * HEAD_WIDTH
-    limit = VMEM_LIMIT + 2 * (kv.size + source.size) + (2 if start is not None else 1) * sums_bytes
+    limit = VMEM_LIMIT + 2 * (kv.size + source.size) + sums_bytes
     flat = [in_vmem(t.reshape(-1, HEAD_WIDTH)) for t in (kv, qd) if t is not None]
-    operands = flat + ([] if start is None else [start])
-    operand_specs = [vmem] * len(flat) + [pl.BlockSpec(memory_space=pl.ANY)] * (start is not None)
+    operands = flat + ([] if start is None else [in_vmem(start)])
     return pl.pallas_call(
         functools.partial(
             attention_kernel,
@@ -371,8 +417,8 @@
             targets,
         ),
         out_shape=out_shape,
-        in_specs=[smem, smem, smem, smem, vmem] + operand_specs,
-        out_specs=[vmem] * len(out_shape),
+        in_specs=[smem, smem, smem, smem, vmem] + [vmem] * len(operands),
+        out_specs=[pl.BlockSpec(memory_space=pl.ANY)] if joined else [vmem] * len(out_shape),
         scratch_shapes=scratch,
         compiler_params=pltpu.CompilerParams(vmem_limit_bytes=limit),
         cost_estimate=pl.CostEstimate(
@@ -380,7 +426,7 @@
             bytes_accessed=2 * (source.size + kv.size) + 8 * length * HEAD_WIDTH,
             transcendentals=pairs,
         ),
-    )(ids, starts, first_block, member, drop, *operands)
+    )(ids, starts, first_block, member, in_hbm(drop), *operands)
 
 
 def per_device(queries, keys, values, grad_out, rand_blocks, global_ids, drop_mask):
@@ -483,12 +529,14 @@
                 total_blocks,
                 tokens,
                 heads,
+                c + 1 < pieces,
             )
         )
         sums = pieces_out[c][heads:]
         if c + 1 < pieces:
-            qd[c + 1], *results = lax.optimization_barrier((qd[c + 1], *pieces_out[c][1:heads]))
-            held.append(results)
+            early = 3 * heads // 4
+            qd[c + 1], *results = lax.optimization_barrier((qd[c + 1], *pieces_out[c][1:early]))
+            held.append([*results, *pieces_out[c][early:heads]])
     runs = shard_blocks // device_blocks
     begin = shard_tokens // pieces
     near = []
@@ -502,7 +550,9 @@
     if whole:
         rest = pieces_out[-1][0]
         if near:
-            rest, near[-1][heads // 2] = lax.optimization_barrier((rest, near[-1][heads // 2]))
+            rest, *near[-1][heads // 2 :] = lax.optimization_barrier(
+                (rest, *near[-1][heads // 2 :])
+            )
         rest = lax.all_to_all(rest, "seq", split_axis=0, concat_axis=0, tiled=True)
     for c in range(len(near)):
         parts = [(0, rows, runs, pieces, c, att), (begin, rows, runs, pieces, c, dq)]

time: 236 us -> 219 us (0.928)
  waiting for transfers between devices: 159 us -> 147 us
  local copies, waits for them, and re-layouts: 13.5 us -> 8.24 us
    ppermute x7, waiting for transfers between devices: 80.2 us -> 53.5 us  [to_shards(): received[k] = lax.ppermute(results[k], 'seq', pairs)]
    all_to_all x1, waiting for transfers between devices: 0.01 us -> 10.3 us  [per_device(): rest = lax.all_to_all(rest, 'seq', split_axis=0, concat_axis=0, tiled=True)]
    unnamed x30 -> x16, local copies, waits for them, and re-layouts: 13.2 us -> 7.26 us
    all_to_all x2, waiting for transfers between devices: 78.6 us -> 83.2 us  [to_heads(): lax.all_to_all(packed, ('seq', 'head'), split_axis=0, concat_axis=0, tile...]
  transfers between devices with their start and end apart: 10 -> 10, of which waited for: 5 -> 5; matrix products, arithmetic and copies ran while one was open for 0% -> 0% of each run, Pallas kernels for 12% -> 13%
where the time goes in v4:
time: 219 us; the launch traced here: 218 us
  waiting for transfers between devices  147 us (67%)
  Pallas kernels  35 us (16%)
  starting transfers between devices  27.4 us (13%)
  local copies, waits for them, and re-layouts  8.24 us (4%)
    all_to_all x2, waiting for transfers between devices, to_heads(): lax.all_to_all(packed, ('seq', 'head'), split_axis=0, concat_axis=0, tile...  83.2 us
    ppermute x7, waiting for transfers between devices, to_shards(): received[k] = lax.ppermute(results[k], 'seq', pairs)  53.5 us
    pallas_call x2, Pallas kernels, attend(): pl.pallas_call(functools.partial(attention_kernel, total_blocks - 1, devi...  25.1 us
    all_to_all x2, starting transfers between devices, to_heads(): lax.all_to_all(packed, ('seq', 'head'), split_axis=0, concat_axis=0, tile...  11.4 us
    ppermute x7, starting transfers between devices, to_shards(): received[k] = lax.ppermute(results[k], 'seq', pairs)  11.2 us
    all_to_all x1, waiting for transfers between devices, per_device(): rest = lax.all_to_all(rest, 'seq', split_axis=0, concat_axis=0, tiled=True)  10.3 us
    unnamed x16, local copies, waits for them, and re-layouts  7.26 us
    pallas_call x2, Pallas kernels, pack(): pl.pallas_call(functools.partial(pack_kernel, heads, groups, tuple(((at,...  6.37 us
  transfers between devices with their start and end apart: 10, of which 5 were waited for; matrix products, arithmetic and copies ran while one was open for 0% of the time, Pallas kernels for 13%

profile of v4, /device:TPU:0, one launch (start us, length us, event | category | flops | bytes accessed | tf_op | source)
XLA Modules:
  0.0 218.5 jit_solution(14684313684756766573)
XLA Ops:
  0.6 4.0 %shard_map.102 = bf16[8,4,400,128]{3,2,1,0:T(8,128)(2,1)} custom-call(s32[8,8,8]{2,1,0:T(8,128)} %refs_0_.2, s32[3,8,8]{2,1,0:T(8,128)} %bitcast.28, bf16[128,4096]{1,0:T(8,128)(2,1)} %refs_2_.1, bf16[128,4096]{1,0:T(8,128)(2,1)} %refs_3_.1, bf16[128,4096]{1,0:T(8,128)(2,1)} %refs_0_.3, bf16[128,4096]{1,0:T(8,128)(2,1)} %refs_1_.1), custom_call_target="tpu_custom_call" | custom-call | bytes 6553600 | tf_op jit(solution)/shard_map/pallas_call | solution.py:112
  4.7 7.3 %all-to-all-start = ((bf16[32,400,128]{2,1,0:T(8,128)(2,1)}), bf16[32,400,128]{2,1,0:T(8,128)(2,1)S(1)}, u32[]{:S(2)}, u32[]{:S(2)}) async-start(bf16[32,400,128]{2,1,0:T(8,128)(2,1)} %bitcast.24), calls=%async_computation | async-start | bytes 6553600 | tf_op jit(solution)/shard_map/all_to_all | solution.py:460
  12.0 0.0 copy-start.7
  12.0 2.3 %shard_map.103 = bf16[8,4,128,128]{3,2,1,0:T(8,128)(2,1)} custom-call(bf16[128,4096]{1,0:T(8,128)(2,1)} %refs_0_.3, bf16[128,4096]{1,0:T(8,128)(2,1)} %refs_1_.1), custom_call_target="tpu_custom_call" | custom-call | bytes 2097152 | tf_op jit(solution)/shard_map/pallas_call | solution.py:112
  14.4 71.9 %all-to-all-done = bf16[32,400,128]{2,1,0:T(8,128)(2,1)S(1)} async-done(((bf16[32,400,128]{2,1,0:T(8,128)(2,1)}), bf16[32,400,128]{2,1,0:T(8,128)(2,1)S(1)}, u32[]{:S(2)}, u32[]{:S(2)}) %all-to-all-start) | async-done | bytes 3276832 | tf_op jit(solution)/shard_map/all_to_all | solution.py:460
  86.2 4.1 %all-to-all-start.1 = ((bf16[32,128,128]{2,1,0:T(8,128)(2,1)}), bf16[32,128,128]{2,1,0:T(8,128)(2,1)}, u32[]{:S(2)}, u32[]{:S(2)}) async-start(bf16[32,128,128]{2,1,0:T(8,128)(2,1)} %bitcast.25), calls=%async_computation.1 | async-start | bytes 2097152 | tf_op jit(solution)/shard_map/all_to_all | solution.py:460
  90.4 0.1 reshape.76
  90.5 0.0 copy-done.7
  90.5 0.1 broadcast_in_dim.2
  90.6 0.1 copy.17
  90.7 0.1 min.12.ids_ref
  90.8 0.6 slice_bitcast_fusion.drop_ref
  91.4 11.9 %shard_map.104 = (bf16[512,128]{1,0:T(8,128)(2,1)}, bf16[512,128]{1,0:T(8,128)(2,1)}, bf16[512,128]{1,0:T(8,128)(2,1)}, bf16[512,128]{1,0:T(8,128)(2,1)}, bf16[5...) custom-call(s32[512]{0:T(512)S(1)} %min.12.ids_ref, ...), custom_call_target="tpu_custom_call" | custom-call | flops 17179869184 | bytes 10747904 | tf_op jit(solution)/shard_map/pallas_call | solution.py:402
  103.2 0.0 copy-start.5
  103.3 1.9 copy-done.5
  105.2 11.3 %all-to-all-done.1 = bf16[32,128,128]{2,1,0:T(8,128)(2,1)} async-done(((bf16[32,128,128]{2,1,0:T(8,128)(2,1)}), bf16[32,128,128]{2,1,0:T(8,128)(2,1)}, u32[]{:S(2)}, u32[]{:S(2)}) %all-to-all-start.1) | async-done | bytes 1048608 | tf_op jit(solution)/shard_map/all_to_all | solution.py:460
  116.5 0.8 collective-permute-start
  117.3 3.1 %collective-permute-start.1 = (bf16[512,128]{1,0:T(8,128)(2,1)}, bf16[512,128]{1,0:T(8,128)(2,1)S(1)}, u32[]{:S(2)}, u32[]{:S(2)}) collective-permute-start(bf16[512,128]{1,0:T(8,128)(2,1)} %get-tuple-element.38), channel_id=1, source_target_pairs={{0,20},{4,16},{8,28},{12,24},{16,4},{20,0},{24,12},{28,8},{1,21},{... | collective-permute-start | bytes 393224 | tf_op jit(solution)/shard_map/ppermute | solution.py:473
  120.4 1.5 collective-permute-start.2
  121.9 2.3 %collective-permute-start.3 = (bf16[512,128]{1,0:T(8,128)(2,1)}, bf16[512,128]{1,0:T(8,128)(2,1)S(1)}, u32[]{:S(2)}, u32[]{:S(2)}) collective-permute-start(bf16[512,128]{1,0:T(8,128)(2,1)} %get-tuple-element.40), channel_id=1, source_target_pairs={{0,28},{4,24},{8,20},{12,16},{16,12},{20,8},{24,4},{28,0},{1,29},{... | collective-permute-start | bytes 393224 | tf_op jit(solution)/shard_map/ppermute | solution.py:473
  124.2 0.0 copy-start.6
  124.2 2.2 %copy-done.6 = f32[4096,256]{1,0:T(8,128)S(1)} copy-done((f32[4096,256]{1,0:T(8,128)S(1)}, f32[4096,256]{1,0:T(8,128)}, u32[]{:S(2)}) %copy-start.6) | copy-done | bytes 4194328
  126.4 13.2 %shard_map.105 = bf16[8,1536,128]{2,1,0:T(8,128)(2,1)} custom-call(s32[512]{0:T(512)S(1)} %min.12.ids_ref, s32[512]{0:T(512)S(1)} %fusion.1.starts_ref, s32[1]{0:T(128)} %bitcast.5.first_ref, s32[1]{0:T(128)} %bitcast.6.member_ref, s32[64,8]{1,0:T(8,128)} %slice_bitcast_fusion.drop_ref, bf16[12800,128]{1,0:T(8,128)(2,1)S(1)} %bitcast.23, ...), custom_call_target="tpu_custom_call" | custom-call | flops 17179869184 | bytes 8519680 | tf_op jit(solution)/shard_map/pallas_call | solution.py:402
  139.6 0.0 copy-start
  139.6 0.0 collective-permute-done.refs_4_
  139.6 0.0 collective-permute-done.1.refs_3_
  139.6 0.0 collective-permute-done.2.refs_2_
  139.7 0.0 copy-start.1
  139.7 0.6 copy-done.1
  140.3 0.0 collective-permute-done.3.refs_1_
  140.3 0.0 copy-start.3
  140.3 0.7 copy-done.3
  141.0 4.9 %all-to-all-start.2 = ((bf16[8,1536,128]{2,1,0:T(8,128)(2,1)}), bf16[8,1536,128]{2,1,0:T(8,128)(2,1)S(1)}, u32[]{:S(2)}, u32[]{:S(2)}) async-start(bf16[8,1536,128]{2,1,0:T(8,128)(2,1)} %shard_map.105), calls=%async_computation.2 | async-start | bytes 6291456 | tf_op jit(solution)/shard_map/all_to_all | solution.py:556
  145.9 2.9 %collective-permute-start.4 = (bf16[512,128]{1,0:T(8,128)(2,1)}, bf16[512,128]{1,0:T(8,128)(2,1)S(1)}, u32[]{:S(2)}, u32[]{:S(2)}) collective-permute-start(bf16[512,128]{1,0:T(8,128)(2,1)} %get-tuple-element.47), channel_id=1, source_target_pairs={{0,12},{4,8},{8,4},{12,0},{16,28},{20,24},{24,20},{28,16},{1,13},{... | collective-permute-start | bytes 393224 | tf_op jit(solution)/shard_map/ppermute | solution.py:473
  148.8 0.6 collective-permute-start.5
  149.3 0.0 collective-permute-start.6
  149.4 52.0 %collective-permute-done.4.refs_5_ = bf16[512,128]{1,0:T(8,128)(2,1)S(1)} collective-permute-done((bf16[512,128]{1,0:T(8,128)(2,1)}, bf16[512,128]{1,0:T(8,128)(2,1)S(1)}, u32[]{:S(2)}, u32[]{:S(2)}) %collective-permute-start.4) | collective-permute-done | bytes 131104 | tf_op jit(solution)/shard_map/ppermute | solution.py:473
  201.4 1.4 collective-permute-done.5.refs_6_
  202.8 0.0 collective-permute-done.6.refs_7_
  202.8 0.0 copy-done
  202.8 0.0 copy-start.2
  202.8 0.9 copy-done.2
  203.7 0.0 copy-start.4
  203.7 0.9 copy-done.4
  204.6 1.3 shard_map.106
  205.9 10.3 %all-to-all-done.2.piece_ref = bf16[8,1536,128]{2,1,0:T(8,128)(2,1)S(1)} async-done(((bf16[8,1536,128]{2,1,0:T(8,128)(2,1)}), bf16[8,1536,128]{2,1,0:T(8,128)(2,1)S(1)}, u32[]{:S(2)}, u32[]{:S(2)}) %all-to-all-start.2) | async-done | bytes 3145760 | tf_op jit(solution)/shard_map/all_to_all | solution.py:556
  216.2 2.3 %shard_map.107 = (bf16[4,2,64,1024]{3,2,1,0:T(8,128)(2,1)}, bf16[4,2,64,1024]{3,2,1,0:T(8,128)(2,1)}, bf16[1,1,512,1024]{3,2,1,0:T(8,128)(2,1)}, bf16[1,1,512,1024]{3,2,1,0:T(8,128)(2,1)}) custom-call(bf16[8,1536,128]{2,1,0:T(8,128)(2,1)S(1)} %all-to-all-done.2.piece_ref, ...), custom_call_target="tpu_custom_call", output_to_operand_aliasing={{0}: (1, {}), {1}: (2, {})} | custom-call | bytes 6291456 | tf_op jit(solution)/shard_map/pallas_call | solution.py:200
  (9 shorter events, 0.1 us)
Async XLA Ops:
  4.7 81.6 %all-to-all-start = ((bf16[32,400,128]{2,1,0:T(8,128)(2,1)}), bf16[32,400,128]{2,1,0:T(8,128)(2,1)S(1)}, u32[]{:S(2)}, u32[]{:S(2)}) async-start(bf16[32,400,128]{2,1,0:T(8,128)(2,1)} %bitcast.24), calls=%async_computation | async-start | bytes 6553600 | tf_op jit(solution)/shard_map/all_to_all | solution.py:460
  12.0 78.5 %copy-start.7 = (s32[2]{0:T(128)S(1)}, s32[2]{0:T(128)}, u32[]{:S(2)}) copy-start(s32[2]{0:T(128)} %param.12) | copy-start | bytes 28
  86.2 30.3 %all-to-all-start.1 = ((bf16[32,128,128]{2,1,0:T(8,128)(2,1)}), bf16[32,128,128]{2,1,0:T(8,128)(2,1)}, u32[]{:S(2)}, u32[]{:S(2)}) async-start(bf16[32,128,128]{2,1,0:T(8,128)(2,1)} %bitcast.25), calls=%async_computation.1 | async-start | bytes 2097152 | tf_op jit(solution)/shard_map/all_to_all | solution.py:460
  103.2 1.9 copy-start.5
  116.5 23.1 %collective-permute-start = (bf16[512,128]{1,0:T(8,128)(2,1)}, bf16[512,128]{1,0:T(8,128)(2,1)S(1)}, u32[]{:S(2)}, u32[]{:S(2)}) collective-permute-start(bf16[512,128]{1,0:T(8,128)(2,1)} %get-tuple-element.37), channel_id=1, source_target_pairs={{0,16},{4,20},{8,24},{12,28},{16,0},{20,4},{24,8},{28,12},{1,17},{... | collective-permute-start | bytes 393224 | tf_op jit(solution)/shard_map/ppermute | solution.py:473
  117.3 22.4 %collective-permute-start.1 = (bf16[512,128]{1,0:T(8,128)(2,1)}, bf16[512,128]{1,0:T(8,128)(2,1)S(1)}, u32[]{:S(2)}, u32[]{:S(2)}) collective-permute-start(bf16[512,128]{1,0:T(8,128)(2,1)} %get-tuple-element.38), channel_id=1, source_target_pairs={{0,20},{4,16},{8,28},{12,24},{16,4},{20,0},{24,12},{28,8},{1,21},{... | collective-permute-start | bytes 393224 | tf_op jit(solution)/shard_map/ppermute | solution.py:473
  120.4 19.3 %collective-permute-start.2 = (bf16[512,128]{1,0:T(8,128)(2,1)}, bf16[512,128]{1,0:T(8,128)(2,1)S(1)}, u32[]{:S(2)}, u32[]{:S(2)}) collective-permute-start(bf16[512,128]{1,0:T(8,128)(2,1)} %get-tuple-element.39), channel_id=1, source_target_pairs={{0,24},{4,28},{8,16},{12,20},{16,8},{20,12},{24,0},{28,4},{1,25},{... | collective-permute-start | bytes 393224 | tf_op jit(solution)/shard_map/ppermute | solution.py:473
  121.9 18.5 %collective-permute-start.3 = (bf16[512,128]{1,0:T(8,128)(2,1)}, bf16[512,128]{1,0:T(8,128)(2,1)S(1)}, u32[]{:S(2)}, u32[]{:S(2)}) collective-permute-start(bf16[512,128]{1,0:T(8,128)(2,1)} %get-tuple-element.40), channel_id=1, source_target_pairs={{0,28},{4,24},{8,20},{12,16},{16,12},{20,8},{24,4},{28,0},{1,29},{... | collective-permute-start | bytes 393224 | tf_op jit(solution)/shard_map/ppermute | solution.py:473
  124.2 2.2 %copy-start.6 = (f32[4096,256]{1,0:T(8,128)S(1)}, f32[4096,256]{1,0:T(8,128)}, u32[]{:S(2)}) copy-start(f32[4096,256]{1,0:T(8,128)} %copy-done.5) | copy-start | bytes 12582916
  139.6 63.2 %copy-start = (bf16[512,128]{1,0:T(8,128)(2,1)S(1)}, bf16[512,128]{1,0:T(8,128)(2,1)}, u32[]{:S(2)}) copy-start(bf16[512,128]{1,0:T(8,128)(2,1)} %get-tuple-element.42.refs_0_) | copy-start | bytes 393220
  139.7 0.7 copy-start.1
  140.3 0.7 copy-start.3
  141.0 75.2 %all-to-all-start.2 = ((bf16[8,1536,128]{2,1,0:T(8,128)(2,1)}), bf16[8,1536,128]{2,1,0:T(8,128)(2,1)S(1)}, u32[]{:S(2)}, u32[]{:S(2)}) async-start(bf16[8,1536,128]{2,1,0:T(8,128)(2,1)} %shard_map.105), calls=%async_computation.2 | async-start | bytes 6291456 | tf_op jit(solution)/shard_map/all_to_all | solution.py:556
  145.9 55.6 %collective-permute-start.4 = (bf16[512,128]{1,0:T(8,128)(2,1)}, bf16[512,128]{1,0:T(8,128)(2,1)S(1)}, u32[]{:S(2)}, u32[]{:S(2)}) collective-permute-start(bf16[512,128]{1,0:T(8,128)(2,1)} %get-tuple-element.47), channel_id=1, source_target_pairs={{0,12},{4,8},{8,4},{12,0},{16,28},{20,24},{24,20},{28,16},{1,13},{... | collective-permute-start | bytes 393224 | tf_op jit(solution)/shard_map/ppermute | solution.py:473
  148.8 54.0 %collective-permute-start.5 = (bf16[512,128]{1,0:T(8,128)(2,1)}, bf16[512,128]{1,0:T(8,128)(2,1)S(1)}, u32[]{:S(2)}, u32[]{:S(2)}) collective-permute-start(bf16[512,128]{1,0:T(8,128)(2,1)} %get-tuple-element.48), channel_id=1, source_target_pairs={{0,8},{4,12},{8,0},{12,4},{16,24},{20,28},{24,16},{28,20},{1,9},{5... | collective-permute-start | bytes 393224 | tf_op jit(solution)/shard_map/ppermute | solution.py:473
  149.3 53.5 %collective-permute-start.6 = (bf16[512,128]{1,0:T(8,128)(2,1)}, bf16[512,128]{1,0:T(8,128)(2,1)S(1)}, u32[]{:S(2)}, u32[]{:S(2)}) collective-permute-start(bf16[512,128]{1,0:T(8,128)(2,1)} %get-tuple-element.49), channel_id=1, source_target_pairs={{0,4},{4,0},{8,12},{12,8},{16,20},{20,16},{24,28},{28,24},{1,5},{5... | collective-permute-start | bytes 393224 | tf_op jit(solution)/shard_map/ppermute | solution.py:473
  202.8 0.9 copy-start.2
  203.7 0.9 copy-start.4

commit v5 on v4

--- a/solution.py
+++ b/solution.py
@@ -17,11 +17,13 @@
 UNROLL = 2
 STRIP = 16
 VMEM_LIMIT = 16 * 1024 * 1024
+VMEM_BYTES = 64 * 1024 * 1024
 
 keep_prob = 0.9
 
 vmem = pl.BlockSpec(memory_space=pltpu.VMEM)
 smem = pl.BlockSpec(memory_space=pltpu.SMEM)
+anywhere = pl.BlockSpec(memory_space=pl.ANY)
 
 
 def in_vmem(array):
@@ -108,7 +110,6 @@
     ]
     if table_rows:
         scratch.append(pltpu.VMEM((table_rows, HEAD_WIDTH), jnp.float32))
-    anywhere = pl.BlockSpec(memory_space=pl.ANY)
     packed = pl.pallas_call(
         functools.partial(
             pack_kernel, heads, groups, tuple((at, rows) for _, at, rows in sources), table_rows
@@ -237,7 +238,8 @@
     start_ref = refs.pop(0) if has_start else None
     out_refs = [refs.pop(0) for _ in range(1 if joined else targets)]
     acc, retain, waiting, near = refs[:4]
-    done, sems = refs[4:] if joined else (None, None)
+    done, sems = refs[4:6] if joined else (None, None)
+    earlier, start_sem = refs[-2:] if has_start else (None, None)
     scale = HEAD_WIDTH ** (-0.5)
     steps = targets * (out_rows // BLOCK_TOKENS)
     slot_of_lane = lax.broadcasted_iota(jnp.int32, (SLOTS, WIDE), 1) // BLOCK_TOKENS
@@ -247,6 +249,9 @@
         drop_ref[...].astype(jnp.float32), expand, preferred_element_type=jnp.float32
     ) * (1.0 / keep_prob)
     acc[...] = jnp.zeros_like(acc)
+    if has_start:
+        fetch = pltpu.make_async_copy(start_ref, earlier, start_sem)
+        fetch.start()
     lane = lax.broadcasted_iota(jnp.int32, (1, WIDE), 1)
     nt = (((1,), (1,)), ((), ()))
     tn = (((0,), (0,)), ((), ()))
@@ -339,6 +344,8 @@
     lax.fori_loop(1, steps // UNROLL, step, 0)
     for u in range(UNROLL):
         finish(steps - UNROLL + u, u)
+    if has_start:
+        fetch.wait()
     if joined:
         rows = acc.shape[0] // targets
         stores = []
@@ -346,7 +353,7 @@
             part = pl.ds(target * rows, rows)
             sums = acc[part, :]
             if has_start:
-                sums += start_ref[part, :]
+                sums += earlier[part, :]
             done[target, pl.ds(0, 2 * out_rows), :] = near[target]
             done[target, pl.ds(2 * out_rows, rows), :] = (sums[:, :HEAD_WIDTH] * scale).astype(
                 jnp.bfloat16
@@ -366,7 +373,7 @@
 
 
 def attend(
-    ids, starts, first_block, member, drop, kv, qd, qd_begin, start, piece, per, joined, device_blocks, total_blocks, tokens, targets, keep_sums
+    ids, starts, first_block, member, drop, kv, qd, qd_begin, start, piece, per, joined, device_blocks, total_blocks, tokens, targets
 ):
     team_blocks = drop.shape[0]
     source = kv if qd is None else qd
@@ -389,16 +396,20 @@
     if joined:
         scratch = [pltpu.VMEM(accumulator, jnp.float32)] + scratch
     else:
-        out_shape.append((pltpu.VMEM if keep_sums else pltpu.HBM)(accumulator, jnp.float32))
+        out_shape.append(pltpu.HBM(accumulator, jnp.float32))
     if joined:
         scratch += [
             pltpu.VMEM(out_shape[0].shape, jnp.bfloat16),
             pltpu.SemaphoreType.DMA((targets,)),
         ]
     sums_bytes = 8 * length * HEAD_WIDTH
-    limit = VMEM_LIMIT + 2 * (kv.size + source.size) + sums_bytes
-    flat = [in_vmem(t.reshape(-1, HEAD_WIDTH)) for t in (kv, qd) if t is not None]
-    operands = flat + ([] if start is None else [in_vmem(start)])
+    limit = VMEM_LIMIT + 2 * (kv.size + source.size) + (1 if start is None else 2) * sums_bytes
+    keep = in_vmem if 2 * limit < VMEM_BYTES else lambda t: t
+    flat = [keep(t.reshape(-1, HEAD_WIDTH)) for t in (kv, qd) if t is not None]
+    if start is not None:
+        scratch += [pltpu.VMEM(accumulator, jnp.float32), pltpu.SemaphoreType.DMA]
+    operands = flat + ([] if start is None else [in_hbm(start)])
+    operand_specs = [vmem] * len(flat) + [anywhere] * (start is not None)
     return pl.pallas_call(
         functools.partial(
             attention_kernel,
@@ -417,8 +428,8 @@
             targets,
         ),
         out_shape=out_shape,
-        in_specs=[smem, smem, smem, smem, vmem] + [vmem] * len(operands),
-        out_specs=[pl.BlockSpec(memory_space=pl.ANY)] if joined else [vmem] * len(out_shape),
+        in_specs=[smem, smem, smem, smem, vmem] + operand_specs,
+        out_specs=[anywhere] if joined else [vmem] * len(out_shape),
         scratch_shapes=scratch,
         compiler_params=pltpu.CompilerParams(vmem_limit_bytes=limit),
         cost_estimate=pl.CostEstimate(
@@ -529,14 +540,13 @@
                 total_blocks,
                 tokens,
                 heads,
-                c + 1 < pieces,
             )
         )
         sums = pieces_out[c][heads:]
         if c + 1 < pieces:
-            early = 3 * heads // 4
-            qd[c + 1], *results = lax.optimization_barrier((qd[c + 1], *pieces_out[c][1:early]))
-            held.append([*results, *pieces_out[c][early:heads]])
+            late = 3 * heads // 4
+            qd[c + 1], *results = lax.optimization_barrier((qd[c + 1], *pieces_out[c][late:heads]))
+            held.append([*pieces_out[c][1:late], *results])
     runs = shard_blocks // device_blocks
     begin = shard_tokens // pieces
     near = []

time: 219 us -> 221 us (level)
  waiting for transfers between devices: 147 us -> 152 us
  local copies, waits for them, and re-layouts: 8.24 us -> 4.1 us
    ppermute x7, waiting for transfers between devices: 53.5 us -> 58.2 us  [to_shards(): received[k] = lax.ppermute(results[k], 'seq', pairs)]
    unnamed x16 -> x12, local copies, waits for them, and re-layouts: 7.26 us -> 3.12 us
  transfers between devices with their start and end apart: 10 -> 10, of which waited for: 5 -> 7; matrix products, arithmetic and copies ran while one was open for 0% -> 0% of each run, Pallas kernels for 13% -> 14%
where the time goes in v5:
time: 221 us; the launch traced here: 220 us
  waiting for transfers between devices  152 us (69%)
  Pallas kernels  36.4 us (16%)
  starting transfers between devices  26.7 us (12%)
  local copies, waits for them, and re-layouts  4.1 us (2%)
    all_to_all x2, waiting for transfers between devices, to_heads(): lax.all_to_all(packed, ('seq', 'head'), split_axis=0, concat_axis=0, tile...  83.9 us
    ppermute x7, waiting for transfers between devices, to_shards(): received[k] = lax.ppermute(results[k], 'seq', pairs)  58.2 us
    pallas_call x2, Pallas kernels, attend(): pl.pallas_call(functools.partial(attention_kernel, total_blocks - 1, devi...  26.4 us
    all_to_all x2, starting transfers between devices, to_heads(): lax.all_to_all(packed, ('seq', 'head'), split_axis=0, concat_axis=0, tile...  11.4 us
    ppermute x7, starting transfers between devices, to_shards(): received[k] = lax.ppermute(results[k], 'seq', pairs)  11.2 us
    all_to_all x1, waiting for transfers between devices, per_device(): rest = lax.all_to_all(rest, 'seq', split_axis=0, concat_axis=0, tiled=True)  10 us
    pallas_call x2, Pallas kernels, pack(): pl.pallas_call(functools.partial(pack_kernel, heads, groups, tuple(((at,...  6.36 us
  transfers between devices with their start and end apart: 10, of which 7 were waited for; matrix products, arithmetic and copies ran while one was open for 0% of the time, Pallas kernels for 14%

profile of v5, /device:TPU:0, one launch (start us, length us, event | category | flops | bytes accessed | tf_op | source)
XLA Modules:
  0.0 220.1 jit_solution(6688699267855902766)
XLA Ops:
  0.6 4.0 %shard_map.102 = bf16[8,4,400,128]{3,2,1,0:T(8,128)(2,1)} custom-call(s32[8,8,8]{2,1,0:T(8,128)} %refs_0_.2, s32[3,8,8]{2,1,0:T(8,128)} %bitcast.28, bf16[128,4096]{1,0:T(8,128)(2,1)} %refs_2_.1, bf16[128,4096]{1,0:T(8,128)(2,1)} %refs_3_.1, bf16[128,4096]{1,0:T(8,128)(2,1)} %refs_0_.3, bf16[128,4096]{1,0:T(8,128)(2,1)} %refs_1_.1), custom_call_target="tpu_custom_call" | custom-call | bytes 6553600 | tf_op jit(solution)/shard_map/pallas_call | solution.py:113
  4.7 7.3 %all-to-all-start = ((bf16[32,400,128]{2,1,0:T(8,128)(2,1)}), bf16[32,400,128]{2,1,0:T(8,128)(2,1)S(1)}, u32[]{:S(2)}, u32[]{:S(2)}) async-start(bf16[32,400,128]{2,1,0:T(8,128)(2,1)} %bitcast.24), calls=%async_computation | async-start | bytes 6553600 | tf_op jit(solution)/shard_map/all_to_all | solution.py:471
  12.0 0.0 copy-start.5
  12.0 2.3 %shard_map.103 = bf16[8,4,128,128]{3,2,1,0:T(8,128)(2,1)} custom-call(bf16[128,4096]{1,0:T(8,128)(2,1)} %refs_0_.3, bf16[128,4096]{1,0:T(8,128)(2,1)} %refs_1_.1), custom_call_target="tpu_custom_call" | custom-call | bytes 2097152 | tf_op jit(solution)/shard_map/pallas_call | solution.py:113
  14.4 71.9 %all-to-all-done = bf16[32,400,128]{2,1,0:T(8,128)(2,1)S(1)} async-done(((bf16[32,400,128]{2,1,0:T(8,128)(2,1)}), bf16[32,400,128]{2,1,0:T(8,128)(2,1)S(1)}, u32[]{:S(2)}, u32[]{:S(2)}) %all-to-all-start) | async-done | bytes 3276832 | tf_op jit(solution)/shard_map/all_to_all | solution.py:471
  86.2 4.1 %all-to-all-start.1 = ((bf16[32,128,128]{2,1,0:T(8,128)(2,1)}), bf16[32,128,128]{2,1,0:T(8,128)(2,1)}, u32[]{:S(2)}, u32[]{:S(2)}) async-start(bf16[32,128,128]{2,1,0:T(8,128)(2,1)} %bitcast.25), calls=%async_computation.1 | async-start | bytes 2097152 | tf_op jit(solution)/shard_map/all_to_all | solution.py:471
  90.4 0.1 reshape.76
  90.4 0.0 copy-done.5
  90.5 0.1 broadcast_in_dim.2
  90.6 0.1 copy.17
  90.6 0.1 min.12.ids_ref
  90.8 0.6 slice_bitcast_fusion.drop_ref
  91.4 13.1 %shard_map.104 = (bf16[512,128]{1,0:T(8,128)(2,1)}, bf16[512,128]{1,0:T(8,128)(2,1)}, bf16[512,128]{1,0:T(8,128)(2,1)}, bf16[512,128]{1,0:T(8,128)(2,1)}, bf16[5...) custom-call(s32[512]{0:T(512)S(1)} %min.12.ids_ref, ...), custom_call_target="tpu_custom_call" | custom-call | flops 17179869184 | bytes 10747904 | tf_op jit(solution)/shard_map/pallas_call | solution.py:413
  104.5 12.0 %all-to-all-done.1 = bf16[32,128,128]{2,1,0:T(8,128)(2,1)} async-done(((bf16[32,128,128]{2,1,0:T(8,128)(2,1)}), bf16[32,128,128]{2,1,0:T(8,128)(2,1)}, u32[]{:S(2)}, u32[]{:S(2)}) %all-to-all-start.1) | async-done | bytes 1048608 | tf_op jit(solution)/shard_map/all_to_all | solution.py:471
  116.5 1.3 collective-permute-start.2
  117.8 3.4 %collective-permute-start.3 = (bf16[512,128]{1,0:T(8,128)(2,1)}, bf16[512,128]{1,0:T(8,128)(2,1)S(1)}, u32[]{:S(2)}, u32[]{:S(2)}) collective-permute-start(bf16[512,128]{1,0:T(8,128)(2,1)} %get-tuple-element.34), channel_id=1, source_target_pairs={{0,28},{4,24},{8,20},{12,16},{16,12},{20,8},{24,4},{28,0},{1,29},{... | collective-permute-start | bytes 393224 | tf_op jit(solution)/shard_map/ppermute | solution.py:484
  121.3 0.0 collective-permute-start
  121.3 2.9 %collective-permute-start.1 = (bf16[512,128]{1,0:T(8,128)(2,1)}, bf16[512,128]{1,0:T(8,128)(2,1)S(1)}, u32[]{:S(2)}, u32[]{:S(2)}) collective-permute-start(bf16[512,128]{1,0:T(8,128)(2,1)} %get-tuple-element.32), channel_id=1, source_target_pairs={{0,20},{4,16},{8,28},{12,24},{16,4},{20,0},{24,12},{28,8},{1,21},{... | collective-permute-start | bytes 393224 | tf_op jit(solution)/shard_map/ppermute | solution.py:484
  124.2 13.3 %shard_map.105 = bf16[8,1536,128]{2,1,0:T(8,128)(2,1)} custom-call(s32[512]{0:T(512)S(1)} %min.12.ids_ref, s32[512]{0:T(512)S(1)} %fusion.1.starts_ref, s32[1]{0:T(128)} %bitcast.5.first_ref, s32[1]{0:T(128)} %bitcast.6.member_ref, s32[64,8]{1,0:T(8,128)} %slice_bitcast_fusion.drop_ref, bf16[12800,128]{1,0:T(8,128)(2,1)S(1)} %bitcast.23, ...), custom_call_target="tpu_custom_call" | custom-call | flops 17179869184 | bytes 8519680 | tf_op jit(solution)/shard_map/pallas_call | solution.py:413
  137.5 0.0 copy-start
  137.5 0.0 collective-permute-done.2.refs_2_
  137.5 0.0 collective-permute-done.3.refs_1_
  137.5 2.6 %collective-permute-done.refs_4_ = bf16[512,128]{1,0:T(8,128)(2,1)S(1)} collective-permute-done((bf16[512,128]{1,0:T(8,128)(2,1)}, bf16[512,128]{1,0:T(8,128)(2,1)S(1)}, u32[]{:S(2)}, u32[]{:S(2)}) %collective-permute-start) | collective-permute-done | bytes 131104 | tf_op jit(solution)/shard_map/ppermute | solution.py:484
  140.1 0.0 copy-start.1
  140.1 0.6 copy-done.1
  140.7 1.5 collective-permute-done.1.refs_3_
  142.2 0.0 copy-start.3
  142.2 0.7 copy-done.3
  142.9 4.2 %all-to-all-start.2 = ((bf16[8,1536,128]{2,1,0:T(8,128)(2,1)}), bf16[8,1536,128]{2,1,0:T(8,128)(2,1)S(1)}, u32[]{:S(2)}, u32[]{:S(2)}) async-start(bf16[8,1536,128]{2,1,0:T(8,128)(2,1)} %shard_map.105), calls=%async_computation.2 | async-start | bytes 6291456 | tf_op jit(solution)/shard_map/all_to_all | solution.py:566
  147.0 2.9 %collective-permute-start.4 = (bf16[512,128]{1,0:T(8,128)(2,1)}, bf16[512,128]{1,0:T(8,128)(2,1)S(1)}, u32[]{:S(2)}, u32[]{:S(2)}) collective-permute-start(bf16[512,128]{1,0:T(8,128)(2,1)} %get-tuple-element.41), channel_id=1, source_target_pairs={{0,12},{4,8},{8,4},{12,0},{16,28},{20,24},{24,20},{28,16},{1,13},{... | collective-permute-start | bytes 393224 | tf_op jit(solution)/shard_map/ppermute | solution.py:484
  150.0 0.6 collective-permute-start.5
  150.5 0.0 collective-permute-start.6
  150.6 52.4 %collective-permute-done.4.refs_5_ = bf16[512,128]{1,0:T(8,128)(2,1)S(1)} collective-permute-done((bf16[512,128]{1,0:T(8,128)(2,1)}, bf16[512,128]{1,0:T(8,128)(2,1)S(1)}, u32[]{:S(2)}, u32[]{:S(2)}) %collective-permute-start.4) | collective-permute-done | bytes 131104 | tf_op jit(solution)/shard_map/ppermute | solution.py:484
  203.0 1.7 collective-permute-done.5.refs_6_
  204.7 0.0 collective-permute-done.6.refs_7_
  204.7 0.0 copy-done
  204.7 0.0 copy-start.2
  204.7 0.9 copy-done.2
  205.6 0.0 copy-start.4
  205.6 0.9 copy-done.4
  206.5 1.3 shard_map.106
  207.8 10.0 %all-to-all-done.2.piece_ref = bf16[8,1536,128]{2,1,0:T(8,128)(2,1)S(1)} async-done(((bf16[8,1536,128]{2,1,0:T(8,128)(2,1)}), bf16[8,1536,128]{2,1,0:T(8,128)(2,1)S(1)}, u32[]{:S(2)}, u32[]{:S(2)}) %all-to-all-start.2) | async-done | bytes 3145760 | tf_op jit(solution)/shard_map/all_to_all | solution.py:566
  217.8 2.3 %shard_map.107 = (bf16[4,2,64,1024]{3,2,1,0:T(8,128)(2,1)}, bf16[4,2,64,1024]{3,2,1,0:T(8,128)(2,1)}, bf16[1,1,512,1024]{3,2,1,0:T(8,128)(2,1)}, bf16[1,1,512,1024]{3,2,1,0:T(8,128)(2,1)}) custom-call(bf16[8,1536,128]{2,1,0:T(8,128)(2,1)S(1)} %all-to-all-done.2.piece_ref, ...), custom_call_target="tpu_custom_call", output_to_operand_aliasing={{0}: (1, {}), {1}: (2, {})} | custom-call | bytes 6291456 | tf_op jit(solution)/shard_map/pallas_call | solution.py:201
  (9 shorter events, 0.1 us)
Async XLA Ops:
  4.7 81.6 %all-to-all-start = ((bf16[32,400,128]{2,1,0:T(8,128)(2,1)}), bf16[32,400,128]{2,1,0:T(8,128)(2,1)S(1)}, u32[]{:S(2)}, u32[]{:S(2)}) async-start(bf16[32,400,128]{2,1,0:T(8,128)(2,1)} %bitcast.24), calls=%async_computation | async-start | bytes 6553600 | tf_op jit(solution)/shard_map/all_to_all | solution.py:471
  12.0 78.5 %copy-start.5 = (s32[2]{0:T(128)S(1)}, s32[2]{0:T(128)}, u32[]{:S(2)}) copy-start(s32[2]{0:T(128)} %param.12) | copy-start | bytes 28
  86.2 30.3 %all-to-all-start.1 = ((bf16[32,128,128]{2,1,0:T(8,128)(2,1)}), bf16[32,128,128]{2,1,0:T(8,128)(2,1)}, u32[]{:S(2)}, u32[]{:S(2)}) async-start(bf16[32,128,128]{2,1,0:T(8,128)(2,1)} %bitcast.25), calls=%async_computation.1 | async-start | bytes 2097152 | tf_op jit(solution)/shard_map/all_to_all | solution.py:471
  116.5 21.0 %collective-permute-start.2 = (bf16[512,128]{1,0:T(8,128)(2,1)}, bf16[512,128]{1,0:T(8,128)(2,1)S(1)}, u32[]{:S(2)}, u32[]{:S(2)}) collective-permute-start(bf16[512,128]{1,0:T(8,128)(2,1)} %get-tuple-element.33), channel_id=1, source_target_pairs={{0,24},{4,28},{8,16},{12,20},{16,8},{20,12},{24,0},{28,4},{1,25},{... | collective-permute-start | bytes 393224 | tf_op jit(solution)/shard_map/ppermute | solution.py:484
  117.8 19.7 %collective-permute-start.3 = (bf16[512,128]{1,0:T(8,128)(2,1)}, bf16[512,128]{1,0:T(8,128)(2,1)S(1)}, u32[]{:S(2)}, u32[]{:S(2)}) collective-permute-start(bf16[512,128]{1,0:T(8,128)(2,1)} %get-tuple-element.34), channel_id=1, source_target_pairs={{0,28},{4,24},{8,20},{12,16},{16,12},{20,8},{24,4},{28,0},{1,29},{... | collective-permute-start | bytes 393224 | tf_op jit(solution)/shard_map/ppermute | solution.py:484
  121.3 18.8 %collective-permute-start = (bf16[512,128]{1,0:T(8,128)(2,1)}, bf16[512,128]{1,0:T(8,128)(2,1)S(1)}, u32[]{:S(2)}, u32[]{:S(2)}) collective-permute-start(bf16[512,128]{1,0:T(8,128)(2,1)} %get-tuple-element.31), channel_id=1, source_target_pairs={{0,16},{4,20},{8,24},{12,28},{16,0},{20,4},{24,8},{28,12},{1,17},{... | collective-permute-start | bytes 393224 | tf_op jit(solution)/shard_map/ppermute | solution.py:484
  121.3 21.0 %collective-permute-start.1 = (bf16[512,128]{1,0:T(8,128)(2,1)}, bf16[512,128]{1,0:T(8,128)(2,1)S(1)}, u32[]{:S(2)}, u32[]{:S(2)}) collective-permute-start(bf16[512,128]{1,0:T(8,128)(2,1)} %get-tuple-element.32), channel_id=1, source_target_pairs={{0,20},{4,16},{8,28},{12,24},{16,4},{20,0},{24,12},{28,8},{1,21},{... | collective-permute-start | bytes 393224 | tf_op jit(solution)/shard_map/ppermute | solution.py:484
  137.5 67.2 %copy-start = (bf16[512,128]{1,0:T(8,128)(2,1)S(1)}, bf16[512,128]{1,0:T(8,128)(2,1)}, u32[]{:S(2)}) copy-start(bf16[512,128]{1,0:T(8,128)(2,1)} %get-tuple-element.36.refs_0_) | copy-start | bytes 393220
  140.1 0.6 copy-start.1
  142.2 0.7 copy-start.3
  142.9 74.9 %all-to-all-start.2 = ((bf16[8,1536,128]{2,1,0:T(8,128)(2,1)}), bf16[8,1536,128]{2,1,0:T(8,128)(2,1)S(1)}, u32[]{:S(2)}, u32[]{:S(2)}) async-start(bf16[8,1536,128]{2,1,0:T(8,128)(2,1)} %shard_map.105), calls=%async_computation.2 | async-start | bytes 6291456 | tf_op jit(solution)/shard_map/all_to_all | solution.py:566
  147.0 55.9 %collective-permute-start.4 = (bf16[512,128]{1,0:T(8,128)(2,1)}, bf16[512,128]{1,0:T(8,128)(2,1)S(1)}, u32[]{:S(2)}, u32[]{:S(2)}) collective-permute-start(bf16[512,128]{1,0:T(8,128)(2,1)} %get-tuple-element.41), channel_id=1, source_target_pairs={{0,12},{4,8},{8,4},{12,0},{16,28},{20,24},{24,20},{28,16},{1,13},{... | collective-permute-start | bytes 393224 | tf_op jit(solution)/shard_map/ppermute | solution.py:484
  150.0 54.7 %collective-permute-start.5 = (bf16[512,128]{1,0:T(8,128)(2,1)}, bf16[512,128]{1,0:T(8,128)(2,1)S(1)}, u32[]{:S(2)}, u32[]{:S(2)}) collective-permute-start(bf16[512,128]{1,0:T(8,128)(2,1)} %get-tuple-element.42), channel_id=1, source_target_pairs={{0,8},{4,12},{8,0},{12,4},{16,24},{20,28},{24,16},{28,20},{1,9},{5... | collective-permute-start | bytes 393224 | tf_op jit(solution)/shard_map/ppermute | solution.py:484
  150.5 54.2 %collective-permute-start.6 = (bf16[512,128]{1,0:T(8,128)(2,1)}, bf16[512,128]{1,0:T(8,128)(2,1)S(1)}, u32[]{:S(2)}, u32[]{:S(2)}) collective-permute-start(bf16[512,128]{1,0:T(8,128)(2,1)} %get-tuple-element.43), channel_id=1, source_target_pairs={{0,4},{4,0},{8,12},{12,8},{16,20},{20,16},{24,28},{28,24},{1,5},{5... | collective-permute-start | bytes 393224 | tf_op jit(solution)/shard_map/ppermute | solution.py:484
  204.7 0.9 copy-start.2
  205.6 0.9 copy-start.4

commit v6 on v5

--- a/solution.py
+++ b/solution.py
@@ -124,91 +124,64 @@
     return packed.reshape(heads * groups, total, HEAD_WIDTH)
 
 
-def unpack_kernel(parts, member_ref, *refs):
-    outs = refs[len(refs) - len(parts) :]
-    heads = outs[0].shape[-1] // HEAD_WIDTH
-    for n in range(heads):
-        k = (heads - n) % heads
-        column = pl.multiple_of((member_ref[0] ^ k) * HEAD_WIDTH, HEAD_WIDTH)
-        for begin, out in zip(parts, outs):
-            runs, _, rows, _ = out.shape
+def unpack_kernel(half, groups, copies, count, member_ref, *refs):
+    refs = list(refs)
+    inputs = [[refs.pop(0) for _ in range(size)] for _, size, _ in groups]
+    sems = refs.pop()
+    stages = refs[len(refs) - copies :]
+    outs = refs[len(refs) - copies - count : len(refs) - copies]
+    local = lax.rem(member_ref[0], half)
+    own_half = member_ref[0] - local
+    stores = []
+    at = 0
+    for (far, _, parts), arrays in zip(groups, inputs):
+        first = own_half ^ half if far else own_half
+        columns = pl.ds(pl.multiple_of(first * HEAD_WIDTH, HEAD_WIDTH), half * HEAD_WIDTH)
+        for begin, rows, runs, piece, n in parts:
             for i in range(runs):
-                out[i, 0, :, pl.ds(column, HEAD_WIDTH)] = refs[n][pl.ds(begin + i * rows, rows), :]
-
-
-def unpack(member, received, parts):
-    heads = len(received)
-    shapes, specs, olds, aliases, size = [], [], [], {}, 0
-    for n, (_, rows, runs, pieces, piece, old) in enumerate(parts):
-        shapes.append(
-            jax.ShapeDtypeStruct((runs, pieces, rows, heads * HEAD_WIDTH), jnp.bfloat16)
-        )
-        specs.append(
-            pl.BlockSpec(
-                (runs, 1, rows, heads * HEAD_WIDTH),
-                functools.partial(lambda piece, h: (0, piece, 0, 0), piece),
-            )
-        )
-        size += rows * runs * heads * HEAD_WIDTH
-        if old is not None:
-            aliases[1 + heads + len(olds)] = n
-            olds.append(old)
+                stage = stages[at]
+                source = pl.ds(begin + i * rows, rows)
+                for j in range(half):
+                    if far:
+                        column = pl.multiple_of((local ^ j) * HEAD_WIDTH, HEAD_WIDTH)
+                        stage[:, pl.ds(column, HEAD_WIDTH)] = arrays[j][source, :]
+                    else:
+                        stage[:, pl.ds(j * HEAD_WIDTH, HEAD_WIDTH)] = arrays[0][j, source, :]
+                stores.append(
+                    pltpu.make_async_copy(stage, outs[n].at[i, piece, :, columns], sems.at[at])
+                )
+                stores[-1].start()
+                at += 1
+    for store in stores:
+        store.wait()
+
+
+def unpack(member, groups, shapes, olds=()):
+    half = groups[0][1][0].shape[0] if not groups[0][0] else len(groups[0][1])
+    arrays = [t for _, each, _ in groups for t in each]
+    stages = [
+        pltpu.VMEM((rows, half * HEAD_WIDTH), jnp.bfloat16)
+        for _, _, parts in groups
+        for _, rows, runs, _, _ in parts
+        for _ in range(runs)
+    ]
+    size = sum(math.prod(stage.shape) for stage in stages)
     return pl.pallas_call(
-        functools.partial(unpack_kernel, tuple(part[0] for part in parts)),
-        grid=(1,),
-        out_shape=shapes,
-        in_specs=[smem]
-        + [pl.BlockSpec(received[0].shape, lambda h: (0, 0))] * heads
-        + [pl.BlockSpec(memory_space=pl.ANY)] * len(olds),
-        out_specs=specs,
-        input_output_aliases=aliases,
+        functools.partial(
+            unpack_kernel,
+            half,
+            tuple((far, len(each), tuple(parts)) for far, each, parts in groups),
+            len(stages),
+            len(shapes),
+        ),
+        out_shape=[pltpu.HBM(shape, jnp.bfloat16) for shape in shapes],
+        in_specs=[smem] + [vmem] * len(arrays) + [anywhere] * len(olds),
+        out_specs=[anywhere] * len(shapes),
+        input_output_aliases={1 + len(arrays) + n: n for n in range(len(olds))},
+        scratch_shapes=stages + [pltpu.SemaphoreType.DMA((len(stages),))],
         compiler_params=pltpu.CompilerParams(vmem_limit_bytes=VMEM_LIMIT),
         cost_estimate=copy_cost(size),
-    )(member, received[0], *received[:0:-1], *olds)
-
-
-def unpack_all_kernel(begins, step_heads, piece_ref, *refs):
-    outs = refs[len(refs) - len(begins) :]
-    for begin, out in zip(begins, outs):
-        runs, _, rows, _ = out.shape
-        for m in range(step_heads):
-            for i in range(runs):
-                out[i, 0, :, pl.ds(m * HEAD_WIDTH, HEAD_WIDTH)] = piece_ref[
-                    m, pl.ds(begin + i * rows, rows), :
-                ]
-
-
-def unpack_all(received, parts):
-    heads, total, _ = received.shape
-    step_heads = 2 if heads % 2 == 0 else 1
-    width = step_heads * HEAD_WIDTH
-    shapes, out_specs, begins, olds, aliases = [], [], [], [], {}
-    size = 0
-    for n, (begin, rows, runs, pieces, piece, old) in enumerate(parts):
-        begins.append(begin)
-        shapes.append(
-            jax.ShapeDtypeStruct((runs, pieces, rows, heads * HEAD_WIDTH), jnp.bfloat16)
-        )
-        out_specs.append(
-            pl.BlockSpec(
-                (runs, 1, rows, width), functools.partial(lambda piece, h: (0, piece, 0, h), piece)
-            )
-        )
-        size += rows * runs * heads * HEAD_WIDTH
-        if old is not None:
-            aliases[1 + len(olds)] = n
-            olds.append(old)
-    return pl.pallas_call(
-        functools.partial(unpack_all_kernel, begins, step_heads),
-        grid=(heads // step_heads,),
-        out_shape=shapes,
-        in_specs=[pl.BlockSpec((step_heads, total, HEAD_WIDTH), lambda h: (h, 0, 0))]
-        + [pl.BlockSpec(memory_space=pl.ANY)] * len(olds),
-        out_specs=out_specs,
-        input_output_aliases=aliases,
-        compiler_params=pltpu.CompilerParams(vmem_limit_bytes=VMEM_LIMIT),
-        cost_estimate=copy_cost(size),
-    )(in_vmem(received), *olds)
+    )(member, *[in_vmem(t) for t in arrays], *olds)
 
 
 def attention_kernel(
@@ -235,11 +208,13 @@
 ):
     refs = list(refs)
     qd_ref = refs.pop(0) if has_qd else kv_ref
-    start_ref = refs.pop(0) if has_start else None
-    out_refs = [refs.pop(0) for _ in range(1 if joined else targets)]
+    start_ref, near_start = (refs.pop(0), refs.pop(0)) if has_start else (None, None)
+    half = targets // 2
+    far_refs = [refs.pop(0) for _ in range(half)]
+    near_ref = refs.pop(0)
     acc, retain, waiting, near = refs[:4]
-    done, sems = refs[4:6] if joined else (None, None)
-    earlier, start_sem = refs[-2:] if has_start else (None, None)
+    if joined:
+        far_done, near_done, sems, earlier, start_sems = refs[4:]
     scale = HEAD_WIDTH ** (-0.5)
     steps = targets * (out_rows // BLOCK_TOKENS)
     slot_of_lane = lax.broadcasted_iota(jnp.int32, (SLOTS, WIDE), 1) // BLOCK_TOKENS
@@ -250,8 +225,15 @@
     ) * (1.0 / keep_prob)
     acc[...] = jnp.zeros_like(acc)
     if has_start:
-        fetch = pltpu.make_async_copy(start_ref, earlier, start_sem)
-        fetch.start()
+        early_rows = near_start.shape[1]
+        fetches = [pltpu.make_async_copy(start_ref, earlier, start_sems.at[0])] + [
+            pltpu.make_async_copy(
+                near_start.at[j], near_done.at[j, pl.ds(0, early_rows), :], start_sems.at[1 + j]
+            )
+            for j in range(half)
+        ]
+        for fetch in fetches:
+            fetch.start()
     lane = lax.broadcasted_iota(jnp.int32, (1, WIDE), 1)
     nt = (((1,), (1,)), ((), ()))
     tn = (((0,), (0,)), ((), ()))
@@ -344,36 +326,43 @@
     lax.fori_loop(1, steps // UNROLL, step, 0)
     for u in range(UNROLL):
         finish(steps - UNROLL + u, u)
-    if has_start:
-        fetch.wait()
+    local = lax.rem(member_ref[0], half)
+    own_half = member_ref[0] - local
+
+    def put(target, ref, begin, done):
+        ref[pl.ds(begin, 2 * out_rows), :] = near[target]
+        if done:
+            rows = acc.shape[0] // targets
+            part = pl.ds(pl.multiple_of(target * rows, rows), rows)
+            sums = acc[part, :] + earlier[part, :]
+            begin += 2 * out_rows
+            ref[pl.ds(begin, rows), :] = (sums[:, :HEAD_WIDTH] * scale).astype(jnp.bfloat16)
+            ref[pl.ds(begin + rows, rows), :] = sums[:, HEAD_WIDTH:].astype(jnp.bfloat16)
+
     if joined:
-        rows = acc.shape[0] // targets
+        for fetch in fetches:
+            fetch.wait()
         stores = []
-        for target in range(targets):
-            part = pl.ds(target * rows, rows)
-            sums = acc[part, :]
-            if has_start:
-                sums += earlier[part, :]
-            done[target, pl.ds(0, 2 * out_rows), :] = near[target]
-            done[target, pl.ds(2 * out_rows, rows), :] = (sums[:, :HEAD_WIDTH] * scale).astype(
-                jnp.bfloat16
-            )
-            done[target, pl.ds(2 * out_rows + rows, rows), :] = sums[:, HEAD_WIDTH:].astype(
-                jnp.bfloat16
-            )
+        for j in range(half):
+            put(member_ref[0] ^ (half + j), far_done.at[j], 0, True)
+            stores.append(pltpu.make_async_copy(far_done.at[j], far_refs[j], sems.at[j]))
+            stores[-1].start()
+        for j in range(half):
+            put(own_half + j, near_done.at[j], early_rows, True)
             stores.append(
-                pltpu.make_async_copy(done.at[target], out_refs[0].at[target], sems.at[target])
+                pltpu.make_async_copy(near_done.at[j], near_ref.at[j], sems.at[half + j])
             )
             stores[-1].start()
         for store in stores:
             store.wait()
     else:
-        for k, out_ref in enumerate(out_refs):
-            out_ref[...] = near[member_ref[0] ^ k]
+        for j in range(half):
+            put(member_ref[0] ^ (half + j), far_refs[j], 0, False)
+            put(own_half + j, near_ref.at[j], 0, False)
 
 
 def attend(
-    ids, starts, first_block, member, drop, kv, qd, qd_begin, start, piece, per, joined, device_blocks, total_blocks, tokens, targets
+    ids, starts, first_block, member, drop, kv, qd, qd_begin, start, near_start, piece, per, joined, device_blocks, total_blocks, tokens, targets
 ):
     team_blocks = drop.shape[0]
     source = kv if qd is None else qd
@@ -382,12 +371,12 @@
     pairs = steps * BLOCK_TOKENS * WIDE
     accumulator = (length, 2 * HEAD_WIDTH)
     out_rows = steps * BLOCK_TOKENS // targets
-    if joined:
-        out_shape = [
-            pltpu.HBM((targets, 2 * out_rows + 2 * length // targets, HEAD_WIDTH), jnp.bfloat16)
-        ]
-    else:
-        out_shape = [pltpu.HBM((2 * out_rows, HEAD_WIDTH), jnp.bfloat16)] * targets
+    half = targets // 2
+    far_rows = 2 * out_rows + (2 * length // targets if joined else 0)
+    near_rows = far_rows + (near_start.shape[1] if joined else 0)
+    out_shape = [pltpu.HBM((far_rows, HEAD_WIDTH), jnp.bfloat16)] * half + [
+        pltpu.HBM((half, near_rows, HEAD_WIDTH), jnp.bfloat16)
+    ]
     scratch = [
         pltpu.VMEM((team_blocks, WIDE), jnp.float32),
         pltpu.VMEM((UNROLL, 2 * BLOCK_TOKENS, WIDE), jnp.bfloat16),
@@ -399,17 +388,18 @@
         out_shape.append(pltpu.HBM(accumulator, jnp.float32))
     if joined:
         scratch += [
-            pltpu.VMEM(out_shape[0].shape, jnp.bfloat16),
+            pltpu.VMEM((half, far_rows, HEAD_WIDTH), jnp.bfloat16),
+            pltpu.VMEM((half, near_rows, HEAD_WIDTH), jnp.bfloat16),
             pltpu.SemaphoreType.DMA((targets,)),
+            pltpu.VMEM(accumulator, jnp.float32),
+            pltpu.SemaphoreType.DMA((1 + half,)),
         ]
     sums_bytes = 8 * length * HEAD_WIDTH
-    limit = VMEM_LIMIT + 2 * (kv.size + source.size) + (1 if start is None else 2) * sums_bytes
+    limit = VMEM_LIMIT + 2 * (kv.size + source.size) + (2 if joined else 1) * sums_bytes
     keep = in_vmem if 2 * limit < VMEM_BYTES else lambda t: t
     flat = [keep(t.reshape(-1, HEAD_WIDTH)) for t in (kv, qd) if t is not None]
-    if start is not None:
-        scratch += [pltpu.VMEM(accumulator, jnp.float32), pltpu.SemaphoreType.DMA]
-    operands = flat + ([] if start is None else [in_hbm(start)])
-    operand_specs = [vmem] * len(flat) + [anywhere] * (start is not None)
+    operands = flat + ([in_hbm(start), in_hbm(near_start)] if joined else [])
+    operand_specs = [vmem] * len(flat) + [anywhere] * (len(operands) - len(flat))
     return pl.pallas_call(
         functools.partial(
             attention_kernel,
@@ -429,7 +419,7 @@
         ),
         out_shape=out_shape,
         in_specs=[smem, smem, smem, smem, vmem] + operand_specs,
-        out_specs=[anywhere] if joined else [vmem] * len(out_shape),
+        out_specs=[anywhere if joined else vmem] * len(out_shape),
         scratch_shapes=scratch,
         compiler_params=pltpu.CompilerParams(vmem_limit_bytes=limit),
         cost_estimate=pl.CostEstimate(
@@ -454,7 +444,8 @@
     total_blocks = shards * shard_blocks
     first_block = team * team_blocks
     whole = teams == 1
-    pieces = device_blocks if whole else 1
+    pieces = 2 if whole and device_blocks == 2 else 1
+    half = heads // 2
     per = device_blocks // pieces
     rows = tokens // pieces
     same_team_all = (
@@ -477,12 +468,21 @@
             axis_index_groups=same_team_all,
         )
 
-    def to_shards(results):
-        received = list(results)
-        for k in reversed(range(1, heads)):
-            pairs = [(s, s ^ k) for s in range(shards)]
-            received[k] = lax.ppermute(results[k], "seq", pairs)
-        return received
+    def exchange_far(results):
+        return [
+            lax.ppermute(t, "seq", [(s, s ^ (half + j)) for s in range(shards)])
+            for j, t in enumerate(results)
+        ]
+
+    def exchange_near(results):
+        return lax.all_to_all(
+            results,
+            "seq",
+            split_axis=0,
+            concat_axis=0,
+            tiled=True,
+            axis_index_groups=[list(range(s, s + half)) for s in range(0, shards, half)],
+        )
 
     table_rows = -(-(shard_blocks + R) // 16) * 16
     sources = [[(queries, c, rows), (grad_out, c, rows)] for c in range(pieces)]
@@ -518,76 +518,88 @@
     )
     listed = jnp.clip(listed, 0, total_blocks - 1).reshape(-1)
     starts = listed // device_blocks * kv.shape[1] + listed % device_blocks * BLOCK_TOKENS
-    pieces_out = []
-    held = []
-    sums = []
-    for c in range(pieces):
-        pieces_out.append(
-            attend(
-                listed,
-                starts,
-                first_block.reshape(1),
-                member.reshape(1),
-                drops,
-                kv,
-                qd[c],
-                qd_begin if qd[c] is None else 0,
-                sums[0] if sums else None,
-                c,
-                per,
-                whole and c == pieces - 1,
-                device_blocks,
-                total_blocks,
-                tokens,
-                heads,
-            )
-        )
-        sums = pieces_out[c][heads:]
-        if c + 1 < pieces:
-            late = 3 * heads // 4
-            qd[c + 1], *results = lax.optimization_barrier((qd[c + 1], *pieces_out[c][late:heads]))
-            held.append([*pieces_out[c][1:late], *results])
+    member = member.reshape(1)
+
+    def run(c, start=None, near_start=None):
+        out = attend(
+            listed,
+            starts,
+            first_block.reshape(1),
+            member,
+            drops,
+            kv,
+            qd[c],
+            qd_begin if qd[c] is None else 0,
+            start,
+            near_start,
+            c,
+            per,
+            start is not None,
+            device_blocks,
+            total_blocks,
+            tokens,
+            heads,
+        )
+        return list(out[:half]), *out[half:]
+
     runs = shard_blocks // device_blocks
     begin = shard_tokens // pieces
-    near = []
-    for c, out in enumerate(pieces_out):
-        if len(out) > 1:
-            results = out[:heads]
-            if c + 1 < pieces:
-                results = [results[0], *held[c]]
-            near.append(to_shards(results))
-    att, dq = None, None
-    if whole:
-        rest = pieces_out[-1][0]
-        if near:
-            rest, *near[-1][heads // 2 :] = lax.optimization_barrier(
-                (rest, *near[-1][heads // 2 :])
+    shapes = [(runs, pieces, rows, heads * HEAD_WIDTH)] * 2 + [
+        (1, 1, shard_tokens, heads * HEAD_WIDTH)
+    ] * 2
+
+    def results_at(first, c):
+        return [(first + n * begin, rows, runs, c, n) for n in range(2)]
+
+    def grads_at(first, n=2):
+        return [(first + i * shard_tokens, shard_tokens, 1, 0, n + i) for i in range(2)]
+
+    far, near, sums = run(0)
+    if pieces == 2:
+        qd[1], *far = lax.optimization_barrier((qd[1], *far))
+        first = exchange_far(far)
+        far, near = run(1, sums, near)
+        for j in range(half):
+            far[j], first[j] = lax.optimization_barrier((far[j], first[j]))
+        near, *first = lax.optimization_barrier((near, *first))
+        last = exchange_far(far)
+        near = exchange_near(near)
+        everything = results_at(0, 0) + results_at(2 * begin, 1) + grads_at(4 * begin)
+        outs = unpack(
+            member, [(False, [near], everything), (True, first, results_at(0, 0))], shapes
+        )
+        outs = unpack(member, [(True, last, results_at(0, 1) + grads_at(2 * begin))], shapes, outs)
+    else:
+        outs = unpack(
+            member,
+            [
+                (False, [exchange_near(near)], results_at(0, 0)),
+                (True, exchange_far(far), results_at(0, 0)),
+            ],
+            shapes[:2],
+        )
+        if not whole:
+            sums = lax.psum_scatter(
+                sums, "seq", scatter_dimension=0, tiled=True, axis_index_groups=same_head
             )
-        rest = lax.all_to_all(rest, "seq", split_axis=0, concat_axis=0, tiled=True)
-    for c in range(len(near)):
-        parts = [(0, rows, runs, pieces, c, att), (begin, rows, runs, pieces, c, dq)]
-        att, dq = unpack(member.reshape(1), near[c], parts)
-    if whole:
-        c = pieces - 1
-        parts = [(0, rows, runs, pieces, c, att), (begin, rows, runs, pieces, c, dq)]
-        grads = [(2 * begin + n * shard_tokens, shard_tokens, 1, 1, 0, None) for n in range(2)]
-        att, dq, dk, dv = unpack_all(rest, parts + grads)
-    else:
-        grads = lax.psum_scatter(
-            sums[0], "seq", scatter_dimension=0, tiled=True, axis_index_groups=same_head
-        ).reshape(heads, shard_tokens, 2, HEAD_WIDTH)
-        grads = jnp.concatenate(
-            [grads[:, :, 0] * HEAD_WIDTH ** (-0.5), grads[:, :, 1]], axis=1
+        sums = sums.reshape(heads, shard_tokens, 2, HEAD_WIDTH)
+        sums = jnp.concatenate(
+            [sums[:, :, 0] * HEAD_WIDTH ** (-0.5), sums[:, :, 1]], axis=1
         ).astype(jnp.bfloat16)
-        grads = to_shards(
-            [lax.dynamic_index_in_dim(grads, member ^ k, 0, keepdims=False) for k in range(heads)]
-        )
-        dk, dv = unpack(
-            member.reshape(1),
-            grads,
-            [(n * shard_tokens, shard_tokens, 1, 1, 0, None) for n in range(2)],
-        )
-    return tuple(t.reshape(shard_tokens, heads * HEAD_WIDTH) for t in (att, dq, dk, dv))
+        far = [
+            lax.dynamic_index_in_dim(sums, member[0] ^ (half + j), 0, keepdims=False)
+            for j in range(half)
+        ]
+        near = lax.dynamic_slice_in_dim(sums, member[0] - lax.rem(member[0], half), half, axis=0)
+        outs += unpack(
+            member,
+            [
+                (False, [exchange_near(near)], grads_at(0, 0)),
+                (True, exchange_far(far), grads_at(0, 0)),
+            ],
+            shapes[2:],
+        )
+    return tuple(t.reshape(shard_tokens, heads * HEAD_WIDTH) for t in outs)
 
 
 def solution(mesh):

time: 221 us -> 225 us (1.018)
  starting transfers between devices: 26.7 us -> 33 us
    ppermute x7 -> x8, waiting for transfers between devices: 58.2 us -> 43.4 us  [exchange_far(): lax.ppermute(t, 'seq', [(s, s ^ half + j) for s in range(shards)])]
    all_to_all x1, waiting for transfers between devices: 10 us -> 22.2 us  [exchange_near(): lax.all_to_all(results, 'seq', split_axis=0, concat_axis=0, tiled=True, a...]
    ppermute x7 -> x8, starting transfers between devices: 11.2 us -> 15.3 us  [exchange_far(): lax.ppermute(t, 'seq', [(s, s ^ half + j) for s in range(shards)])]
  transfers between devices with their start and end apart: 10 -> 11, of which waited for: 7 -> 7; matrix products, arithmetic and copies ran while one was open for 0% -> 0% of each run, Pallas kernels for 14% -> 14%
where the time goes in v6:
time: 225 us
  waiting for transfers between devices  150 us (67%)
  Pallas kernels  37.1 us (16%)
  starting transfers between devices  33 us (15%)
  local copies, waits for them, and re-layouts  4.09 us (2%)
    all_to_all x2, waiting for transfers between devices, to_heads(): lax.all_to_all(packed, ('seq', 'head'), split_axis=0, concat_axis=0, tile...  83.9 us
    ppermute x8, waiting for transfers between devices, exchange_far(): lax.ppermute(t, 'seq', [(s, s ^ half + j) for s in range(shards)])  43.4 us
    pallas_call x2, Pallas kernels, attend(): pl.pallas_call(functools.partial(attention_kernel, total_blocks - 1, devi...  26.7 us
    all_to_all x1, waiting for transfers between devices, exchange_near(): lax.all_to_all(results, 'seq', split_axis=0, concat_axis=0, tiled=True, a...  22.2 us
    ppermute x8, starting transfers between devices, exchange_far(): lax.ppermute(t, 'seq', [(s, s ^ half + j) for s in range(shards)])  15.3 us
    all_to_all x2, starting transfers between devices, to_heads(): lax.all_to_all(packed, ('seq', 'head'), split_axis=0, concat_axis=0, tile...  11.4 us
    pallas_call x2, Pallas kernels, pack(): pl.pallas_call(functools.partial(pack_kernel, heads, groups, tuple(((at,...  6.36 us
    all_to_all x1, starting transfers between devices, exchange_near(): lax.all_to_all(results, 'seq', split_axis=0, concat_axis=0, tiled=True, a...  6.32 us
  transfers between devices with their start and end apart: 11, of which 7 were waited for; matrix products, arithmetic and copies ran while one was open for 0% of the time, Pallas kernels for 14%

profile of v6, /device:TPU:0, one launch (start us, length us, event | category | flops | bytes accessed | tf_op | source)
XLA Modules:
  0.0 224.5 jit_solution(78074048449152589)
XLA Ops:
  0.6 4.0 %shard_map.102 = bf16[8,4,400,128]{3,2,1,0:T(8,128)(2,1)} custom-call(s32[8,8,8]{2,1,0:T(8,128)} %refs_0_.2, s32[3,8,8]{2,1,0:T(8,128)} %bitcast.30, bf16[128,4096]{1,0:T(8,128)(2,1)} %refs_2_.1, bf16[128,4096]{1,0:T(8,128)(2,1)} %refs_3_.1, bf16[128,4096]{1,0:T(8,128)(2,1)} %refs_0_.3, bf16[128,4096]{1,0:T(8,128)(2,1)} %refs_1_.1), custom_call_target="tpu_custom_call" | custom-call | bytes 6553600 | tf_op jit(solution)/shard_map/pallas_call | solution.py:113
  4.7 7.3 %all-to-all-start = ((bf16[32,400,128]{2,1,0:T(8,128)(2,1)}), bf16[32,400,128]{2,1,0:T(8,128)(2,1)S(1)}, u32[]{:S(2)}, u32[]{:S(2)}) async-start(bf16[32,400,128]{2,1,0:T(8,128)(2,1)} %bitcast.24), calls=%async_computation | async-start | bytes 6553600 | tf_op jit(solution)/shard_map/all_to_all | solution.py:462
  12.0 0.0 copy-start.4
  12.0 2.3 %shard_map.103 = bf16[8,4,128,128]{3,2,1,0:T(8,128)(2,1)} custom-call(bf16[128,4096]{1,0:T(8,128)(2,1)} %refs_0_.3, bf16[128,4096]{1,0:T(8,128)(2,1)} %refs_1_.1), custom_call_target="tpu_custom_call" | custom-call | bytes 2097152 | tf_op jit(solution)/shard_map/pallas_call | solution.py:113
  14.4 71.9 %all-to-all-done = bf16[32,400,128]{2,1,0:T(8,128)(2,1)S(1)} async-done(((bf16[32,400,128]{2,1,0:T(8,128)(2,1)}), bf16[32,400,128]{2,1,0:T(8,128)(2,1)S(1)}, u32[]{:S(2)}, u32[]{:S(2)}) %all-to-all-start) | async-done | bytes 3276832 | tf_op jit(solution)/shard_map/all_to_all | solution.py:462
  86.2 4.1 %all-to-all-start.1 = ((bf16[32,128,128]{2,1,0:T(8,128)(2,1)}), bf16[32,128,128]{2,1,0:T(8,128)(2,1)}, u32[]{:S(2)}, u32[]{:S(2)}) async-start(bf16[32,128,128]{2,1,0:T(8,128)(2,1)} %bitcast.25), calls=%async_computation.1 | async-start | bytes 2097152 | tf_op jit(solution)/shard_map/all_to_all | solution.py:462
  90.4 0.1 reshape.75
  90.5 0.0 copy-done.4
  90.5 0.1 broadcast_in_dim.2
  90.6 0.1 copy.19
  90.6 0.1 min.12.ids_ref
  90.8 0.6 slice_bitcast_fusion.drop_ref
  91.4 13.2 %shard_map.104 = (bf16[512,128]{1,0:T(8,128)(2,1)}, bf16[512,128]{1,0:T(8,128)(2,1)}, bf16[512,128]{1,0:T(8,128)(2,1)}, bf16[512,128]{1,0:T(8,128)(2,1)}, bf16[4...) custom-call(s32[512]{0:T(512)S(1)} %min.12.ids_ref, s32[512]{0:T(512)S(1)} %fusion.1.starts_ref, s32[1]{0:T(128)} %bitcast.6.first_ref, ...), custom_call_target="tpu_custom_call" | custom-call | flops 17179869184 | bytes 10747904 | tf_op jit(solution)/shard_map/pallas_call | solution.py:403
  104.5 12.0 %all-to-all-done.1 = bf16[32,128,128]{2,1,0:T(8,128)(2,1)} async-done(((bf16[32,128,128]{2,1,0:T(8,128)(2,1)}), bf16[32,128,128]{2,1,0:T(8,128)(2,1)}, u32[]{:S(2)}, u32[]{:S(2)}) %all-to-all-start.1) | async-done | bytes 1048608 | tf_op jit(solution)/shard_map/all_to_all | solution.py:462
  116.5 0.8 collective-permute-start
  117.3 3.1 %collective-permute-start.2 = (bf16[512,128]{1,0:T(8,128)(2,1)}, bf16[512,128]{1,0:T(8,128)(2,1)S(1)}, u32[]{:S(2)}, u32[]{:S(2)}) collective-permute-start(bf16[512,128]{1,0:T(8,128)(2,1)} %get-tuple-element.52), channel_id=1, source_target_pairs={{0,20},{4,16},{8,28},{12,24},{16,4},{20,0},{24,12},{28,8},{1,21},{... | collective-permute-start | bytes 393224 | tf_op jit(solution)/shard_map/ppermute | solution.py:473
  120.4 1.5 collective-permute-start.4
  121.8 2.3 %collective-permute-start.6 = (bf16[512,128]{1,0:T(8,128)(2,1)}, bf16[512,128]{1,0:T(8,128)(2,1)S(1)}, u32[]{:S(2)}, u32[]{:S(2)}) collective-permute-start(bf16[512,128]{1,0:T(8,128)(2,1)} %get-tuple-element.58), channel_id=1, source_target_pairs={{0,28},{4,24},{8,20},{12,16},{16,12},{20,8},{24,4},{28,0},{1,29},{... | collective-permute-start | bytes 393224 | tf_op jit(solution)/shard_map/ppermute | solution.py:473
  124.2 13.6 %shard_map.105 = (bf16[1536,128]{1,0:T(8,128)(2,1)}, bf16[1536,128]{1,0:T(8,128)(2,1)}, bf16[1536,128]{1,0:T(8,128)(2,1)}, bf16[1536,128]{1,0:T(8,128)(2,1)}, bf16[4,2048,128]{2,1,0:T(8,128)(2,1)}) custom-call(s32[512]{0:T(512)S(1)} %min.12.ids_ref, s32[512]{0:T(512)S(1)} %fusion.1.starts_ref, s32[1]{0:T(128)} %bitcast.6.first_ref, s32[1]{0:T(128)} %bitcast.member_ref, ...), custom_call_target="tpu_custom_call" | custom-call | flops 17179869184 | bytes 8519680 | tf_op jit(solution)/shard_map/pallas_call | solution.py:403
  137.8 0.0 collective-permute-done.refs_1_
  137.8 0.0 collective-permute-done.2.refs_2_
  137.8 0.0 collective-permute-done.4.refs_3_
  137.8 0.0 copy-start
  137.8 0.6 copy-done
  138.4 0.0 collective-permute-done.6.refs_4_
  138.4 0.0 copy-start.2
  138.4 0.7 copy-done.2
  139.1 6.3 %all-to-all-start.2 = ((bf16[4,2048,128]{2,1,0:T(8,128)(2,1)}), bf16[4,2048,128]{2,1,0:T(8,128)(2,1)S(1)}, u32[]{:S(2)}, u32[]{:S(2)}) async-start(bf16[4,2048,128]{2,1,0:T(8,128)(2,1)} %get-tuple-element.65), calls=%async_computation.2 | async-start | bytes 4194304 | tf_op jit(solution)/shard_map/all_to_all | solution.py:478
  145.4 4.5 %collective-permute-start.7 = (bf16[1536,128]{1,0:T(8,128)(2,1)}, bf16[1536,128]{1,0:T(8,128)(2,1)S(1)}, u32[]{:S(2)}, u32[]{:S(2)}) collective-permute-start(bf16[1536,128]{1,0:T(8,128)(2,1)} %get-tuple-element.59), channel_id=1, source_target_pairs={{0,28},{4,24},{8,20},{12,16},{16,12},{20,8},{24,4},{28,0},{1,29},{... | collective-permute-start | bytes 1179656 | tf_op jit(solution)/shard_map/ppermute | solution.py:473
  149.9 0.8 collective-permute-start.5
  150.7 0.0 collective-permute-start.3
  150.7 2.4 %collective-permute-start.1 = (bf16[1536,128]{1,0:T(8,128)(2,1)}, bf16[1536,128]{1,0:T(8,128)(2,1)}, u32[]{:S(2)}, u32[]{:S(2)}) collective-permute-start(bf16[1536,128]{1,0:T(8,128)(2,1)} %get-tuple-element.50), channel_id=1, source_target_pairs={{0,16},{4,20},{8,24},{12,28},{16,0},{20,4},{24,8},{28,12},{1,17},{... | collective-permute-start | bytes 1179656 | tf_op jit(solution)/shard_map/ppermute | solution.py:473
  153.1 22.2 %all-to-all-done.2.refs_0_ = bf16[4,2048,128]{2,1,0:T(8,128)(2,1)S(1)} async-done(((bf16[4,2048,128]{2,1,0:T(8,128)(2,1)}), bf16[4,2048,128]{2,1,0:T(8,128)(2,1)S(1)}, u32[]{:S(2)}, u32[]{:S(2)}) %all-to-all-start.2) | async-done | bytes 2097184 | tf_op jit(solution)/shard_map/all_to_all | solution.py:478
  175.3 0.0 copy-start.1
  175.3 0.9 copy-done.1
  176.2 0.0 copy-start.3
  176.2 0.9 copy-done.3
  177.1 1.7 shard_map.106
  178.8 12.3 %collective-permute-done.7.refs_3_ = bf16[1536,128]{1,0:T(8,128)(2,1)S(1)} collective-permute-done((bf16[1536,128]{1,0:T(8,128)(2,1)}, bf16[1536,128]{1,0:T(8,128)(2,1)S(1)}, u32[]{:S(2)}, u32[]{:S(2)}) %collective-permute-start.7) | collective-permute-done | bytes 393248 | tf_op jit(solution)/shard_map/ppermute | solution.py:473
  191.1 7.3 %collective-permute-done.5.refs_2_ = bf16[1536,128]{1,0:T(8,128)(2,1)S(1)} collective-permute-done((bf16[1536,128]{1,0:T(8,128)(2,1)}, bf16[1536,128]{1,0:T(8,128)(2,1)S(1)}, u32[]{:S(2)}, u32[]{:S(2)}) %collective-permute-start.5) | collective-permute-done | bytes 393248 | tf_op jit(solution)/shard_map/ppermute | solution.py:473
  198.5 18.0 %collective-permute-done.3.refs_1_ = bf16[1536,128]{1,0:T(8,128)(2,1)S(1)} collective-permute-done((bf16[1536,128]{1,0:T(8,128)(2,1)}, bf16[1536,128]{1,0:T(8,128)(2,1)S(1)}, u32[]{:S(2)}, u32[]{:S(2)}) %collective-permute-start.3) | collective-permute-done | bytes 393248 | tf_op jit(solution)/shard_map/ppermute | solution.py:473
  216.4 5.8 %collective-permute-done.1.refs_0_ = bf16[1536,128]{1,0:T(8,128)(2,1)} collective-permute-done((bf16[1536,128]{1,0:T(8,128)(2,1)}, bf16[1536,128]{1,0:T(8,128)(2,1)}, u32[]{:S(2)}, u32[]{:S(2)}) %collective-permute-start.1) | collective-permute-done | bytes 393248 | tf_op jit(solution)/shard_map/ppermute | solution.py:473
  222.2 2.3 %shard_map.107 = (bf16[4,2,64,1024]{3,2,1,0:T(8,128)(2,1)}, bf16[4,2,64,1024]{3,2,1,0:T(8,128)(2,1)}, bf16[1,1,512,1024]{3,2,1,0:T(8,128)(2,1)}, bf16[1,1,512,1024]{3,2,1,0:T(8,128)(2,1)}) custom-call(s32[1]{0:T(128)} %bitcast.member_ref, ...), custom_call_target="tpu_custom_call", output_to_operand_aliasing={{0}: (5, {}), {1}: (6, {}), {2}: (7, {}), {3}: (8, {})} | custom-call | bytes 3145728 | tf_op jit(solution)/shard_map/pallas_call | solution.py:169
  (9 shorter events, 0.1 us)
Async XLA Ops:
  4.7 81.6 %all-to-all-start = ((bf16[32,400,128]{2,1,0:T(8,128)(2,1)}), bf16[32,400,128]{2,1,0:T(8,128)(2,1)S(1)}, u32[]{:S(2)}, u32[]{:S(2)}) async-start(bf16[32,400,128]{2,1,0:T(8,128)(2,1)} %bitcast.24), calls=%async_computation | async-start | bytes 6553600 | tf_op jit(solution)/shard_map/all_to_all | solution.py:462
  12.0 78.5 %copy-start.4 = (s32[2]{0:T(128)S(1)}, s32[2]{0:T(128)}, u32[]{:S(2)}) copy-start(s32[2]{0:T(128)} %param.12) | copy-start | bytes 28
  86.2 30.3 %all-to-all-start.1 = ((bf16[32,128,128]{2,1,0:T(8,128)(2,1)}), bf16[32,128,128]{2,1,0:T(8,128)(2,1)}, u32[]{:S(2)}, u32[]{:S(2)}) async-start(bf16[32,128,128]{2,1,0:T(8,128)(2,1)} %bitcast.25), calls=%async_computation.1 | async-start | bytes 2097152 | tf_op jit(solution)/shard_map/all_to_all | solution.py:462
  116.5 21.2 %collective-permute-start = (bf16[512,128]{1,0:T(8,128)(2,1)}, bf16[512,128]{1,0:T(8,128)(2,1)S(1)}, u32[]{:S(2)}, u32[]{:S(2)}) collective-permute-start(bf16[512,128]{1,0:T(8,128)(2,1)} %get-tuple-element.49), channel_id=1, source_target_pairs={{0,16},{4,20},{8,24},{12,28},{16,0},{20,4},{24,8},{28,12},{1,17},{... | collective-permute-start | bytes 393224 | tf_op jit(solution)/shard_map/ppermute | solution.py:473
  117.3 20.5 %collective-permute-start.2 = (bf16[512,128]{1,0:T(8,128)(2,1)}, bf16[512,128]{1,0:T(8,128)(2,1)S(1)}, u32[]{:S(2)}, u32[]{:S(2)}) collective-permute-start(bf16[512,128]{1,0:T(8,128)(2,1)} %get-tuple-element.52), channel_id=1, source_target_pairs={{0,20},{4,16},{8,28},{12,24},{16,4},{20,0},{24,12},{28,8},{1,21},{... | collective-permute-start | bytes 393224 | tf_op jit(solution)/shard_map/ppermute | solution.py:473
  120.4 17.4 %collective-permute-start.4 = (bf16[512,128]{1,0:T(8,128)(2,1)}, bf16[512,128]{1,0:T(8,128)(2,1)S(1)}, u32[]{:S(2)}, u32[]{:S(2)}) collective-permute-start(bf16[512,128]{1,0:T(8,128)(2,1)} %get-tuple-element.55), channel_id=1, source_target_pairs={{0,24},{4,28},{8,16},{12,20},{16,8},{20,12},{24,0},{28,4},{1,25},{... | collective-permute-start | bytes 393224 | tf_op jit(solution)/shard_map/ppermute | solution.py:473
  121.8 16.6 %collective-permute-start.6 = (bf16[512,128]{1,0:T(8,128)(2,1)}, bf16[512,128]{1,0:T(8,128)(2,1)S(1)}, u32[]{:S(2)}, u32[]{:S(2)}) collective-permute-start(bf16[512,128]{1,0:T(8,128)(2,1)} %get-tuple-element.58), channel_id=1, source_target_pairs={{0,28},{4,24},{8,20},{12,16},{16,12},{20,8},{24,4},{28,0},{1,29},{... | collective-permute-start | bytes 393224 | tf_op jit(solution)/shard_map/ppermute | solution.py:473
  137.8 0.7 copy-start
  138.4 0.7 copy-start.2
  139.1 36.2 %all-to-all-start.2 = ((bf16[4,2048,128]{2,1,0:T(8,128)(2,1)}), bf16[4,2048,128]{2,1,0:T(8,128)(2,1)S(1)}, u32[]{:S(2)}, u32[]{:S(2)}) async-start(bf16[4,2048,128]{2,1,0:T(8,128)(2,1)} %get-tuple-element.65), calls=%async_computation.2 | async-start | bytes 4194304 | tf_op jit(solution)/shard_map/all_to_all | solution.py:478
  145.4 45.7 %collective-permute-start.7 = (bf16[1536,128]{1,0:T(8,128)(2,1)}, bf16[1536,128]{1,0:T(8,128)(2,1)S(1)}, u32[]{:S(2)}, u32[]{:S(2)}) collective-permute-start(bf16[1536,128]{1,0:T(8,128)(2,1)} %get-tuple-element.59), channel_id=1, source_target_pairs={{0,28},{4,24},{8,20},{12,16},{16,12},{20,8},{24,4},{28,0},{1,29},{... | collective-permute-start | bytes 1179656 | tf_op jit(solution)/shard_map/ppermute | solution.py:473
  149.9 48.5 %collective-permute-start.5 = (bf16[1536,128]{1,0:T(8,128)(2,1)}, bf16[1536,128]{1,0:T(8,128)(2,1)S(1)}, u32[]{:S(2)}, u32[]{:S(2)}) collective-permute-start(bf16[1536,128]{1,0:T(8,128)(2,1)} %get-tuple-element.56), channel_id=1, source_target_pairs={{0,24},{4,28},{8,16},{12,20},{16,8},{20,12},{24,0},{28,4},{1,25},{... | collective-permute-start | bytes 1179656 | tf_op jit(solution)/shard_map/ppermute | solution.py:473
  150.7 65.7 %collective-permute-start.3 = (bf16[1536,128]{1,0:T(8,128)(2,1)}, bf16[1536,128]{1,0:T(8,128)(2,1)S(1)}, u32[]{:S(2)}, u32[]{:S(2)}) collective-permute-start(bf16[1536,128]{1,0:T(8,128)(2,1)} %get-tuple-element.53), channel_id=1, source_target_pairs={{0,20},{4,16},{8,28},{12,24},{16,4},{20,0},{24,12},{28,8},{1,21},{... | collective-permute-start | bytes 1179656 | tf_op jit(solution)/shard_map/ppermute | solution.py:473
  150.7 71.5 %collective-permute-start.1 = (bf16[1536,128]{1,0:T(8,128)(2,1)}, bf16[1536,128]{1,0:T(8,128)(2,1)}, u32[]{:S(2)}, u32[]{:S(2)}) collective-permute-start(bf16[1536,128]{1,0:T(8,128)(2,1)} %get-tuple-element.50), channel_id=1, source_target_pairs={{0,16},{4,20},{8,24},{12,28},{16,0},{20,4},{24,8},{28,12},{1,17},{... | collective-permute-start | bytes 1179656 | tf_op jit(solution)/shard_map/ppermute | solution.py:473
  175.3 0.9 copy-start.1
  176.2 0.9 copy-start.3

commit v7 on v5

--- a/solution.py
+++ b/solution.py
@@ -237,8 +237,9 @@
     qd_ref = refs.pop(0) if has_qd else kv_ref
     start_ref = refs.pop(0) if has_start else None
     out_refs = [refs.pop(0) for _ in range(1 if joined else targets)]
-    acc, retain, waiting, near = refs[:4]
-    done, sems = refs[4:6] if joined else (None, None)
+    sums_ref = None if joined else refs.pop(0)
+    acc, retain, waiting, near, sems = refs[:5]
+    done = refs[5] if joined else None
     earlier, start_sem = refs[-2:] if has_start else (None, None)
     scale = HEAD_WIDTH ** (-0.5)
     steps = targets * (out_rows // BLOCK_TOKENS)
@@ -368,8 +369,19 @@
         for store in stores:
             store.wait()
     else:
+        rows = acc.shape[0] // targets
+        stores = [
+            pltpu.make_async_copy(
+                acc.at[pl.ds(n * rows, rows), :], sums_ref.at[pl.ds(n * rows, rows), :], sems.at[n]
+            )
+            for n in range(targets)
+        ]
+        for store in stores:
+            store.start()
         for k, out_ref in enumerate(out_refs):
             out_ref[...] = near[member_ref[0] ^ k]
+        for store in stores:
+            store.wait()
 
 
 def attend(
@@ -393,15 +405,13 @@
         pltpu.VMEM((UNROLL, 2 * BLOCK_TOKENS, WIDE), jnp.bfloat16),
         pltpu.VMEM((targets, 2 * out_rows, HEAD_WIDTH), jnp.bfloat16),
     ]
-    if joined:
-        scratch = [pltpu.VMEM(accumulator, jnp.float32)] + scratch
-    else:
+    scratch = [pltpu.VMEM(accumulator, jnp.float32)] + scratch + [
+        pltpu.SemaphoreType.DMA((targets,))
+    ]
+    if not joined:
         out_shape.append(pltpu.HBM(accumulator, jnp.float32))
     if joined:
-        scratch += [
-            pltpu.VMEM(out_shape[0].shape, jnp.bfloat16),
-            pltpu.SemaphoreType.DMA((targets,)),
-        ]
+        scratch.append(pltpu.VMEM(out_shape[0].shape, jnp.bfloat16))
     sums_bytes = 8 * length * HEAD_WIDTH
     limit = VMEM_LIMIT + 2 * (kv.size + source.size) + (1 if start is None else 2) * sums_bytes
     keep = in_vmem if 2 * limit < VMEM_BYTES else lambda t: t
@@ -429,7 +439,7 @@
         ),
         out_shape=out_shape,
         in_specs=[smem, smem, smem, smem, vmem] + operand_specs,
-        out_specs=[anywhere] if joined else [vmem] * len(out_shape),
+        out_specs=[anywhere] if joined else [vmem] * targets + [anywhere],
         scratch_shapes=scratch,
         compiler_params=pltpu.CompilerParams(vmem_limit_bytes=limit),
         cost_estimate=pl.CostEstimate(
@@ -544,9 +554,7 @@
         )
         sums = pieces_out[c][heads:]
         if c + 1 < pieces:
-            late = 3 * heads // 4
-            qd[c + 1], *results = lax.optimization_barrier((qd[c + 1], *pieces_out[c][late:heads]))
-            held.append([*pieces_out[c][1:late], *results])
+            held.append(pieces_out[c][1:heads])
     runs = shard_blocks // device_blocks
     begin = shard_tokens // pieces
     near = []

time: 221 us -> 219 us (level)
  local copies, waits for them, and re-layouts: 4.1 us -> 1 us
    ppermute x7, waiting for transfers between devices: 58.2 us -> 53.7 us  [to_shards(): received[k] = lax.ppermute(results[k], 'seq', pairs)]
    all_to_all x2, waiting for transfers between devices: 83.9 us -> 87 us  [to_heads(): lax.all_to_all(packed, ('seq', 'head'), split_axis=0, concat_axis=0, tile...]
    unnamed x12 -> x4, local copies, waits for them, and re-layouts: 3.12 us -> 0.01 us
  transfers between devices with their start and end apart: 10 -> 10, of which waited for: 7 -> 5; matrix products, arithmetic and copies ran while one was open for 0% -> 0% of each run, Pallas kernels for 14% -> 15%
where the time goes in v7:
time: 219 us; the launch traced here: 218 us
  waiting for transfers between devices  152 us (69%)
  Pallas kernels  38.2 us (17%)
  starting transfers between devices  26.3 us (12%)
    all_to_all x2, waiting for transfers between devices, to_heads(): lax.all_to_all(packed, ('seq', 'head'), split_axis=0, concat_axis=0, tile...  87 us
    ppermute x7, waiting for transfers between devices, to_shards(): received[k] = lax.ppermute(results[k], 'seq', pairs)  53.7 us
    pallas_call x2, Pallas kernels, attend(): pl.pallas_call(functools.partial(attention_kernel, total_blocks - 1, devi...  27.3 us
    all_to_all x2, starting transfers between devices, to_heads(): lax.all_to_all(packed, ('seq', 'head'), split_axis=0, concat_axis=0, tile...  11.4 us
    ppermute x7, starting transfers between devices, to_shards(): received[k] = lax.ppermute(results[k], 'seq', pairs)  11.3 us
    all_to_all x1, waiting for transfers between devices, per_device(): rest = lax.all_to_all(rest, 'seq', split_axis=0, concat_axis=0, tiled=True)  11 us
    pallas_call x2, Pallas kernels, pack(): pl.pallas_call(functools.partial(pack_kernel, heads, groups, tuple(((at,...  6.36 us
  transfers between devices with their start and end apart: 10, of which 5 were waited for; matrix products, arithmetic and copies ran while one was open for 0% of the time, Pallas kernels for 15%

profile of v7, /device:TPU:0, one launch (start us, length us, event | category | flops | bytes accessed | tf_op | source)
XLA Modules:
  0.0 218.1 jit_solution(686064423459906490)
XLA Ops:
  0.6 4.0 %shard_map.102 = bf16[8,4,400,128]{3,2,1,0:T(8,128)(2,1)} custom-call(s32[8,8,8]{2,1,0:T(8,128)} %refs_0_.2, s32[3,8,8]{2,1,0:T(8,128)} %bitcast.28, bf16[128,4096]{1,0:T(8,128)(2,1)} %refs_2_.1, bf16[128,4096]{1,0:T(8,128)(2,1)} %refs_3_.1, bf16[128,4096]{1,0:T(8,128)(2,1)} %refs_0_.3, bf16[128,4096]{1,0:T(8,128)(2,1)} %refs_1_.1), custom_call_target="tpu_custom_call" | custom-call | bytes 6553600 | tf_op jit(solution)/shard_map/pallas_call | solution.py:113
  4.7 7.3 %all-to-all-start = ((bf16[32,400,128]{2,1,0:T(8,128)(2,1)}), bf16[32,400,128]{2,1,0:T(8,128)(2,1)S(1)}, u32[]{:S(2)}, u32[]{:S(2)}) async-start(bf16[32,400,128]{2,1,0:T(8,128)(2,1)} %bitcast.24), calls=%async_computation | async-start | bytes 6553600 | tf_op jit(solution)/shard_map/all_to_all | solution.py:481
  12.0 0.0 copy-start.1
  12.0 2.3 %shard_map.103 = bf16[8,4,128,128]{3,2,1,0:T(8,128)(2,1)} custom-call(bf16[128,4096]{1,0:T(8,128)(2,1)} %refs_0_.3, bf16[128,4096]{1,0:T(8,128)(2,1)} %refs_1_.1), custom_call_target="tpu_custom_call" | custom-call | bytes 2097152 | tf_op jit(solution)/shard_map/pallas_call | solution.py:113
  14.4 71.9 %all-to-all-done = bf16[32,400,128]{2,1,0:T(8,128)(2,1)S(1)} async-done(((bf16[32,400,128]{2,1,0:T(8,128)(2,1)}), bf16[32,400,128]{2,1,0:T(8,128)(2,1)S(1)}, u32[]{:S(2)}, u32[]{:S(2)}) %all-to-all-start) | async-done | bytes 3276832 | tf_op jit(solution)/shard_map/all_to_all | solution.py:481
  86.2 4.1 %all-to-all-start.1 = ((bf16[32,128,128]{2,1,0:T(8,128)(2,1)}), bf16[32,128,128]{2,1,0:T(8,128)(2,1)}, u32[]{:S(2)}, u32[]{:S(2)}) async-start(bf16[32,128,128]{2,1,0:T(8,128)(2,1)} %bitcast.25), calls=%async_computation.1 | async-start | bytes 2097152 | tf_op jit(solution)/shard_map/all_to_all | solution.py:481
  90.4 0.1 reshape.76
  90.5 0.0 copy-done.1
  90.5 0.1 broadcast_in_dim.2
  90.6 0.1 copy.17
  90.6 0.1 min.12.ids_ref
  90.8 0.6 slice_bitcast_fusion.drop_ref
  91.4 14.0 %shard_map.104 = (bf16[512,128]{1,0:T(8,128)(2,1)}, bf16[512,128]{1,0:T(8,128)(2,1)}, bf16[512,128]{1,0:T(8,128)(2,1)}, bf16[512,128]{1,0:T(8,128)(2,1)}, bf16[5...) custom-call(s32[512]{0:T(512)S(1)} %min.12.ids_ref, ...), custom_call_target="tpu_custom_call" | custom-call | flops 17179869184 | bytes 10747904 | tf_op jit(solution)/shard_map/pallas_call | solution.py:423
  105.3 2.6 %collective-permute-start = (bf16[512,128]{1,0:T(8,128)(2,1)}, bf16[512,128]{1,0:T(8,128)(2,1)S(1)}, u32[]{:S(2)}, u32[]{:S(2)}) collective-permute-start(bf16[512,128]{1,0:T(8,128)(2,1)} %get-tuple-element.25), channel_id=1, source_target_pairs={{0,16},{4,20},{8,24},{12,28},{16,0},{20,4},{24,8},{28,12},{1,17},{... | collective-permute-start | bytes 393224 | tf_op jit(solution)/shard_map/ppermute | solution.py:494
  108.0 1.5 collective-permute-start.1
  109.5 3.3 %collective-permute-start.2 = (bf16[512,128]{1,0:T(8,128)(2,1)}, bf16[512,128]{1,0:T(8,128)(2,1)}, u32[]{:S(2)}, u32[]{:S(2)}) collective-permute-start(bf16[512,128]{1,0:T(8,128)(2,1)} %get-tuple-element.27), channel_id=1, source_target_pairs={{0,24},{4,28},{8,16},{12,20},{16,8},{20,12},{24,0},{28,4},{1,25},{... | collective-permute-start | bytes 393224 | tf_op jit(solution)/shard_map/ppermute | solution.py:494
  112.8 0.3 collective-permute-start.3
  113.1 15.2 %all-to-all-done.1 = bf16[32,128,128]{2,1,0:T(8,128)(2,1)} async-done(((bf16[32,128,128]{2,1,0:T(8,128)(2,1)}), bf16[32,128,128]{2,1,0:T(8,128)(2,1)}, u32[]{:S(2)}, u32[]{:S(2)}) %all-to-all-start.1) | async-done | bytes 1048608 | tf_op jit(solution)/shard_map/all_to_all | solution.py:481
  128.2 13.4 %shard_map.105 = bf16[8,1536,128]{2,1,0:T(8,128)(2,1)} custom-call(s32[512]{0:T(512)S(1)} %min.12.ids_ref, s32[512]{0:T(512)S(1)} %fusion.1.starts_ref, s32[1]{0:T(128)} %bitcast.5.first_ref, s32[1]{0:T(128)} %bitcast.6.member_ref, s32[64,8]{1,0:T(8,128)} %slice_bitcast_fusion.drop_ref, bf16[12800,128]{1,0:T(8,128)(2,1)S(1)} %bitcast.23, ...), custom_call_target="tpu_custom_call" | custom-call | flops 17179869184 | bytes 8519680 | tf_op jit(solution)/shard_map/pallas_call | solution.py:423
  141.6 0.0 copy-start
  141.6 0.0 collective-permute-done.refs_4_
  141.6 0.0 collective-permute-done.1.refs_3_
  141.6 0.0 collective-permute-done.2.refs_2_
  141.6 0.0 collective-permute-done.3.refs_1_
  141.6 3.7 %all-to-all-start.2 = ((bf16[8,1536,128]{2,1,0:T(8,128)(2,1)}), bf16[8,1536,128]{2,1,0:T(8,128)(2,1)S(1)}, u32[]{:S(2)}, u32[]{:S(2)}) async-start(bf16[8,1536,128]{2,1,0:T(8,128)(2,1)} %shard_map.105), calls=%async_computation.2 | async-start | bytes 6291456 | tf_op jit(solution)/shard_map/all_to_all | solution.py:574
  145.3 2.8 %collective-permute-start.4 = (bf16[512,128]{1,0:T(8,128)(2,1)}, bf16[512,128]{1,0:T(8,128)(2,1)S(1)}, u32[]{:S(2)}, u32[]{:S(2)}) collective-permute-start(bf16[512,128]{1,0:T(8,128)(2,1)} %get-tuple-element.35), channel_id=1, source_target_pairs={{0,12},{4,8},{8,4},{12,0},{16,28},{20,24},{24,20},{28,16},{1,13},{... | collective-permute-start | bytes 393224 | tf_op jit(solution)/shard_map/ppermute | solution.py:494
  148.1 0.5 collective-permute-start.5
  148.7 0.2 collective-permute-start.6
  148.9 52.2 %collective-permute-done.4.refs_5_ = bf16[512,128]{1,0:T(8,128)(2,1)S(1)} collective-permute-done((bf16[512,128]{1,0:T(8,128)(2,1)}, bf16[512,128]{1,0:T(8,128)(2,1)S(1)}, u32[]{:S(2)}, u32[]{:S(2)}) %collective-permute-start.4) | collective-permute-done | bytes 131104 | tf_op jit(solution)/shard_map/ppermute | solution.py:494
  201.1 1.5 collective-permute-done.5.refs_6_
  202.5 0.0 collective-permute-done.6.refs_7_
  202.5 0.0 copy-done
  202.6 2.2 %shard_map.106 = (bf16[4,2,64,1024]{3,2,1,0:T(8,128)(2,1)}, bf16[4,2,64,1024]{3,2,1,0:T(8,128)(2,1)}) custom-call(s32[1]{0:T(128)} %bitcast.6.member_ref, bf16[512,128]{1,0:T(8,128)(2,1)S(1)} %copy-done, bf16[512,128]{1,0:T(8,128)(2,1)} %collective-permute-done.3.refs_1_, bf16[512,128]{1,0:T(8,128)(2,1)} %collective-permute-done.2.refs_2_, ...), custom_call_target="tpu_custom_call" | custom-call | bytes 2097152 | tf_op jit(solution)/shard_map/pallas_call | solution.py:156
  204.8 11.0 %all-to-all-done.2.piece_ref = bf16[8,1536,128]{2,1,0:T(8,128)(2,1)S(1)} async-done(((bf16[8,1536,128]{2,1,0:T(8,128)(2,1)}), bf16[8,1536,128]{2,1,0:T(8,128)(2,1)S(1)}, u32[]{:S(2)}, u32[]{:S(2)}) %all-to-all-start.2) | async-done | bytes 3145760 | tf_op jit(solution)/shard_map/all_to_all | solution.py:574
  215.8 2.3 %shard_map.107 = (bf16[4,2,64,1024]{3,2,1,0:T(8,128)(2,1)}, bf16[4,2,64,1024]{3,2,1,0:T(8,128)(2,1)}, bf16[1,1,512,1024]{3,2,1,0:T(8,128)(2,1)}, bf16[1,1,512,1024]{3,2,1,0:T(8,128)(2,1)}) custom-call(bf16[8,1536,128]{2,1,0:T(8,128)(2,1)S(1)} %all-to-all-done.2.piece_ref, ...), custom_call_target="tpu_custom_call", output_to_operand_aliasing={{0}: (1, {}), {1}: (2, {})} | custom-call | bytes 6291456 | tf_op jit(solution)/shard_map/pallas_call | solution.py:201
  (9 shorter events, 0.1 us)
Async XLA Ops:
  4.7 81.6 %all-to-all-start = ((bf16[32,400,128]{2,1,0:T(8,128)(2,1)}), bf16[32,400,128]{2,1,0:T(8,128)(2,1)S(1)}, u32[]{:S(2)}, u32[]{:S(2)}) async-start(bf16[32,400,128]{2,1,0:T(8,128)(2,1)} %bitcast.24), calls=%async_computation | async-start | bytes 6553600 | tf_op jit(solution)/shard_map/all_to_all | solution.py:481
  12.0 78.5 %copy-start.1 = (s32[2]{0:T(128)S(1)}, s32[2]{0:T(128)}, u32[]{:S(2)}) copy-start(s32[2]{0:T(128)} %param.12) | copy-start | bytes 28
  86.2 42.0 %all-to-all-start.1 = ((bf16[32,128,128]{2,1,0:T(8,128)(2,1)}), bf16[32,128,128]{2,1,0:T(8,128)(2,1)}, u32[]{:S(2)}, u32[]{:S(2)}) async-start(bf16[32,128,128]{2,1,0:T(8,128)(2,1)} %bitcast.25), calls=%async_computation.1 | async-start | bytes 2097152 | tf_op jit(solution)/shard_map/all_to_all | solution.py:481
  105.3 36.3 %collective-permute-start = (bf16[512,128]{1,0:T(8,128)(2,1)}, bf16[512,128]{1,0:T(8,128)(2,1)S(1)}, u32[]{:S(2)}, u32[]{:S(2)}) collective-permute-start(bf16[512,128]{1,0:T(8,128)(2,1)} %get-tuple-element.25), channel_id=1, source_target_pairs={{0,16},{4,20},{8,24},{12,28},{16,0},{20,4},{24,8},{28,12},{1,17},{... | collective-permute-start | bytes 393224 | tf_op jit(solution)/shard_map/ppermute | solution.py:494
  108.0 33.6 %collective-permute-start.1 = (bf16[512,128]{1,0:T(8,128)(2,1)}, bf16[512,128]{1,0:T(8,128)(2,1)S(1)}, u32[]{:S(2)}, u32[]{:S(2)}) collective-permute-start(bf16[512,128]{1,0:T(8,128)(2,1)} %get-tuple-element.26), channel_id=1, source_target_pairs={{0,20},{4,16},{8,28},{12,24},{16,4},{20,0},{24,12},{28,8},{1,21},{... | collective-permute-start | bytes 393224 | tf_op jit(solution)/shard_map/ppermute | solution.py:494
  109.5 32.2 %collective-permute-start.2 = (bf16[512,128]{1,0:T(8,128)(2,1)}, bf16[512,128]{1,0:T(8,128)(2,1)}, u32[]{:S(2)}, u32[]{:S(2)}) collective-permute-start(bf16[512,128]{1,0:T(8,128)(2,1)} %get-tuple-element.27), channel_id=1, source_target_pairs={{0,24},{4,28},{8,16},{12,20},{16,8},{20,12},{24,0},{28,4},{1,25},{... | collective-permute-start | bytes 393224 | tf_op jit(solution)/shard_map/ppermute | solution.py:494
  112.8 28.9 %collective-permute-start.3 = (bf16[512,128]{1,0:T(8,128)(2,1)}, bf16[512,128]{1,0:T(8,128)(2,1)}, u32[]{:S(2)}, u32[]{:S(2)}) collective-permute-start(bf16[512,128]{1,0:T(8,128)(2,1)} %get-tuple-element.28), channel_id=1, source_target_pairs={{0,28},{4,24},{8,20},{12,16},{16,12},{20,8},{24,4},{28,0},{1,29},{... | collective-permute-start | bytes 393224 | tf_op jit(solution)/shard_map/ppermute | solution.py:494
  141.6 61.0 %copy-start = (bf16[512,128]{1,0:T(8,128)(2,1)S(1)}, bf16[512,128]{1,0:T(8,128)(2,1)}, u32[]{:S(2)}) copy-start(bf16[512,128]{1,0:T(8,128)(2,1)} %get-tuple-element.30.refs_0_) | copy-start | bytes 393220
  141.6 74.1 %all-to-all-start.2 = ((bf16[8,1536,128]{2,1,0:T(8,128)(2,1)}), bf16[8,1536,128]{2,1,0:T(8,128)(2,1)S(1)}, u32[]{:S(2)}, u32[]{:S(2)}) async-start(bf16[8,1536,128]{2,1,0:T(8,128)(2,1)} %shard_map.105), calls=%async_computation.2 | async-start | bytes 6291456 | tf_op jit(solution)/shard_map/all_to_all | solution.py:574
  145.3 55.8 %collective-permute-start.4 = (bf16[512,128]{1,0:T(8,128)(2,1)}, bf16[512,128]{1,0:T(8,128)(2,1)S(1)}, u32[]{:S(2)}, u32[]{:S(2)}) collective-permute-start(bf16[512,128]{1,0:T(8,128)(2,1)} %get-tuple-element.35), channel_id=1, source_target_pairs={{0,12},{4,8},{8,4},{12,0},{16,28},{20,24},{24,20},{28,16},{1,13},{... | collective-permute-start | bytes 393224 | tf_op jit(solution)/shard_map/ppermute | solution.py:494
  148.1 54.4 %collective-permute-start.5 = (bf16[512,128]{1,0:T(8,128)(2,1)}, bf16[512,128]{1,0:T(8,128)(2,1)S(1)}, u32[]{:S(2)}, u32[]{:S(2)}) collective-permute-start(bf16[512,128]{1,0:T(8,128)(2,1)} %get-tuple-element.36), channel_id=1, source_target_pairs={{0,8},{4,12},{8,0},{12,4},{16,24},{20,28},{24,16},{28,20},{1,9},{5... | collective-permute-start | bytes 393224 | tf_op jit(solution)/shard_map/ppermute | solution.py:494
  148.7 53.9 %collective-permute-start.6 = (bf16[512,128]{1,0:T(8,128)(2,1)}, bf16[512,128]{1,0:T(8,128)(2,1)S(1)}, u32[]{:S(2)}, u32[]{:S(2)}) collective-permute-start(bf16[512,128]{1,0:T(8,128)(2,1)} %get-tuple-element.37), channel_id=1, source_target_pairs={{0,4},{4,0},{8,12},{12,8},{16,20},{20,16},{24,28},{28,24},{1,5},{5... | collective-permute-start | bytes 393224 | tf_op jit(solution)/shard_map/ppermute | solution.py:494

commit v8 on v7

--- a/solution.py
+++ b/solution.py
@@ -464,6 +464,7 @@
     total_blocks = shards * shard_blocks
     first_block = team * team_blocks
     whole = teams == 1
+    half = heads // 2
     pieces = device_blocks if whole else 1
     per = device_blocks // pieces
     rows = tokens // pieces
@@ -487,9 +488,9 @@
             axis_index_groups=same_team_all,
         )
 
-    def to_shards(results):
+    def to_shards(results, partners):
         received = list(results)
-        for k in reversed(range(1, heads)):
+        for k in reversed(partners):
             pairs = [(s, s ^ k) for s in range(shards)]
             received[k] = lax.ppermute(results[k], "seq", pairs)
         return received
@@ -529,7 +530,7 @@
     listed = jnp.clip(listed, 0, total_blocks - 1).reshape(-1)
     starts = listed // device_blocks * kv.shape[1] + listed % device_blocks * BLOCK_TOKENS
     pieces_out = []
-    held = []
+    near = []
     sums = []
     for c in range(pieces):
         pieces_out.append(
@@ -554,23 +555,22 @@
         )
         sums = pieces_out[c][heads:]
         if c + 1 < pieces:
-            held.append(pieces_out[c][1:heads])
+            late = 3 * heads // 4
+            ready = list(pieces_out[c][:heads])
+            ready = to_shards(ready, range(late, heads))
+            qd[c + 1], *ready[late:] = lax.optimization_barrier((qd[c + 1], *ready[late:]))
+            qd[c + 1], *ready[half:late] = lax.optimization_barrier((qd[c + 1], *ready[half:late]))
+            near.append(to_shards(ready, range(half, late)))
     runs = shard_blocks // device_blocks
     begin = shard_tokens // pieces
-    near = []
-    for c, out in enumerate(pieces_out):
-        if len(out) > 1:
-            results = out[:heads]
-            if c + 1 < pieces:
-                results = [results[0], *held[c]]
-            near.append(to_shards(results))
+    if not whole:
+        near.append(to_shards(pieces_out[-1][:heads], range(1, heads)))
     att, dq = None, None
     if whole:
         rest = pieces_out[-1][0]
         if near:
-            rest, *near[-1][heads // 2 :] = lax.optimization_barrier(
-                (rest, *near[-1][heads // 2 :])
-            )
+            rest, *near[-1] = lax.optimization_barrier((rest, *near[-1]))
+            near[-1] = to_shards(near[-1], range(1, half))
         rest = lax.all_to_all(rest, "seq", split_axis=0, concat_axis=0, tiled=True)
     for c in range(len(near)):
         parts = [(0, rows, runs, pieces, c, att), (begin, rows, runs, pieces, c, dq)]
@@ -588,7 +588,8 @@
             [grads[:, :, 0] * HEAD_WIDTH ** (-0.5), grads[:, :, 1]], axis=1
         ).astype(jnp.bfloat16)
         grads = to_shards(
-            [lax.dynamic_index_in_dim(grads, member ^ k, 0, keepdims=False) for k in range(heads)]
+            [lax.dynamic_index_in_dim(grads, member ^ k, 0, keepdims=False) for k in range(heads)],
+            range(1, heads),
         )
         dk, dv = unpack(
             member.reshape(1),

time: 219 us -> 222 us (1.014)
  starting transfers between devices: 26.3 us -> 31.5 us
  waiting for transfers between devices: 152 us -> 148 us
  local copies, waits for them, and re-layouts: 1 us -> 4.1 us
    ppermute x7, starting transfers between devices: 11.3 us -> 15.1 us  [to_shards(): received[k] = lax.ppermute(results[k], 'seq', pairs)]
    unnamed x4 -> x12, local copies, waits for them, and re-layouts: 0.01 us -> 3.11 us
    all_to_all x2, waiting for transfers between devices: 87 us -> 84.1 us  [to_heads(): lax.all_to_all(packed, ('seq', 'head'), split_axis=0, concat_axis=0, tile...]
  transfers between devices with their start and end apart: 10 -> 10, of which waited for: 5 -> 5; matrix products, arithmetic and copies ran while one was open for 0% -> 0% of each run, Pallas kernels for 15% -> 14%
where the time goes in v8:
time: 222 us
  waiting for transfers between devices  148 us (67%)
  Pallas kernels  37.2 us (17%)
  starting transfers between devices  31.5 us (14%)
  local copies, waits for them, and re-layouts  4.1 us (2%)
    all_to_all x2, waiting for transfers between devices, to_heads(): lax.all_to_all(packed, ('seq', 'head'), split_axis=0, concat_axis=0, tile...  84.1 us
    ppermute x7, waiting for transfers between devices, to_shards(): received[k] = lax.ppermute(results[k], 'seq', pairs)  53.6 us
    pallas_call x2, Pallas kernels, attend(): pl.pallas_call(functools.partial(attention_kernel, total_blocks - 1, devi...  27.3 us
    ppermute x7, starting transfers between devices, to_shards(): received[k] = lax.ppermute(results[k], 'seq', pairs)  15.1 us
    all_to_all x2, starting transfers between devices, to_heads(): lax.all_to_all(packed, ('seq', 'head'), split_axis=0, concat_axis=0, tile...  11.4 us
    all_to_all x1, waiting for transfers between devices, per_device(): rest = lax.all_to_all(rest, 'seq', split_axis=0, concat_axis=0, tiled=True)  10.2 us
    pallas_call x2, Pallas kernels, pack(): pl.pallas_call(functools.partial(pack_kernel, heads, groups, tuple(((at,...  6.36 us
    all_to_all x1, starting transfers between devices, per_device(): rest = lax.all_to_all(rest, 'seq', split_axis=0, concat_axis=0, tiled=True)  5.07 us
  transfers between devices with their start and end apart: 10, of which 5 were waited for; matrix products, arithmetic and copies ran while one was open for 0% of the time, Pallas kernels for 14%

profile of v8, /device:TPU:0, one launch (start us, length us, event | category | flops | bytes accessed | tf_op | source)
XLA Modules:
  0.0 221.6 jit_solution(5958745754350465713)
XLA Ops:
  0.6 4.0 %shard_map.102 = bf16[8,4,400,128]{3,2,1,0:T(8,128)(2,1)} custom-call(s32[8,8,8]{2,1,0:T(8,128)} %refs_0_.2, s32[3,8,8]{2,1,0:T(8,128)} %bitcast.28, bf16[128,4096]{1,0:T(8,128)(2,1)} %refs_2_.1, bf16[128,4096]{1,0:T(8,128)(2,1)} %refs_3_.1, bf16[128,4096]{1,0:T(8,128)(2,1)} %refs_0_.3, bf16[128,4096]{1,0:T(8,128)(2,1)} %refs_1_.1), custom_call_target="tpu_custom_call" | custom-call | bytes 6553600 | tf_op jit(solution)/shard_map/pallas_call | solution.py:113
  4.7 7.3 %all-to-all-start = ((bf16[32,400,128]{2,1,0:T(8,128)(2,1)}), bf16[32,400,128]{2,1,0:T(8,128)(2,1)S(1)}, u32[]{:S(2)}, u32[]{:S(2)}) async-start(bf16[32,400,128]{2,1,0:T(8,128)(2,1)} %bitcast.24), calls=%async_computation | async-start | bytes 6553600 | tf_op jit(solution)/shard_map/all_to_all | solution.py:482
  12.0 0.0 copy-start.5
  12.0 2.3 %shard_map.103 = bf16[8,4,128,128]{3,2,1,0:T(8,128)(2,1)} custom-call(bf16[128,4096]{1,0:T(8,128)(2,1)} %refs_0_.3, bf16[128,4096]{1,0:T(8,128)(2,1)} %refs_1_.1), custom_call_target="tpu_custom_call" | custom-call | bytes 2097152 | tf_op jit(solution)/shard_map/pallas_call | solution.py:113
  14.4 71.9 %all-to-all-done = bf16[32,400,128]{2,1,0:T(8,128)(2,1)S(1)} async-done(((bf16[32,400,128]{2,1,0:T(8,128)(2,1)}), bf16[32,400,128]{2,1,0:T(8,128)(2,1)S(1)}, u32[]{:S(2)}, u32[]{:S(2)}) %all-to-all-start) | async-done | bytes 3276832 | tf_op jit(solution)/shard_map/all_to_all | solution.py:482
  86.2 4.1 %all-to-all-start.1 = ((bf16[32,128,128]{2,1,0:T(8,128)(2,1)}), bf16[32,128,128]{2,1,0:T(8,128)(2,1)}, u32[]{:S(2)}, u32[]{:S(2)}) async-start(bf16[32,128,128]{2,1,0:T(8,128)(2,1)} %bitcast.25), calls=%async_computation.1 | async-start | bytes 2097152 | tf_op jit(solution)/shard_map/all_to_all | solution.py:482
  90.4 0.1 reshape.76
  90.4 0.0 copy-done.5
  90.5 0.1 broadcast_in_dim.2
  90.6 0.1 copy.17
  90.6 0.1 min.12.ids_ref
  90.8 0.6 slice_bitcast_fusion.drop_ref
  91.4 13.9 %shard_map.104 = (bf16[512,128]{1,0:T(8,128)(2,1)}, bf16[512,128]{1,0:T(8,128)(2,1)}, bf16[512,128]{1,0:T(8,128)(2,1)}, bf16[512,128]{1,0:T(8,128)(2,1)}, bf16[5...) custom-call(s32[512]{0:T(512)S(1)} %min.12.ids_ref, ...), custom_call_target="tpu_custom_call" | custom-call | flops 17179869184 | bytes 10747904 | tf_op jit(solution)/shard_map/pallas_call | solution.py:423
  105.3 3.6 %collective-permute-start = (bf16[512,128]{1,0:T(8,128)(2,1)}, bf16[512,128]{1,0:T(8,128)(2,1)S(1)}, u32[]{:S(2)}, u32[]{:S(2)}) collective-permute-start(bf16[512,128]{1,0:T(8,128)(2,1)} %get-tuple-element.34), channel_id=1, source_target_pairs={{0,24},{4,28},{8,16},{12,20},{16,8},{20,12},{24,0},{28,4},{1,25},{... | collective-permute-start | bytes 393224 | tf_op jit(solution)/shard_map/ppermute | solution.py:495
  108.9 1.4 collective-permute-start.1
  110.3 12.3 %all-to-all-done.1 = bf16[32,128,128]{2,1,0:T(8,128)(2,1)} async-done(((bf16[32,128,128]{2,1,0:T(8,128)(2,1)}), bf16[32,128,128]{2,1,0:T(8,128)(2,1)}, u32[]{:S(2)}, u32[]{:S(2)}) %all-to-all-start.1) | async-done | bytes 1048608 | tf_op jit(solution)/shard_map/all_to_all | solution.py:482
  122.6 0.0 collective-permute-done.refs_2_
  122.6 0.0 collective-permute-done.1.refs_1_
  122.6 6.5 %collective-permute-start.2 = (bf16[512,128]{1,0:T(8,128)(2,1)}, bf16[512,128]{1,0:T(8,128)(2,1)S(1)}, u32[]{:S(2)}, u32[]{:S(2)}) collective-permute-start(bf16[512,128]{1,0:T(8,128)(2,1)} %get-tuple-element.45), channel_id=1, source_target_pairs={{0,16},{4,20},{8,24},{12,28},{16,0},{20,4},{24,8},{28,12},{1,17},{... | collective-permute-start | bytes 393224 | tf_op jit(solution)/shard_map/ppermute | solution.py:495
  129.1 0.0 collective-permute-start.3
  129.2 13.3 %shard_map.105 = bf16[8,1536,128]{2,1,0:T(8,128)(2,1)} custom-call(s32[512]{0:T(512)S(1)} %min.12.ids_ref, s32[512]{0:T(512)S(1)} %fusion.1.starts_ref, s32[1]{0:T(128)} %bitcast.5.first_ref, s32[1]{0:T(128)} %bitcast.6.member_ref, s32[64,8]{1,0:T(8,128)} %slice_bitcast_fusion.drop_ref, bf16[12800,128]{1,0:T(8,128)(2,1)S(1)} %bitcast.23, ...), custom_call_target="tpu_custom_call" | custom-call | flops 17179869184 | bytes 8519680 | tf_op jit(solution)/shard_map/pallas_call | solution.py:423
  142.5 0.0 copy-start
  142.5 0.0 collective-permute-done.2.refs_4_
  142.5 0.0 copy-start.1
  142.5 0.6 copy-done.1
  143.2 0.0 collective-permute-done.3.refs_3_
  143.2 0.0 copy-start.3
  143.2 0.7 copy-done.3
  143.8 5.1 %all-to-all-start.2 = ((bf16[8,1536,128]{2,1,0:T(8,128)(2,1)}), bf16[8,1536,128]{2,1,0:T(8,128)(2,1)S(1)}, u32[]{:S(2)}, u32[]{:S(2)}) async-start(bf16[8,1536,128]{2,1,0:T(8,128)(2,1)} %shard_map.105), calls=%async_computation.2 | async-start | bytes 6291456 | tf_op jit(solution)/shard_map/all_to_all | solution.py:574
  148.9 2.9 %collective-permute-start.4 = (bf16[512,128]{1,0:T(8,128)(2,1)}, bf16[512,128]{1,0:T(8,128)(2,1)S(1)}, u32[]{:S(2)}, u32[]{:S(2)}) collective-permute-start(bf16[512,128]{1,0:T(8,128)(2,1)} %get-tuple-element.55), channel_id=1, source_target_pairs={{0,12},{4,8},{8,4},{12,0},{16,28},{20,24},{24,20},{28,16},{1,13},{... | collective-permute-start | bytes 393224 | tf_op jit(solution)/shard_map/ppermute | solution.py:495
  151.8 0.6 collective-permute-start.5
  152.4 0.0 collective-permute-start.6
  152.4 52.2 %collective-permute-done.4.refs_5_ = bf16[512,128]{1,0:T(8,128)(2,1)S(1)} collective-permute-done((bf16[512,128]{1,0:T(8,128)(2,1)}, bf16[512,128]{1,0:T(8,128)(2,1)S(1)}, u32[]{:S(2)}, u32[]{:S(2)}) %collective-permute-start.4) | collective-permute-done | bytes 131104 | tf_op jit(solution)/shard_map/ppermute | solution.py:495
  204.6 1.4 collective-permute-done.5.refs_6_
  206.0 0.0 collective-permute-done.6.refs_7_
  206.0 0.0 copy-done
  206.0 0.0 copy-start.2
  206.0 0.9 copy-done.2
  206.9 0.0 copy-start.4
  206.9 0.9 copy-done.4
  207.8 1.3 shard_map.106
  209.1 10.2 %all-to-all-done.2.piece_ref = bf16[8,1536,128]{2,1,0:T(8,128)(2,1)S(1)} async-done(((bf16[8,1536,128]{2,1,0:T(8,128)(2,1)}), bf16[8,1536,128]{2,1,0:T(8,128)(2,1)S(1)}, u32[]{:S(2)}, u32[]{:S(2)}) %all-to-all-start.2) | async-done | bytes 3145760 | tf_op jit(solution)/shard_map/all_to_all | solution.py:574
  219.3 2.3 %shard_map.107 = (bf16[4,2,64,1024]{3,2,1,0:T(8,128)(2,1)}, bf16[4,2,64,1024]{3,2,1,0:T(8,128)(2,1)}, bf16[1,1,512,1024]{3,2,1,0:T(8,128)(2,1)}, bf16[1,1,512,1024]{3,2,1,0:T(8,128)(2,1)}) custom-call(bf16[8,1536,128]{2,1,0:T(8,128)(2,1)S(1)} %all-to-all-done.2.piece_ref, ...), custom_call_target="tpu_custom_call", output_to_operand_aliasing={{0}: (1, {}), {1}: (2, {})} | custom-call | bytes 6291456 | tf_op jit(solution)/shard_map/pallas_call | solution.py:201
  (9 shorter events, 0.1 us)
Async XLA Ops:
  4.7 81.6 %all-to-all-start = ((bf16[32,400,128]{2,1,0:T(8,128)(2,1)}), bf16[32,400,128]{2,1,0:T(8,128)(2,1)S(1)}, u32[]{:S(2)}, u32[]{:S(2)}) async-start(bf16[32,400,128]{2,1,0:T(8,128)(2,1)} %bitcast.24), calls=%async_computation | async-start | bytes 6553600 | tf_op jit(solution)/shard_map/all_to_all | solution.py:482
  12.0 78.5 %copy-start.5 = (s32[2]{0:T(128)S(1)}, s32[2]{0:T(128)}, u32[]{:S(2)}) copy-start(s32[2]{0:T(128)} %param.12) | copy-start | bytes 28
  86.2 36.4 %all-to-all-start.1 = ((bf16[32,128,128]{2,1,0:T(8,128)(2,1)}), bf16[32,128,128]{2,1,0:T(8,128)(2,1)}, u32[]{:S(2)}, u32[]{:S(2)}) async-start(bf16[32,128,128]{2,1,0:T(8,128)(2,1)} %bitcast.25), calls=%async_computation.1 | async-start | bytes 2097152 | tf_op jit(solution)/shard_map/all_to_all | solution.py:482
  105.3 17.3 %collective-permute-start = (bf16[512,128]{1,0:T(8,128)(2,1)}, bf16[512,128]{1,0:T(8,128)(2,1)S(1)}, u32[]{:S(2)}, u32[]{:S(2)}) collective-permute-start(bf16[512,128]{1,0:T(8,128)(2,1)} %get-tuple-element.34), channel_id=1, source_target_pairs={{0,24},{4,28},{8,16},{12,20},{16,8},{20,12},{24,0},{28,4},{1,25},{... | collective-permute-start | bytes 393224 | tf_op jit(solution)/shard_map/ppermute | solution.py:495
  108.9 13.7 %collective-permute-start.1 = (bf16[512,128]{1,0:T(8,128)(2,1)}, bf16[512,128]{1,0:T(8,128)(2,1)S(1)}, u32[]{:S(2)}, u32[]{:S(2)}) collective-permute-start(bf16[512,128]{1,0:T(8,128)(2,1)} %get-tuple-element.35), channel_id=1, source_target_pairs={{0,28},{4,24},{8,20},{12,16},{16,12},{20,8},{24,4},{28,0},{1,29},{... | collective-permute-start | bytes 393224 | tf_op jit(solution)/shard_map/ppermute | solution.py:495
  122.6 19.9 %collective-permute-start.2 = (bf16[512,128]{1,0:T(8,128)(2,1)}, bf16[512,128]{1,0:T(8,128)(2,1)S(1)}, u32[]{:S(2)}, u32[]{:S(2)}) collective-permute-start(bf16[512,128]{1,0:T(8,128)(2,1)} %get-tuple-element.45), channel_id=1, source_target_pairs={{0,16},{4,20},{8,24},{12,28},{16,0},{20,4},{24,8},{28,12},{1,17},{... | collective-permute-start | bytes 393224 | tf_op jit(solution)/shard_map/ppermute | solution.py:495
  129.1 14.0 %collective-permute-start.3 = (bf16[512,128]{1,0:T(8,128)(2,1)}, bf16[512,128]{1,0:T(8,128)(2,1)S(1)}, u32[]{:S(2)}, u32[]{:S(2)}) collective-permute-start(bf16[512,128]{1,0:T(8,128)(2,1)} %get-tuple-element.46), channel_id=1, source_target_pairs={{0,20},{4,16},{8,28},{12,24},{16,4},{20,0},{24,12},{28,8},{1,21},{... | collective-permute-start | bytes 393224 | tf_op jit(solution)/shard_map/ppermute | solution.py:495
  142.5 63.5 %copy-start = (bf16[512,128]{1,0:T(8,128)(2,1)S(1)}, bf16[512,128]{1,0:T(8,128)(2,1)}, u32[]{:S(2)}) copy-start(bf16[512,128]{1,0:T(8,128)(2,1)} %get-tuple-element.50.refs_0_) | copy-start | bytes 393220
  142.5 0.6 copy-start.1
  143.2 0.7 copy-start.3
  143.8 75.5 %all-to-all-start.2 = ((bf16[8,1536,128]{2,1,0:T(8,128)(2,1)}), bf16[8,1536,128]{2,1,0:T(8,128)(2,1)S(1)}, u32[]{:S(2)}, u32[]{:S(2)}) async-start(bf16[8,1536,128]{2,1,0:T(8,128)(2,1)} %shard_map.105), calls=%async_computation.2 | async-start | bytes 6291456 | tf_op jit(solution)/shard_map/all_to_all | solution.py:574
  148.9 55.7 %collective-permute-start.4 = (bf16[512,128]{1,0:T(8,128)(2,1)}, bf16[512,128]{1,0:T(8,128)(2,1)S(1)}, u32[]{:S(2)}, u32[]{:S(2)}) collective-permute-start(bf16[512,128]{1,0:T(8,128)(2,1)} %get-tuple-element.55), channel_id=1, source_target_pairs={{0,12},{4,8},{8,4},{12,0},{16,28},{20,24},{24,20},{28,16},{1,13},{... | collective-permute-start | bytes 393224 | tf_op jit(solution)/shard_map/ppermute | solution.py:495
  151.8 54.2 %collective-permute-start.5 = (bf16[512,128]{1,0:T(8,128)(2,1)}, bf16[512,128]{1,0:T(8,128)(2,1)S(1)}, u32[]{:S(2)}, u32[]{:S(2)}) collective-permute-start(bf16[512,128]{1,0:T(8,128)(2,1)} %get-tuple-element.56), channel_id=1, source_target_pairs={{0,8},{4,12},{8,0},{12,4},{16,24},{20,28},{24,16},{28,20},{1,9},{5... | collective-permute-start | bytes 393224 | tf_op jit(solution)/shard_map/ppermute | solution.py:495
  152.4 53.6 %collective-permute-start.6 = (bf16[512,128]{1,0:T(8,128)(2,1)}, bf16[512,128]{1,0:T(8,128)(2,1)S(1)}, u32[]{:S(2)}, u32[]{:S(2)}) collective-permute-start(bf16[512,128]{1,0:T(8,128)(2,1)} %get-tuple-element.57), channel_id=1, source_target_pairs={{0,4},{4,0},{8,12},{12,8},{16,20},{20,16},{24,28},{28,24},{1,5},{5... | collective-permute-start | bytes 393224 | tf_op jit(solution)/shard_map/ppermute | solution.py:495
  206.0 0.9 copy-start.2
  206.9 0.9 copy-start.4

commit v9 on v7

--- a/solution.py
+++ b/solution.py
@@ -14,7 +14,7 @@
 G = 2
 SLOTS = 3 + G + R
 WIDE = SLOTS * BLOCK_TOKENS
-UNROLL = 2
+UNROLL = 4
 STRIP = 16
 VMEM_LIMIT = 16 * 1024 * 1024
 VMEM_BYTES = 64 * 1024 * 1024
@@ -52,16 +52,16 @@
     count = len(sources)
     arrays, out_ref = refs[:count], refs[count]
     wholes, packed, in_sems, out_sems = refs[count + 1 : -3], refs[-3], refs[-2], refs[-1]
-    width = heads * HEAD_WIDTH
+    width = groups * heads * HEAD_WIDTH // 2
     loads = []
-    for g in range(groups):
+    for h in range(2):
         for n, (at, rows) in enumerate(sources):
-            columns = pl.ds(g * width, width)
+            columns = pl.ds(h * width, width)
             loads.append(
                 pltpu.make_async_copy(
                     arrays[n].at[pl.ds(at * rows, rows), columns],
                     wholes[n].at[:, columns],
-                    in_sems.at[g, n],
+                    in_sems.at[h, n],
                 )
             )
     for load in loads:
@@ -81,8 +81,9 @@
                 packed[m, g, pl.ds(begin, table_rows), :] = rounded
     stores = []
     for g in range(groups):
-        for n in range(count):
-            loads[g * count + n].wait()
+        if g % (groups // 2) == 0:
+            for n in range(count):
+                loads[g // (groups // 2) * count + n].wait()
         for m in range(heads):
             begin = 0
             for n, (_, rows) in enumerate(sources):
@@ -90,10 +91,10 @@
                     :, pl.ds((g * heads + m) * HEAD_WIDTH, HEAD_WIDTH)
                 ]
                 begin += rows
-            stores.append(
-                pltpu.make_async_copy(packed.at[m, g], out_ref.at[m, g], out_sems.at[g, m])
-            )
-            stores[-1].start()
+        stores.append(
+            pltpu.make_async_copy(packed.at[:, g], out_ref.at[:, g], out_sems.at[g])
+        )
+        stores[-1].start()
     for store in stores:
         store.wait()
 
@@ -105,8 +106,8 @@
         pltpu.VMEM((rows, groups * heads * HEAD_WIDTH), jnp.bfloat16) for _, _, rows in sources
     ] + [
         pltpu.VMEM(shape, jnp.bfloat16),
-        pltpu.SemaphoreType.DMA((groups, len(sources))),
-        pltpu.SemaphoreType.DMA((groups, heads)),
+        pltpu.SemaphoreType.DMA((2, len(sources))),
+        pltpu.SemaphoreType.DMA((groups,)),
     ]
     if table_rows:
         scratch.append(pltpu.VMEM((table_rows, HEAD_WIDTH), jnp.float32))

time: 219 us -> 218 us (level)
  Pallas kernels: 38.2 us -> 36 us
  transfers between devices with their start and end apart: 10 -> 10, of which waited for: 5 -> 5; matrix products, arithmetic and copies ran while one was open for 0% -> 0% of each run, Pallas kernels for 15% -> 14%
where the time goes in v9:
time: 218 us; the launch traced here: 217 us
  waiting for transfers between devices  153 us (70%)
  Pallas kernels  36 us (17%)
  starting transfers between devices  26.3 us (12%)
    all_to_all x2, waiting for transfers between devices, to_heads(): lax.all_to_all(packed, ('seq', 'head'), split_axis=0, concat_axis=0, tile...  88.2 us
    ppermute x7, waiting for transfers between devices, to_shards(): received[k] = lax.ppermute(results[k], 'seq', pairs)  53.7 us
    pallas_call x2, Pallas kernels, attend(): pl.pallas_call(functools.partial(attention_kernel, total_blocks - 1, devi...  25.3 us
    all_to_all x2, starting transfers between devices, to_heads(): lax.all_to_all(packed, ('seq', 'head'), split_axis=0, concat_axis=0, tile...  11.4 us
    ppermute x7, starting transfers between devices, to_shards(): received[k] = lax.ppermute(results[k], 'seq', pairs)  11.3 us
    all_to_all x1, waiting for transfers between devices, per_device(): rest = lax.all_to_all(rest, 'seq', split_axis=0, concat_axis=0, tiled=True)  11 us
    pallas_call x2, Pallas kernels, pack(): pl.pallas_call(functools.partial(pack_kernel, heads, groups, tuple(((at,...  6.16 us
  transfers between devices with their start and end apart: 10, of which 5 were waited for; matrix products, arithmetic and copies ran while one was open for 0% of the time, Pallas kernels for 14%

profile of v9, /device:TPU:0, one launch (start us, length us, event | category | flops | bytes accessed | tf_op | source)
XLA Modules:
  0.0 217.1 jit_solution(15907759086156767453)
XLA Ops:
  0.6 4.1 %shard_map.102 = bf16[8,4,400,128]{3,2,1,0:T(8,128)(2,1)} custom-call(s32[8,8,8]{2,1,0:T(8,128)} %refs_0_.2, s32[3,8,8]{2,1,0:T(8,128)} %bitcast.28, bf16[128,4096]{1,0:T(8,128)(2,1)} %refs_2_.1, bf16[128,4096]{1,0:T(8,128)(2,1)} %refs_3_.1, bf16[128,4096]{1,0:T(8,128)(2,1)} %refs_0_.3, bf16[128,4096]{1,0:T(8,128)(2,1)} %refs_1_.1), custom_call_target="tpu_custom_call" | custom-call | bytes 6553600 | tf_op jit(solution)/shard_map/pallas_call | solution.py:114
  4.7 7.3 %all-to-all-start = ((bf16[32,400,128]{2,1,0:T(8,128)(2,1)}), bf16[32,400,128]{2,1,0:T(8,128)(2,1)S(1)}, u32[]{:S(2)}, u32[]{:S(2)}) async-start(bf16[32,400,128]{2,1,0:T(8,128)(2,1)} %bitcast.24), calls=%async_computation | async-start | bytes 6553600 | tf_op jit(solution)/shard_map/all_to_all | solution.py:482
  12.0 0.0 copy-start.1
  12.0 2.1 shard_map.103
  14.2 72.1 %all-to-all-done = bf16[32,400,128]{2,1,0:T(8,128)(2,1)S(1)} async-done(((bf16[32,400,128]{2,1,0:T(8,128)(2,1)}), bf16[32,400,128]{2,1,0:T(8,128)(2,1)S(1)}, u32[]{:S(2)}, u32[]{:S(2)}) %all-to-all-start) | async-done | bytes 3276832 | tf_op jit(solution)/shard_map/all_to_all | solution.py:482
  86.3 4.1 %all-to-all-start.1 = ((bf16[32,128,128]{2,1,0:T(8,128)(2,1)}), bf16[32,128,128]{2,1,0:T(8,128)(2,1)}, u32[]{:S(2)}, u32[]{:S(2)}) async-start(bf16[32,128,128]{2,1,0:T(8,128)(2,1)} %bitcast.25), calls=%async_computation.1 | async-start | bytes 2097152 | tf_op jit(solution)/shard_map/all_to_all | solution.py:482
  90.4 0.1 reshape.76
  90.5 0.0 copy-done.1
  90.5 0.1 broadcast_in_dim.2
  90.6 0.1 copy.17
  90.7 0.1 min.12.ids_ref
  90.8 0.6 slice_bitcast_fusion.drop_ref
  91.4 13.0 %shard_map.104 = (bf16[512,128]{1,0:T(8,128)(2,1)}, bf16[512,128]{1,0:T(8,128)(2,1)}, bf16[512,128]{1,0:T(8,128)(2,1)}, bf16[512,128]{1,0:T(8,128)(2,1)}, bf16[5...) custom-call(s32[512]{0:T(512)S(1)} %min.12.ids_ref, ...), custom_call_target="tpu_custom_call" | custom-call | flops 17179869184 | bytes 10747904 | tf_op jit(solution)/shard_map/pallas_call | solution.py:424
  104.4 2.7 %collective-permute-start = (bf16[512,128]{1,0:T(8,128)(2,1)}, bf16[512,128]{1,0:T(8,128)(2,1)S(1)}, u32[]{:S(2)}, u32[]{:S(2)}) collective-permute-start(bf16[512,128]{1,0:T(8,128)(2,1)} %get-tuple-element.25), channel_id=1, source_target_pairs={{0,16},{4,20},{8,24},{12,28},{16,0},{20,4},{24,8},{28,12},{1,17},{... | collective-permute-start | bytes 393224 | tf_op jit(solution)/shard_map/ppermute | solution.py:495
  107.1 1.5 collective-permute-start.1
  108.5 3.3 %collective-permute-start.2 = (bf16[512,128]{1,0:T(8,128)(2,1)}, bf16[512,128]{1,0:T(8,128)(2,1)}, u32[]{:S(2)}, u32[]{:S(2)}) collective-permute-start(bf16[512,128]{1,0:T(8,128)(2,1)} %get-tuple-element.27), channel_id=1, source_target_pairs={{0,24},{4,28},{8,16},{12,20},{16,8},{20,12},{24,0},{28,4},{1,25},{... | collective-permute-start | bytes 393224 | tf_op jit(solution)/shard_map/ppermute | solution.py:495
  111.9 0.2 collective-permute-start.3
  112.1 16.2 %all-to-all-done.1 = bf16[32,128,128]{2,1,0:T(8,128)(2,1)} async-done(((bf16[32,128,128]{2,1,0:T(8,128)(2,1)}), bf16[32,128,128]{2,1,0:T(8,128)(2,1)}, u32[]{:S(2)}, u32[]{:S(2)}) %all-to-all-start.1) | async-done | bytes 1048608 | tf_op jit(solution)/shard_map/all_to_all | solution.py:482
  128.3 12.3 %shard_map.105 = bf16[8,1536,128]{2,1,0:T(8,128)(2,1)} custom-call(s32[512]{0:T(512)S(1)} %min.12.ids_ref, s32[512]{0:T(512)S(1)} %fusion.1.starts_ref, s32[1]{0:T(128)} %bitcast.5.first_ref, s32[1]{0:T(128)} %bitcast.6.member_ref, s32[64,8]{1,0:T(8,128)} %slice_bitcast_fusion.drop_ref, bf16[12800,128]{1,0:T(8,128)(2,1)S(1)} %bitcast.23, ...), custom_call_target="tpu_custom_call" | custom-call | flops 17179869184 | bytes 8519680 | tf_op jit(solution)/shard_map/pallas_call | solution.py:424
  140.6 0.0 copy-start
  140.6 0.0 collective-permute-done.refs_4_
  140.6 0.0 collective-permute-done.1.refs_3_
  140.6 0.0 collective-permute-done.2.refs_2_
  140.7 0.0 collective-permute-done.3.refs_1_
  140.7 3.7 %all-to-all-start.2 = ((bf16[8,1536,128]{2,1,0:T(8,128)(2,1)}), bf16[8,1536,128]{2,1,0:T(8,128)(2,1)S(1)}, u32[]{:S(2)}, u32[]{:S(2)}) async-start(bf16[8,1536,128]{2,1,0:T(8,128)(2,1)} %shard_map.105), calls=%async_computation.2 | async-start | bytes 6291456 | tf_op jit(solution)/shard_map/all_to_all | solution.py:575
  144.3 2.8 %collective-permute-start.4 = (bf16[512,128]{1,0:T(8,128)(2,1)}, bf16[512,128]{1,0:T(8,128)(2,1)S(1)}, u32[]{:S(2)}, u32[]{:S(2)}) collective-permute-start(bf16[512,128]{1,0:T(8,128)(2,1)} %get-tuple-element.35), channel_id=1, source_target_pairs={{0,12},{4,8},{8,4},{12,0},{16,28},{20,24},{24,20},{28,16},{1,13},{... | collective-permute-start | bytes 393224 | tf_op jit(solution)/shard_map/ppermute | solution.py:495
  147.2 0.5 collective-permute-start.5
  147.7 0.2 collective-permute-start.6
  147.9 52.2 %collective-permute-done.4.refs_5_ = bf16[512,128]{1,0:T(8,128)(2,1)S(1)} collective-permute-done((bf16[512,128]{1,0:T(8,128)(2,1)}, bf16[512,128]{1,0:T(8,128)(2,1)S(1)}, u32[]{:S(2)}, u32[]{:S(2)}) %collective-permute-start.4) | collective-permute-done | bytes 131104 | tf_op jit(solution)/shard_map/ppermute | solution.py:495
  200.1 1.5 collective-permute-done.5.refs_6_
  201.6 0.0 collective-permute-done.6.refs_7_
  201.6 0.0 copy-done
  201.6 2.2 %shard_map.106 = (bf16[4,2,64,1024]{3,2,1,0:T(8,128)(2,1)}, bf16[4,2,64,1024]{3,2,1,0:T(8,128)(2,1)}) custom-call(s32[1]{0:T(128)} %bitcast.6.member_ref, bf16[512,128]{1,0:T(8,128)(2,1)S(1)} %copy-done, bf16[512,128]{1,0:T(8,128)(2,1)} %collective-permute-done.3.refs_1_, bf16[512,128]{1,0:T(8,128)(2,1)} %collective-permute-done.2.refs_2_, ...), custom_call_target="tpu_custom_call" | custom-call | bytes 2097152 | tf_op jit(solution)/shard_map/pallas_call | solution.py:157
  203.8 11.0 %all-to-all-done.2.piece_ref = bf16[8,1536,128]{2,1,0:T(8,128)(2,1)S(1)} async-done(((bf16[8,1536,128]{2,1,0:T(8,128)(2,1)}), bf16[8,1536,128]{2,1,0:T(8,128)(2,1)S(1)}, u32[]{:S(2)}, u32[]{:S(2)}) %all-to-all-start.2) | async-done | bytes 3145760 | tf_op jit(solution)/shard_map/all_to_all | solution.py:575
  214.8 2.3 %shard_map.107 = (bf16[4,2,64,1024]{3,2,1,0:T(8,128)(2,1)}, bf16[4,2,64,1024]{3,2,1,0:T(8,128)(2,1)}, bf16[1,1,512,1024]{3,2,1,0:T(8,128)(2,1)}, bf16[1,1,512,1024]{3,2,1,0:T(8,128)(2,1)}) custom-call(bf16[8,1536,128]{2,1,0:T(8,128)(2,1)S(1)} %all-to-all-done.2.piece_ref, ...), custom_call_target="tpu_custom_call", output_to_operand_aliasing={{0}: (1, {}), {1}: (2, {})} | custom-call | bytes 6291456 | tf_op jit(solution)/shard_map/pallas_call | solution.py:202
  (9 shorter events, 0.1 us)
Async XLA Ops:
  4.7 81.6 %all-to-all-start = ((bf16[32,400,128]{2,1,0:T(8,128)(2,1)}), bf16[32,400,128]{2,1,0:T(8,128)(2,1)S(1)}, u32[]{:S(2)}, u32[]{:S(2)}) async-start(bf16[32,400,128]{2,1,0:T(8,128)(2,1)} %bitcast.24), calls=%async_computation | async-start | bytes 6553600 | tf_op jit(solution)/shard_map/all_to_all | solution.py:482
  12.0 78.5 %copy-start.1 = (s32[2]{0:T(128)S(1)}, s32[2]{0:T(128)}, u32[]{:S(2)}) copy-start(s32[2]{0:T(128)} %param.12) | copy-start | bytes 28
  86.3 42.0 %all-to-all-start.1 = ((bf16[32,128,128]{2,1,0:T(8,128)(2,1)}), bf16[32,128,128]{2,1,0:T(8,128)(2,1)}, u32[]{:S(2)}, u32[]{:S(2)}) async-start(bf16[32,128,128]{2,1,0:T(8,128)(2,1)} %bitcast.25), calls=%async_computation.1 | async-start | bytes 2097152 | tf_op jit(solution)/shard_map/all_to_all | solution.py:482
  104.4 36.2 %collective-permute-start = (bf16[512,128]{1,0:T(8,128)(2,1)}, bf16[512,128]{1,0:T(8,128)(2,1)S(1)}, u32[]{:S(2)}, u32[]{:S(2)}) collective-permute-start(bf16[512,128]{1,0:T(8,128)(2,1)} %get-tuple-element.25), channel_id=1, source_target_pairs={{0,16},{4,20},{8,24},{12,28},{16,0},{20,4},{24,8},{28,12},{1,17},{... | collective-permute-start | bytes 393224 | tf_op jit(solution)/shard_map/ppermute | solution.py:495
  107.1 33.6 %collective-permute-start.1 = (bf16[512,128]{1,0:T(8,128)(2,1)}, bf16[512,128]{1,0:T(8,128)(2,1)S(1)}, u32[]{:S(2)}, u32[]{:S(2)}) collective-permute-start(bf16[512,128]{1,0:T(8,128)(2,1)} %get-tuple-element.26), channel_id=1, source_target_pairs={{0,20},{4,16},{8,28},{12,24},{16,4},{20,0},{24,12},{28,8},{1,21},{... | collective-permute-start | bytes 393224 | tf_op jit(solution)/shard_map/ppermute | solution.py:495
  108.5 32.1 %collective-permute-start.2 = (bf16[512,128]{1,0:T(8,128)(2,1)}, bf16[512,128]{1,0:T(8,128)(2,1)}, u32[]{:S(2)}, u32[]{:S(2)}) collective-permute-start(bf16[512,128]{1,0:T(8,128)(2,1)} %get-tuple-element.27), channel_id=1, source_target_pairs={{0,24},{4,28},{8,16},{12,20},{16,8},{20,12},{24,0},{28,4},{1,25},{... | collective-permute-start | bytes 393224 | tf_op jit(solution)/shard_map/ppermute | solution.py:495
  111.9 28.8 %collective-permute-start.3 = (bf16[512,128]{1,0:T(8,128)(2,1)}, bf16[512,128]{1,0:T(8,128)(2,1)}, u32[]{:S(2)}, u32[]{:S(2)}) collective-permute-start(bf16[512,128]{1,0:T(8,128)(2,1)} %get-tuple-element.28), channel_id=1, source_target_pairs={{0,28},{4,24},{8,20},{12,16},{16,12},{20,8},{24,4},{28,0},{1,29},{... | collective-permute-start | bytes 393224 | tf_op jit(solution)/shard_map/ppermute | solution.py:495
  140.6 61.0 %copy-start = (bf16[512,128]{1,0:T(8,128)(2,1)S(1)}, bf16[512,128]{1,0:T(8,128)(2,1)}, u32[]{:S(2)}) copy-start(bf16[512,128]{1,0:T(8,128)(2,1)} %get-tuple-element.30.refs_0_) | copy-start | bytes 393220
  140.7 74.1 %all-to-all-start.2 = ((bf16[8,1536,128]{2,1,0:T(8,128)(2,1)}), bf16[8,1536,128]{2,1,0:T(8,128)(2,1)S(1)}, u32[]{:S(2)}, u32[]{:S(2)}) async-start(bf16[8,1536,128]{2,1,0:T(8,128)(2,1)} %shard_map.105), calls=%async_computation.2 | async-start | bytes 6291456 | tf_op jit(solution)/shard_map/all_to_all | solution.py:575
  144.3 55.8 %collective-permute-start.4 = (bf16[512,128]{1,0:T(8,128)(2,1)}, bf16[512,128]{1,0:T(8,128)(2,1)S(1)}, u32[]{:S(2)}, u32[]{:S(2)}) collective-permute-start(bf16[512,128]{1,0:T(8,128)(2,1)} %get-tuple-element.35), channel_id=1, source_target_pairs={{0,12},{4,8},{8,4},{12,0},{16,28},{20,24},{24,20},{28,16},{1,13},{... | collective-permute-start | bytes 393224 | tf_op jit(solution)/shard_map/ppermute | solution.py:495
  147.2 54.4 %collective-permute-start.5 = (bf16[512,128]{1,0:T(8,128)(2,1)}, bf16[512,128]{1,0:T(8,128)(2,1)S(1)}, u32[]{:S(2)}, u32[]{:S(2)}) collective-permute-start(bf16[512,128]{1,0:T(8,128)(2,1)} %get-tuple-element.36), channel_id=1, source_target_pairs={{0,8},{4,12},{8,0},{12,4},{16,24},{20,28},{24,16},{28,20},{1,9},{5... | collective-permute-start | bytes 393224 | tf_op jit(solution)/shard_map/ppermute | solution.py:495
  147.7 53.9 %collective-permute-start.6 = (bf16[512,128]{1,0:T(8,128)(2,1)}, bf16[512,128]{1,0:T(8,128)(2,1)S(1)}, u32[]{:S(2)}, u32[]{:S(2)}) collective-permute-start(bf16[512,128]{1,0:T(8,128)(2,1)} %get-tuple-element.37), channel_id=1, source_target_pairs={{0,4},{4,0},{8,12},{12,8},{16,20},{20,16},{24,28},{28,24},{1,5},{5... | collective-permute-start | bytes 393224 | tf_op jit(solution)/shard_map/ppermute | solution.py:495

commit v10 on v9

--- a/solution.py
+++ b/solution.py
@@ -48,7 +48,9 @@
 def pack_kernel(heads, groups, sources, table_rows, *refs):
     refs = list(refs)
     if table_rows:
-        drop_ref, rand_ref, table = refs.pop(0), refs.pop(0), refs.pop()
+        drop_hbm, rand_hbm = refs.pop(0), refs.pop(0)
+        table, drop_ref, rand_ref, table_sems = refs[-4:]
+        refs = refs[:-4]
     count = len(sources)
     arrays, out_ref = refs[:count], refs[count]
     wholes, packed, in_sems, out_sems = refs[count + 1 : -3], refs[-3], refs[-2], refs[-1]
@@ -68,6 +70,14 @@
         load.start()
     begin = sum(rows for _, rows in sources)
     if table_rows:
+        fetches = [
+            pltpu.make_async_copy(drop_hbm, drop_ref, table_sems.at[0]),
+            pltpu.make_async_copy(rand_hbm, rand_ref, table_sems.at[1]),
+        ]
+        for fetch in fetches:
+            fetch.start()
+        for fetch in fetches:
+            fetch.wait()
         blocks = drop_ref.shape[1]
         table[...] = jnp.zeros_like(table)
         for m in range(heads):
@@ -111,12 +121,14 @@
     ]
     if table_rows:
         scratch.append(pltpu.VMEM((table_rows, HEAD_WIDTH), jnp.float32))
+        scratch += [pltpu.VMEM(t.shape, t.dtype) for t in tables]
+        scratch.append(pltpu.SemaphoreType.DMA((len(tables),)))
     packed = pl.pallas_call(
         functools.partial(
             pack_kernel, heads, groups, tuple((at, rows) for _, at, rows in sources), table_rows
         ),
         out_shape=pltpu.HBM(shape, jnp.bfloat16),
-        in_specs=[vmem] * len(tables) + [anywhere] * len(sources),
+        in_specs=[anywhere] * (len(tables) + len(sources)),
         out_specs=anywhere,
         scratch_shapes=scratch,
         compiler_params=pltpu.CompilerParams(vmem_limit_bytes=VMEM_LIMIT),
@@ -168,47 +180,44 @@
     )(member, received[0], *received[:0:-1], *olds)
 
 
-def unpack_all_kernel(begins, step_heads, piece_ref, *refs):
-    outs = refs[len(refs) - len(begins) :]
-    for begin, out in zip(begins, outs):
-        runs, _, rows, _ = out.shape
-        for m in range(step_heads):
-            for i in range(runs):
-                out[i, 0, :, pl.ds(m * HEAD_WIDTH, HEAD_WIDTH)] = piece_ref[
+def unpack_all_kernel(parts, piece_ref, *refs):
+    sems = refs[-1]
+    stages = refs[-1 - len(parts) : -1]
+    outs = refs[-1 - 2 * len(parts) : -1 - len(parts)]
+    stores = []
+    for (begin, rows, runs, _, piece), stage, out in zip(parts, stages, outs):
+        for i in range(runs):
+            for m in range(piece_ref.shape[0]):
+                stage[i, :, pl.ds(m * HEAD_WIDTH, HEAD_WIDTH)] = piece_ref[
                     m, pl.ds(begin + i * rows, rows), :
                 ]
+            stores.append(
+                pltpu.make_async_copy(stage.at[i], out.at[i, piece], sems.at[len(stores)])
+            )
+            stores[-1].start()
+    for store in stores:
+        store.wait()
 
 
 def unpack_all(received, parts):
-    heads, total, _ = received.shape
-    step_heads = 2 if heads % 2 == 0 else 1
-    width = step_heads * HEAD_WIDTH
-    shapes, out_specs, begins, olds, aliases = [], [], [], [], {}
-    size = 0
-    for n, (begin, rows, runs, pieces, piece, old) in enumerate(parts):
-        begins.append(begin)
-        shapes.append(
-            jax.ShapeDtypeStruct((runs, pieces, rows, heads * HEAD_WIDTH), jnp.bfloat16)
-        )
-        out_specs.append(
-            pl.BlockSpec(
-                (runs, 1, rows, width), functools.partial(lambda piece, h: (0, piece, 0, h), piece)
-            )
-        )
-        size += rows * runs * heads * HEAD_WIDTH
+    heads = received.shape[0]
+    shapes, stages, olds, aliases, count = [], [], [], {}, 0
+    for n, (_, rows, runs, pieces, _, old) in enumerate(parts):
+        shapes.append(pltpu.HBM((runs, pieces, rows, heads * HEAD_WIDTH), jnp.bfloat16))
+        stages.append(pltpu.VMEM((runs, rows, heads * HEAD_WIDTH), jnp.bfloat16))
+        count += runs
         if old is not None:
             aliases[1 + len(olds)] = n
             olds.append(old)
     return pl.pallas_call(
-        functools.partial(unpack_all_kernel, begins, step_heads),
-        grid=(heads // step_heads,),
+        functools.partial(unpack_all_kernel, tuple(part[:-1] for part in parts)),
         out_shape=shapes,
-        in_specs=[pl.BlockSpec((step_heads, total, HEAD_WIDTH), lambda h: (h, 0, 0))]
-        + [pl.BlockSpec(memory_space=pl.ANY)] * len(olds),
-        out_specs=out_specs,
+        in_specs=[vmem] + [anywhere] * len(olds),
+        out_specs=[anywhere] * len(shapes),
         input_output_aliases=aliases,
+        scratch_shapes=stages + [pltpu.SemaphoreType.DMA((count,))],
         compiler_params=pltpu.CompilerParams(vmem_limit_bytes=VMEM_LIMIT),
-        cost_estimate=copy_cost(size),
+        cost_estimate=copy_cost(received.size),
     )(in_vmem(received), *olds)
 
 
@@ -579,7 +588,9 @@
     if whole:
         c = pieces - 1
         parts = [(0, rows, runs, pieces, c, att), (begin, rows, runs, pieces, c, dq)]
-        grads = [(2 * begin + n * shard_tokens, shard_tokens, 1, 1, 0, None) for n in range(2)]
+        grads = [
+            (2 * begin + n * shard_tokens, shard_tokens // runs, runs, 1, 0, None) for n in range(2)
+        ]
         att, dq, dk, dv = unpack_all(rest, parts + grads)
     else:
         grads = lax.psum_scatter(

time: 218 us -> 217 us (level)
  no operation moved by 1% of the time
where the time goes in v10:
time: 217 us; the launch traced here: 216 us
  waiting for transfers between devices  153 us (71%)
  Pallas kernels  35.3 us (16%)
  starting transfers between devices  26.3 us (12%)
    all_to_all x2, waiting for transfers between devices, to_heads(): lax.all_to_all(packed, ('seq', 'head'), split_axis=0, concat_axis=0, tile...  88.2 us
    ppermute x7, waiting for transfers between devices, to_shards(): received[k] = lax.ppermute(results[k], 'seq', pairs)  53.7 us
    pallas_call x2, Pallas kernels, attend(): pl.pallas_call(functools.partial(attention_kernel, total_blocks - 1, devi...  25.4 us
    all_to_all x2, starting transfers between devices, to_heads(): lax.all_to_all(packed, ('seq', 'head'), split_axis=0, concat_axis=0, tile...  11.4 us
    ppermute x7, starting transfers between devices, to_shards(): received[k] = lax.ppermute(results[k], 'seq', pairs)  11.3 us
    all_to_all x1, waiting for transfers between devices, per_device(): rest = lax.all_to_all(rest, 'seq', split_axis=0, concat_axis=0, tiled=True)  11 us
    pallas_call x2, Pallas kernels, pack(): pl.pallas_call(functools.partial(pack_kernel, heads, groups, tuple(((at,...  5.89 us
  transfers between devices with their start and end apart: 10, of which 5 were waited for; matrix products, arithmetic and copies ran while one was open for 0% of the time, Pallas kernels for 14%

profile of v10, /device:TPU:0, one launch (start us, length us, event | category | flops | bytes accessed | tf_op | source)
XLA Modules:
  0.0 216.4 jit_solution(1582617958653863098)
XLA Ops:
  0.6 3.8 %shard_map.102 = bf16[8,4,400,128]{3,2,1,0:T(8,128)(2,1)} custom-call(s32[8,8,8]{2,1,0:T(8,128)} %refs_0_.2, s32[3,8,8]{2,1,0:T(8,128)} %bitcast.28, bf16[128,4096]{1,0:T(8,128)(2,1)} %refs_2_.1, bf16[128,4096]{1,0:T(8,128)(2,1)} %refs_3_.1, bf16[128,4096]{1,0:T(8,128)(2,1)} %refs_0_.3, bf16[128,4096]{1,0:T(8,128)(2,1)} %refs_1_.1), custom_call_target="tpu_custom_call" | custom-call | bytes 6553600 | tf_op jit(solution)/shard_map/pallas_call | solution.py:126
  4.4 7.3 %all-to-all-start = ((bf16[32,400,128]{2,1,0:T(8,128)(2,1)}), bf16[32,400,128]{2,1,0:T(8,128)(2,1)S(1)}, u32[]{:S(2)}, u32[]{:S(2)}) async-start(bf16[32,400,128]{2,1,0:T(8,128)(2,1)} %bitcast.24), calls=%async_computation | async-start | bytes 6553600 | tf_op jit(solution)/shard_map/all_to_all | solution.py:491
  11.7 0.0 copy-start.1
  11.7 2.1 shard_map.103
  13.9 72.1 %all-to-all-done = bf16[32,400,128]{2,1,0:T(8,128)(2,1)S(1)} async-done(((bf16[32,400,128]{2,1,0:T(8,128)(2,1)}), bf16[32,400,128]{2,1,0:T(8,128)(2,1)S(1)}, u32[]{:S(2)}, u32[]{:S(2)}) %all-to-all-start) | async-done | bytes 3276832 | tf_op jit(solution)/shard_map/all_to_all | solution.py:491
  86.0 4.1 %all-to-all-start.1 = ((bf16[32,128,128]{2,1,0:T(8,128)(2,1)}), bf16[32,128,128]{2,1,0:T(8,128)(2,1)}, u32[]{:S(2)}, u32[]{:S(2)}) async-start(bf16[32,128,128]{2,1,0:T(8,128)(2,1)} %bitcast.25), calls=%async_computation.1 | async-start | bytes 2097152 | tf_op jit(solution)/shard_map/all_to_all | solution.py:491
  90.1 0.1 reshape.76
  90.2 0.0 copy-done.1
  90.2 0.1 broadcast_in_dim.2
  90.3 0.1 copy.17
  90.4 0.1 min.12.ids_ref
  90.5 0.6 slice_bitcast_fusion.drop_ref
  91.1 13.0 %shard_map.104 = (bf16[512,128]{1,0:T(8,128)(2,1)}, bf16[512,128]{1,0:T(8,128)(2,1)}, bf16[512,128]{1,0:T(8,128)(2,1)}, bf16[512,128]{1,0:T(8,128)(2,1)}, bf16[5...) custom-call(s32[512]{0:T(512)S(1)} %min.12.ids_ref, ...), custom_call_target="tpu_custom_call" | custom-call | flops 17179869184 | bytes 10747904 | tf_op jit(solution)/shard_map/pallas_call | solution.py:433
  104.1 2.7 %collective-permute-start = (bf16[512,128]{1,0:T(8,128)(2,1)}, bf16[512,128]{1,0:T(8,128)(2,1)S(1)}, u32[]{:S(2)}, u32[]{:S(2)}) collective-permute-start(bf16[512,128]{1,0:T(8,128)(2,1)} %get-tuple-element.25), channel_id=1, source_target_pairs={{0,16},{4,20},{8,24},{12,28},{16,0},{20,4},{24,8},{28,12},{1,17},{... | collective-permute-start | bytes 393224 | tf_op jit(solution)/shard_map/ppermute | solution.py:504
  106.8 1.5 collective-permute-start.1
  108.3 3.3 %collective-permute-start.2 = (bf16[512,128]{1,0:T(8,128)(2,1)}, bf16[512,128]{1,0:T(8,128)(2,1)}, u32[]{:S(2)}, u32[]{:S(2)}) collective-permute-start(bf16[512,128]{1,0:T(8,128)(2,1)} %get-tuple-element.27), channel_id=1, source_target_pairs={{0,24},{4,28},{8,16},{12,20},{16,8},{20,12},{24,0},{28,4},{1,25},{... | collective-permute-start | bytes 393224 | tf_op jit(solution)/shard_map/ppermute | solution.py:504
  111.6 0.2 collective-permute-start.3
  111.9 16.1 %all-to-all-done.1 = bf16[32,128,128]{2,1,0:T(8,128)(2,1)} async-done(((bf16[32,128,128]{2,1,0:T(8,128)(2,1)}), bf16[32,128,128]{2,1,0:T(8,128)(2,1)}, u32[]{:S(2)}, u32[]{:S(2)}) %all-to-all-start.1) | async-done | bytes 1048608 | tf_op jit(solution)/shard_map/all_to_all | solution.py:491
  128.0 12.4 %shard_map.105 = bf16[8,1536,128]{2,1,0:T(8,128)(2,1)} custom-call(s32[512]{0:T(512)S(1)} %min.12.ids_ref, s32[512]{0:T(512)S(1)} %fusion.1.starts_ref, s32[1]{0:T(128)} %bitcast.5.first_ref, s32[1]{0:T(128)} %bitcast.6.member_ref, s32[64,8]{1,0:T(8,128)} %slice_bitcast_fusion.drop_ref, bf16[12800,128]{1,0:T(8,128)(2,1)S(1)} %bitcast.23, ...), custom_call_target="tpu_custom_call" | custom-call | flops 17179869184 | bytes 8519680 | tf_op jit(solution)/shard_map/pallas_call | solution.py:433
  140.4 0.0 copy-start
  140.4 0.0 collective-permute-done.refs_4_
  140.4 0.0 collective-permute-done.1.refs_3_
  140.4 0.0 collective-permute-done.2.refs_2_
  140.4 0.0 collective-permute-done.3.refs_1_
  140.4 3.7 %all-to-all-start.2 = ((bf16[8,1536,128]{2,1,0:T(8,128)(2,1)}), bf16[8,1536,128]{2,1,0:T(8,128)(2,1)S(1)}, u32[]{:S(2)}, u32[]{:S(2)}) async-start(bf16[8,1536,128]{2,1,0:T(8,128)(2,1)} %shard_map.105), calls=%async_computation.2 | async-start | bytes 6291456 | tf_op jit(solution)/shard_map/all_to_all | solution.py:584
  144.1 2.8 %collective-permute-start.4 = (bf16[512,128]{1,0:T(8,128)(2,1)}, bf16[512,128]{1,0:T(8,128)(2,1)S(1)}, u32[]{:S(2)}, u32[]{:S(2)}) collective-permute-start(bf16[512,128]{1,0:T(8,128)(2,1)} %get-tuple-element.35), channel_id=1, source_target_pairs={{0,12},{4,8},{8,4},{12,0},{16,28},{20,24},{24,20},{28,16},{1,13},{... | collective-permute-start | bytes 393224 | tf_op jit(solution)/shard_map/ppermute | solution.py:504
  146.9 0.5 collective-permute-start.5
  147.5 0.2 collective-permute-start.6
  147.6 52.2 %collective-permute-done.4.refs_5_ = bf16[512,128]{1,0:T(8,128)(2,1)S(1)} collective-permute-done((bf16[512,128]{1,0:T(8,128)(2,1)}, bf16[512,128]{1,0:T(8,128)(2,1)S(1)}, u32[]{:S(2)}, u32[]{:S(2)}) %collective-permute-start.4) | collective-permute-done | bytes 131104 | tf_op jit(solution)/shard_map/ppermute | solution.py:504
  199.9 1.5 collective-permute-done.5.refs_6_
  201.3 0.0 collective-permute-done.6.refs_7_
  201.3 0.0 copy-done
  201.3 2.2 %shard_map.106 = (bf16[4,2,64,1024]{3,2,1,0:T(8,128)(2,1)}, bf16[4,2,64,1024]{3,2,1,0:T(8,128)(2,1)}) custom-call(s32[1]{0:T(128)} %bitcast.6.member_ref, bf16[512,128]{1,0:T(8,128)(2,1)S(1)} %copy-done, bf16[512,128]{1,0:T(8,128)(2,1)} %collective-permute-done.3.refs_1_, bf16[512,128]{1,0:T(8,128)(2,1)} %collective-permute-done.2.refs_2_, ...), custom_call_target="tpu_custom_call" | custom-call | bytes 2097152 | tf_op jit(solution)/shard_map/pallas_call | solution.py:169
  203.6 11.0 %all-to-all-done.2.piece_ref = bf16[8,1536,128]{2,1,0:T(8,128)(2,1)S(1)} async-done(((bf16[8,1536,128]{2,1,0:T(8,128)(2,1)}), bf16[8,1536,128]{2,1,0:T(8,128)(2,1)S(1)}, u32[]{:S(2)}, u32[]{:S(2)}) %all-to-all-start.2) | async-done | bytes 3145760 | tf_op jit(solution)/shard_map/all_to_all | solution.py:584
  214.6 1.8 shard_map.107
  (9 shorter events, 0.1 us)
Async XLA Ops:
  4.4 81.6 %all-to-all-start = ((bf16[32,400,128]{2,1,0:T(8,128)(2,1)}), bf16[32,400,128]{2,1,0:T(8,128)(2,1)S(1)}, u32[]{:S(2)}, u32[]{:S(2)}) async-start(bf16[32,400,128]{2,1,0:T(8,128)(2,1)} %bitcast.24), calls=%async_computation | async-start | bytes 6553600 | tf_op jit(solution)/shard_map/all_to_all | solution.py:491
  11.7 78.5 %copy-start.1 = (s32[2]{0:T(128)S(1)}, s32[2]{0:T(128)}, u32[]{:S(2)}) copy-start(s32[2]{0:T(128)} %param.12) | copy-start | bytes 28
  86.0 42.0 %all-to-all-start.1 = ((bf16[32,128,128]{2,1,0:T(8,128)(2,1)}), bf16[32,128,128]{2,1,0:T(8,128)(2,1)}, u32[]{:S(2)}, u32[]{:S(2)}) async-start(bf16[32,128,128]{2,1,0:T(8,128)(2,1)} %bitcast.25), calls=%async_computation.1 | async-start | bytes 2097152 | tf_op jit(solution)/shard_map/all_to_all | solution.py:491
  104.1 36.2 %collective-permute-start = (bf16[512,128]{1,0:T(8,128)(2,1)}, bf16[512,128]{1,0:T(8,128)(2,1)S(1)}, u32[]{:S(2)}, u32[]{:S(2)}) collective-permute-start(bf16[512,128]{1,0:T(8,128)(2,1)} %get-tuple-element.25), channel_id=1, source_target_pairs={{0,16},{4,20},{8,24},{12,28},{16,0},{20,4},{24,8},{28,12},{1,17},{... | collective-permute-start | bytes 393224 | tf_op jit(solution)/shard_map/ppermute | solution.py:504
  106.8 33.6 %collective-permute-start.1 = (bf16[512,128]{1,0:T(8,128)(2,1)}, bf16[512,128]{1,0:T(8,128)(2,1)S(1)}, u32[]{:S(2)}, u32[]{:S(2)}) collective-permute-start(bf16[512,128]{1,0:T(8,128)(2,1)} %get-tuple-element.26), channel_id=1, source_target_pairs={{0,20},{4,16},{8,28},{12,24},{16,4},{20,0},{24,12},{28,8},{1,21},{... | collective-permute-start | bytes 393224 | tf_op jit(solution)/shard_map/ppermute | solution.py:504
  108.3 32.1 %collective-permute-start.2 = (bf16[512,128]{1,0:T(8,128)(2,1)}, bf16[512,128]{1,0:T(8,128)(2,1)}, u32[]{:S(2)}, u32[]{:S(2)}) collective-permute-start(bf16[512,128]{1,0:T(8,128)(2,1)} %get-tuple-element.27), channel_id=1, source_target_pairs={{0,24},{4,28},{8,16},{12,20},{16,8},{20,12},{24,0},{28,4},{1,25},{... | collective-permute-start | bytes 393224 | tf_op jit(solution)/shard_map/ppermute | solution.py:504
  111.6 28.8 %collective-permute-start.3 = (bf16[512,128]{1,0:T(8,128)(2,1)}, bf16[512,128]{1,0:T(8,128)(2,1)}, u32[]{:S(2)}, u32[]{:S(2)}) collective-permute-start(bf16[512,128]{1,0:T(8,128)(2,1)} %get-tuple-element.28), channel_id=1, source_target_pairs={{0,28},{4,24},{8,20},{12,16},{16,12},{20,8},{24,4},{28,0},{1,29},{... | collective-permute-start | bytes 393224 | tf_op jit(solution)/shard_map/ppermute | solution.py:504
  140.4 61.0 %copy-start = (bf16[512,128]{1,0:T(8,128)(2,1)S(1)}, bf16[512,128]{1,0:T(8,128)(2,1)}, u32[]{:S(2)}) copy-start(bf16[512,128]{1,0:T(8,128)(2,1)} %get-tuple-element.30.refs_0_) | copy-start | bytes 393220
  140.4 74.2 %all-to-all-start.2 = ((bf16[8,1536,128]{2,1,0:T(8,128)(2,1)}), bf16[8,1536,128]{2,1,0:T(8,128)(2,1)S(1)}, u32[]{:S(2)}, u32[]{:S(2)}) async-start(bf16[8,1536,128]{2,1,0:T(8,128)(2,1)} %shard_map.105), calls=%async_computation.2 | async-start | bytes 6291456 | tf_op jit(solution)/shard_map/all_to_all | solution.py:584
  144.1 55.8 %collective-permute-start.4 = (bf16[512,128]{1,0:T(8,128)(2,1)}, bf16[512,128]{1,0:T(8,128)(2,1)S(1)}, u32[]{:S(2)}, u32[]{:S(2)}) collective-permute-start(bf16[512,128]{1,0:T(8,128)(2,1)} %get-tuple-element.35), channel_id=1, source_target_pairs={{0,12},{4,8},{8,4},{12,0},{16,28},{20,24},{24,20},{28,16},{1,13},{... | collective-permute-start | bytes 393224 | tf_op jit(solution)/shard_map/ppermute | solution.py:504
  146.9 54.4 %collective-permute-start.5 = (bf16[512,128]{1,0:T(8,128)(2,1)}, bf16[512,128]{1,0:T(8,128)(2,1)S(1)}, u32[]{:S(2)}, u32[]{:S(2)}) collective-permute-start(bf16[512,128]{1,0:T(8,128)(2,1)} %get-tuple-element.36), channel_id=1, source_target_pairs={{0,8},{4,12},{8,0},{12,4},{16,24},{20,28},{24,16},{28,20},{1,9},{5... | collective-permute-start | bytes 393224 | tf_op jit(solution)/shard_map/ppermute | solution.py:504
  147.5 53.9 %collective-permute-start.6 = (bf16[512,128]{1,0:T(8,128)(2,1)}, bf16[512,128]{1,0:T(8,128)(2,1)S(1)}, u32[]{:S(2)}, u32[]{:S(2)}) collective-permute-start(bf16[512,128]{1,0:T(8,128)(2,1)} %get-tuple-element.37), channel_id=1, source_target_pairs={{0,4},{4,0},{8,12},{12,8},{16,20},{20,16},{24,28},{28,24},{1,5},{5... | collective-permute-start | bytes 393224 | tf_op jit(solution)/shard_map/ppermute | solution.py:504

commit v11 on v10

--- a/solution.py
+++ b/solution.py
@@ -14,7 +14,7 @@
 G = 2
 SLOTS = 3 + G + R
 WIDE = SLOTS * BLOCK_TOKENS
-UNROLL = 4
+UNROLL = 8
 STRIP = 16
 VMEM_LIMIT = 16 * 1024 * 1024
 VMEM_BYTES = 64 * 1024 * 1024
@@ -54,9 +54,9 @@
     count = len(sources)
     arrays, out_ref = refs[:count], refs[count]
     wholes, packed, in_sems, out_sems = refs[count + 1 : -3], refs[-3], refs[-2], refs[-1]
-    width = groups * heads * HEAD_WIDTH // 2
+    width = heads * HEAD_WIDTH
     loads = []
-    for h in range(2):
+    for h in range(groups):
         for n, (at, rows) in enumerate(sources):
             columns = pl.ds(h * width, width)
             loads.append(
@@ -91,9 +91,8 @@
                 packed[m, g, pl.ds(begin, table_rows), :] = rounded
     stores = []
     for g in range(groups):
-        if g % (groups // 2) == 0:
-            for n in range(count):
-                loads[g // (groups // 2) * count + n].wait()
+        for n in range(count):
+            loads[g * count + n].wait()
         for m in range(heads):
             begin = 0
             for n, (_, rows) in enumerate(sources):
@@ -116,7 +115,7 @@
         pltpu.VMEM((rows, groups * heads * HEAD_WIDTH), jnp.bfloat16) for _, _, rows in sources
     ] + [
         pltpu.VMEM(shape, jnp.bfloat16),
-        pltpu.SemaphoreType.DMA((2, len(sources))),
+        pltpu.SemaphoreType.DMA((groups, len(sources))),
         pltpu.SemaphoreType.DMA((groups,)),
     ]
     if table_rows:

time: 217 us -> 217 us (level)
  transfers between devices with their start and end apart: 10 -> 10, of which waited for: 5 -> 5; matrix products, arithmetic and copies ran while one was open for 0% -> 0% of each run, Pallas kernels for 14% -> 13%
where the time goes in v11:
time: 217 us; the launch traced here: 216 us
  waiting for transfers between devices  153 us (71%)
  Pallas kernels  34.6 us (16%)
  starting transfers between devices  26.3 us (12%)
    all_to_all x2, waiting for transfers between devices, to_heads(): lax.all_to_all(packed, ('seq', 'head'), split_axis=0, concat_axis=0, tile...  88.5 us
    ppermute x7, waiting for transfers between devices, to_shards(): received[k] = lax.ppermute(results[k], 'seq', pairs)  53.7 us
    pallas_call x2, Pallas kernels, attend(): pl.pallas_call(functools.partial(attention_kernel, total_blocks - 1, devi...  24.6 us
    all_to_all x2, starting transfers between devices, to_heads(): lax.all_to_all(packed, ('seq', 'head'), split_axis=0, concat_axis=0, tile...  11.4 us
    ppermute x7, starting transfers between devices, to_shards(): received[k] = lax.ppermute(results[k], 'seq', pairs)  11.3 us
    all_to_all x1, waiting for transfers between devices, per_device(): rest = lax.all_to_all(rest, 'seq', split_axis=0, concat_axis=0, tiled=True)  11 us
    pallas_call x2, Pallas kernels, pack(): pl.pallas_call(functools.partial(pack_kernel, heads, groups, tuple(((at,...  6 us
  transfers between devices with their start and end apart: 10, of which 5 were waited for; matrix products, arithmetic and copies ran while one was open for 0% of the time, Pallas kernels for 13%

profile of v11, /device:TPU:0, one launch (start us, length us, event | category | flops | bytes accessed | tf_op | source)
XLA Modules:
  0.0 216.0 jit_solution(2483983780291836542)
XLA Ops:
  0.6 3.9 %shard_map.102 = bf16[8,4,400,128]{3,2,1,0:T(8,128)(2,1)} custom-call(s32[8,8,8]{2,1,0:T(8,128)} %refs_0_.2, s32[3,8,8]{2,1,0:T(8,128)} %bitcast.28, bf16[128,4096]{1,0:T(8,128)(2,1)} %refs_2_.1, bf16[128,4096]{1,0:T(8,128)(2,1)} %refs_3_.1, bf16[128,4096]{1,0:T(8,128)(2,1)} %refs_0_.3, bf16[128,4096]{1,0:T(8,128)(2,1)} %refs_1_.1), custom_call_target="tpu_custom_call" | custom-call | bytes 6553600 | tf_op jit(solution)/shard_map/pallas_call | solution.py:125
  4.5 7.3 %all-to-all-start = ((bf16[32,400,128]{2,1,0:T(8,128)(2,1)}), bf16[32,400,128]{2,1,0:T(8,128)(2,1)S(1)}, u32[]{:S(2)}, u32[]{:S(2)}) async-start(bf16[32,400,128]{2,1,0:T(8,128)(2,1)} %bitcast.24), calls=%async_computation | async-start | bytes 6553600 | tf_op jit(solution)/shard_map/all_to_all | solution.py:490
  11.8 0.0 copy-start.1
  11.8 2.1 shard_map.103
  14.0 72.1 %all-to-all-done = bf16[32,400,128]{2,1,0:T(8,128)(2,1)S(1)} async-done(((bf16[32,400,128]{2,1,0:T(8,128)(2,1)}), bf16[32,400,128]{2,1,0:T(8,128)(2,1)S(1)}, u32[]{:S(2)}, u32[]{:S(2)}) %all-to-all-start) | async-done | bytes 3276832 | tf_op jit(solution)/shard_map/all_to_all | solution.py:490
  86.1 4.1 %all-to-all-start.1 = ((bf16[32,128,128]{2,1,0:T(8,128)(2,1)}), bf16[32,128,128]{2,1,0:T(8,128)(2,1)}, u32[]{:S(2)}, u32[]{:S(2)}) async-start(bf16[32,128,128]{2,1,0:T(8,128)(2,1)} %bitcast.25), calls=%async_computation.1 | async-start | bytes 2097152 | tf_op jit(solution)/shard_map/all_to_all | solution.py:490
  90.2 0.1 reshape.76
  90.3 0.0 copy-done.1
  90.3 0.1 broadcast_in_dim.2
  90.4 0.1 copy.17
  90.5 0.1 min.12.ids_ref
  90.6 0.6 slice_bitcast_fusion.drop_ref
  91.2 12.6 %shard_map.104 = (bf16[512,128]{1,0:T(8,128)(2,1)}, bf16[512,128]{1,0:T(8,128)(2,1)}, bf16[512,128]{1,0:T(8,128)(2,1)}, bf16[512,128]{1,0:T(8,128)(2,1)}, bf16[5...) custom-call(s32[512]{0:T(512)S(1)} %min.12.ids_ref, ...), custom_call_target="tpu_custom_call" | custom-call | flops 17179869184 | bytes 10747904 | tf_op jit(solution)/shard_map/pallas_call | solution.py:432
  103.9 2.7 %collective-permute-start = (bf16[512,128]{1,0:T(8,128)(2,1)}, bf16[512,128]{1,0:T(8,128)(2,1)S(1)}, u32[]{:S(2)}, u32[]{:S(2)}) collective-permute-start(bf16[512,128]{1,0:T(8,128)(2,1)} %get-tuple-element.25), channel_id=1, source_target_pairs={{0,16},{4,20},{8,24},{12,28},{16,0},{20,4},{24,8},{28,12},{1,17},{... | collective-permute-start | bytes 393224 | tf_op jit(solution)/shard_map/ppermute | solution.py:503
  106.5 1.5 collective-permute-start.1
  108.0 3.3 %collective-permute-start.2 = (bf16[512,128]{1,0:T(8,128)(2,1)}, bf16[512,128]{1,0:T(8,128)(2,1)}, u32[]{:S(2)}, u32[]{:S(2)}) collective-permute-start(bf16[512,128]{1,0:T(8,128)(2,1)} %get-tuple-element.27), channel_id=1, source_target_pairs={{0,24},{4,28},{8,16},{12,20},{16,8},{20,12},{24,0},{28,4},{1,25},{... | collective-permute-start | bytes 393224 | tf_op jit(solution)/shard_map/ppermute | solution.py:503
  111.3 0.3 collective-permute-start.3
  111.6 16.5 %all-to-all-done.1 = bf16[32,128,128]{2,1,0:T(8,128)(2,1)} async-done(((bf16[32,128,128]{2,1,0:T(8,128)(2,1)}), bf16[32,128,128]{2,1,0:T(8,128)(2,1)}, u32[]{:S(2)}, u32[]{:S(2)}) %all-to-all-start.1) | async-done | bytes 1048608 | tf_op jit(solution)/shard_map/all_to_all | solution.py:490
  128.1 11.9 %shard_map.105 = bf16[8,1536,128]{2,1,0:T(8,128)(2,1)} custom-call(s32[512]{0:T(512)S(1)} %min.12.ids_ref, s32[512]{0:T(512)S(1)} %fusion.1.starts_ref, s32[1]{0:T(128)} %bitcast.5.first_ref, s32[1]{0:T(128)} %bitcast.6.member_ref, s32[64,8]{1,0:T(8,128)} %slice_bitcast_fusion.drop_ref, bf16[12800,128]{1,0:T(8,128)(2,1)S(1)} %bitcast.23, ...), custom_call_target="tpu_custom_call" | custom-call | flops 17179869184 | bytes 8519680 | tf_op jit(solution)/shard_map/pallas_call | solution.py:432
  140.0 0.0 copy-start
  140.0 0.0 collective-permute-done.refs_4_
  140.0 0.0 collective-permute-done.1.refs_3_
  140.0 0.0 collective-permute-done.2.refs_2_
  140.1 0.0 collective-permute-done.3.refs_1_
  140.1 3.7 %all-to-all-start.2 = ((bf16[8,1536,128]{2,1,0:T(8,128)(2,1)}), bf16[8,1536,128]{2,1,0:T(8,128)(2,1)S(1)}, u32[]{:S(2)}, u32[]{:S(2)}) async-start(bf16[8,1536,128]{2,1,0:T(8,128)(2,1)} %shard_map.105), calls=%async_computation.2 | async-start | bytes 6291456 | tf_op jit(solution)/shard_map/all_to_all | solution.py:583
  143.7 2.8 %collective-permute-start.4 = (bf16[512,128]{1,0:T(8,128)(2,1)}, bf16[512,128]{1,0:T(8,128)(2,1)S(1)}, u32[]{:S(2)}, u32[]{:S(2)}) collective-permute-start(bf16[512,128]{1,0:T(8,128)(2,1)} %get-tuple-element.35), channel_id=1, source_target_pairs={{0,12},{4,8},{8,4},{12,0},{16,28},{20,24},{24,20},{28,16},{1,13},{... | collective-permute-start | bytes 393224 | tf_op jit(solution)/shard_map/ppermute | solution.py:503
  146.6 0.5 collective-permute-start.5
  147.1 0.2 collective-permute-start.6
  147.3 52.2 %collective-permute-done.4.refs_5_ = bf16[512,128]{1,0:T(8,128)(2,1)S(1)} collective-permute-done((bf16[512,128]{1,0:T(8,128)(2,1)}, bf16[512,128]{1,0:T(8,128)(2,1)S(1)}, u32[]{:S(2)}, u32[]{:S(2)}) %collective-permute-start.4) | collective-permute-done | bytes 131104 | tf_op jit(solution)/shard_map/ppermute | solution.py:503
  199.5 1.5 collective-permute-done.5.refs_6_
  201.0 0.0 collective-permute-done.6.refs_7_
  201.0 0.0 copy-done
  201.0 2.2 %shard_map.106 = (bf16[4,2,64,1024]{3,2,1,0:T(8,128)(2,1)}, bf16[4,2,64,1024]{3,2,1,0:T(8,128)(2,1)}) custom-call(s32[1]{0:T(128)} %bitcast.6.member_ref, bf16[512,128]{1,0:T(8,128)(2,1)S(1)} %copy-done, bf16[512,128]{1,0:T(8,128)(2,1)} %collective-permute-done.3.refs_1_, bf16[512,128]{1,0:T(8,128)(2,1)} %collective-permute-done.2.refs_2_, ...), custom_call_target="tpu_custom_call" | custom-call | bytes 2097152 | tf_op jit(solution)/shard_map/pallas_call | solution.py:168
  203.2 11.0 %all-to-all-done.2.piece_ref = bf16[8,1536,128]{2,1,0:T(8,128)(2,1)S(1)} async-done(((bf16[8,1536,128]{2,1,0:T(8,128)(2,1)}), bf16[8,1536,128]{2,1,0:T(8,128)(2,1)S(1)}, u32[]{:S(2)}, u32[]{:S(2)}) %all-to-all-start.2) | async-done | bytes 3145760 | tf_op jit(solution)/shard_map/all_to_all | solution.py:583
  214.2 1.8 shard_map.107
  (9 shorter events, 0.1 us)
Async XLA Ops:
  4.5 81.6 %all-to-all-start = ((bf16[32,400,128]{2,1,0:T(8,128)(2,1)}), bf16[32,400,128]{2,1,0:T(8,128)(2,1)S(1)}, u32[]{:S(2)}, u32[]{:S(2)}) async-start(bf16[32,400,128]{2,1,0:T(8,128)(2,1)} %bitcast.24), calls=%async_computation | async-start | bytes 6553600 | tf_op jit(solution)/shard_map/all_to_all | solution.py:490
  11.8 78.5 %copy-start.1 = (s32[2]{0:T(128)S(1)}, s32[2]{0:T(128)}, u32[]{:S(2)}) copy-start(s32[2]{0:T(128)} %param.12) | copy-start | bytes 28
  86.1 42.0 %all-to-all-start.1 = ((bf16[32,128,128]{2,1,0:T(8,128)(2,1)}), bf16[32,128,128]{2,1,0:T(8,128)(2,1)}, u32[]{:S(2)}, u32[]{:S(2)}) async-start(bf16[32,128,128]{2,1,0:T(8,128)(2,1)} %bitcast.25), calls=%async_computation.1 | async-start | bytes 2097152 | tf_op jit(solution)/shard_map/all_to_all | solution.py:490
  103.9 36.2 %collective-permute-start = (bf16[512,128]{1,0:T(8,128)(2,1)}, bf16[512,128]{1,0:T(8,128)(2,1)S(1)}, u32[]{:S(2)}, u32[]{:S(2)}) collective-permute-start(bf16[512,128]{1,0:T(8,128)(2,1)} %get-tuple-element.25), channel_id=1, source_target_pairs={{0,16},{4,20},{8,24},{12,28},{16,0},{20,4},{24,8},{28,12},{1,17},{... | collective-permute-start | bytes 393224 | tf_op jit(solution)/shard_map/ppermute | solution.py:503
  106.5 33.5 %collective-permute-start.1 = (bf16[512,128]{1,0:T(8,128)(2,1)}, bf16[512,128]{1,0:T(8,128)(2,1)S(1)}, u32[]{:S(2)}, u32[]{:S(2)}) collective-permute-start(bf16[512,128]{1,0:T(8,128)(2,1)} %get-tuple-element.26), channel_id=1, source_target_pairs={{0,20},{4,16},{8,28},{12,24},{16,4},{20,0},{24,12},{28,8},{1,21},{... | collective-permute-start | bytes 393224 | tf_op jit(solution)/shard_map/ppermute | solution.py:503
  108.0 32.1 %collective-permute-start.2 = (bf16[512,128]{1,0:T(8,128)(2,1)}, bf16[512,128]{1,0:T(8,128)(2,1)}, u32[]{:S(2)}, u32[]{:S(2)}) collective-permute-start(bf16[512,128]{1,0:T(8,128)(2,1)} %get-tuple-element.27), channel_id=1, source_target_pairs={{0,24},{4,28},{8,16},{12,20},{16,8},{20,12},{24,0},{28,4},{1,25},{... | collective-permute-start | bytes 393224 | tf_op jit(solution)/shard_map/ppermute | solution.py:503
  111.3 28.7 %collective-permute-start.3 = (bf16[512,128]{1,0:T(8,128)(2,1)}, bf16[512,128]{1,0:T(8,128)(2,1)}, u32[]{:S(2)}, u32[]{:S(2)}) collective-permute-start(bf16[512,128]{1,0:T(8,128)(2,1)} %get-tuple-element.28), channel_id=1, source_target_pairs={{0,28},{4,24},{8,20},{12,16},{16,12},{20,8},{24,4},{28,0},{1,29},{... | collective-permute-start | bytes 393224 | tf_op jit(solution)/shard_map/ppermute | solution.py:503
  140.0 61.0 %copy-start = (bf16[512,128]{1,0:T(8,128)(2,1)S(1)}, bf16[512,128]{1,0:T(8,128)(2,1)}, u32[]{:S(2)}) copy-start(bf16[512,128]{1,0:T(8,128)(2,1)} %get-tuple-element.30.refs_0_) | copy-start | bytes 393220
  140.1 74.1 %all-to-all-start.2 = ((bf16[8,1536,128]{2,1,0:T(8,128)(2,1)}), bf16[8,1536,128]{2,1,0:T(8,128)(2,1)S(1)}, u32[]{:S(2)}, u32[]{:S(2)}) async-start(bf16[8,1536,128]{2,1,0:T(8,128)(2,1)} %shard_map.105), calls=%async_computation.2 | async-start | bytes 6291456 | tf_op jit(solution)/shard_map/all_to_all | solution.py:583
  143.7 55.8 %collective-permute-start.4 = (bf16[512,128]{1,0:T(8,128)(2,1)}, bf16[512,128]{1,0:T(8,128)(2,1)S(1)}, u32[]{:S(2)}, u32[]{:S(2)}) collective-permute-start(bf16[512,128]{1,0:T(8,128)(2,1)} %get-tuple-element.35), channel_id=1, source_target_pairs={{0,12},{4,8},{8,4},{12,0},{16,28},{20,24},{24,20},{28,16},{1,13},{... | collective-permute-start | bytes 393224 | tf_op jit(solution)/shard_map/ppermute | solution.py:503
  146.6 54.4 %collective-permute-start.5 = (bf16[512,128]{1,0:T(8,128)(2,1)}, bf16[512,128]{1,0:T(8,128)(2,1)S(1)}, u32[]{:S(2)}, u32[]{:S(2)}) collective-permute-start(bf16[512,128]{1,0:T(8,128)(2,1)} %get-tuple-element.36), channel_id=1, source_target_pairs={{0,8},{4,12},{8,0},{12,4},{16,24},{20,28},{24,16},{28,20},{1,9},{5... | collective-permute-start | bytes 393224 | tf_op jit(solution)/shard_map/ppermute | solution.py:503
  147.1 53.9 %collective-permute-start.6 = (bf16[512,128]{1,0:T(8,128)(2,1)}, bf16[512,128]{1,0:T(8,128)(2,1)S(1)}, u32[]{:S(2)}, u32[]{:S(2)}) collective-permute-start(bf16[512,128]{1,0:T(8,128)(2,1)} %get-tuple-element.37), channel_id=1, source_target_pairs={{0,4},{4,0},{8,12},{12,8},{16,20},{20,16},{24,28},{28,24},{1,5},{5... | collective-permute-start | bytes 393224 | tf_op jit(solution)/shard_map/ppermute | solution.py:503

commit v12 on v11

--- a/solution.py
+++ b/solution.py
@@ -249,7 +249,7 @@
     sums_ref = None if joined else refs.pop(0)
     acc, retain, waiting, near, sems = refs[:5]
     done = refs[5] if joined else None
-    earlier, start_sem = refs[-2:] if has_start else (None, None)
+    start_sems = refs[-1] if has_start else None
     scale = HEAD_WIDTH ** (-0.5)
     steps = targets * (out_rows // BLOCK_TOKENS)
     slot_of_lane = lax.broadcasted_iota(jnp.int32, (SLOTS, WIDE), 1) // BLOCK_TOKENS
@@ -258,10 +258,16 @@
     retain[...] = jnp.dot(
         drop_ref[...].astype(jnp.float32), expand, preferred_element_type=jnp.float32
     ) * (1.0 / keep_prob)
-    acc[...] = jnp.zeros_like(acc)
+    shares = [pl.ds(n * (acc.shape[0] // targets), acc.shape[0] // targets) for n in range(targets)]
+    fetches = []
     if has_start:
-        fetch = pltpu.make_async_copy(start_ref, earlier, start_sem)
-        fetch.start()
+        for n, share in enumerate(shares):
+            fetches.append(
+                pltpu.make_async_copy(start_ref.at[share, :], acc.at[share, :], start_sems.at[n])
+            )
+            fetches[-1].start()
+    else:
+        acc[...] = jnp.zeros_like(acc)
     lane = lax.broadcasted_iota(jnp.int32, (1, WIDE), 1)
     nt = (((1,), (1,)), ((), ()))
     tn = (((0,), (0,)), ((), ()))
@@ -351,19 +357,16 @@
 
     for u in range(UNROLL):
         factor(u, u, *score(u))
+    for fetch in fetches:
+        fetch.wait()
     lax.fori_loop(1, steps // UNROLL, step, 0)
     for u in range(UNROLL):
         finish(steps - UNROLL + u, u)
-    if has_start:
-        fetch.wait()
     if joined:
         rows = acc.shape[0] // targets
         stores = []
-        for target in range(targets):
-            part = pl.ds(target * rows, rows)
-            sums = acc[part, :]
-            if has_start:
-                sums += earlier[part, :]
+        for target, share in enumerate(shares):
+            sums = acc[share, :]
             done[target, pl.ds(0, 2 * out_rows), :] = near[target]
             done[target, pl.ds(2 * out_rows, rows), :] = (sums[:, :HEAD_WIDTH] * scale).astype(
                 jnp.bfloat16
@@ -378,12 +381,9 @@
         for store in stores:
             store.wait()
     else:
-        rows = acc.shape[0] // targets
         stores = [
-            pltpu.make_async_copy(
-                acc.at[pl.ds(n * rows, rows), :], sums_ref.at[pl.ds(n * rows, rows), :], sems.at[n]
-            )
-            for n in range(targets)
+            pltpu.make_async_copy(acc.at[share, :], sums_ref.at[share, :], sems.at[n])
+            for n, share in enumerate(shares)
         ]
         for store in stores:
             store.start()
@@ -422,11 +422,11 @@
     if joined:
         scratch.append(pltpu.VMEM(out_shape[0].shape, jnp.bfloat16))
     sums_bytes = 8 * length * HEAD_WIDTH
-    limit = VMEM_LIMIT + 2 * (kv.size + source.size) + (1 if start is None else 2) * sums_bytes
+    limit = VMEM_LIMIT + 2 * (kv.size + source.size) + sums_bytes
     keep = in_vmem if 2 * limit < VMEM_BYTES else lambda t: t
     flat = [keep(t.reshape(-1, HEAD_WIDTH)) for t in (kv, qd) if t is not None]
     if start is not None:
-        scratch += [pltpu.VMEM(accumulator, jnp.float32), pltpu.SemaphoreType.DMA]
+        scratch.append(pltpu.SemaphoreType.DMA((targets,)))
     operands = flat + ([] if start is None else [in_hbm(start)])
     operand_specs = [vmem] * len(flat) + [anywhere] * (start is not None)
     return pl.pallas_call(

time: 217 us -> 218 us (level)
  transfers between devices with their start and end apart: 10 -> 10, of which waited for: 5 -> 5; matrix products, arithmetic and copies ran while one was open for 0% -> 0% of each run, Pallas kernels for 13% -> 14%
where the time goes in v12:
time: 218 us
  waiting for transfers between devices  153 us (70%)
  Pallas kernels  36.2 us (17%)
  starting transfers between devices  26.3 us (12%)
    all_to_all x2, waiting for transfers between devices, to_heads(): lax.all_to_all(packed, ('seq', 'head'), split_axis=0, concat_axis=0, tile...  88.6 us
    ppermute x7, waiting for transfers between devices, to_shards(): received[k] = lax.ppermute(results[k], 'seq', pairs)  53.7 us
    pallas_call x2, Pallas kernels, attend(): pl.pallas_call(functools.partial(attention_kernel, total_blocks - 1, devi...  26.1 us
    all_to_all x2, starting transfers between devices, to_heads(): lax.all_to_all(packed, ('seq', 'head'), split_axis=0, concat_axis=0, tile...  11.4 us
    ppermute x7, starting transfers between devices, to_shards(): received[k] = lax.ppermute(results[k], 'seq', pairs)  11.3 us
    all_to_all x1, waiting for transfers between devices, per_device(): rest = lax.all_to_all(rest, 'seq', split_axis=0, concat_axis=0, tiled=True)  11 us
    pallas_call x2, Pallas kernels, pack(): pl.pallas_call(functools.partial(pack_kernel, heads, groups, tuple(((at,...  6 us
  transfers between devices with their start and end apart: 10, of which 5 were waited for; matrix products, arithmetic and copies ran while one was open for 0% of the time, Pallas kernels for 14%

profile of v12, /device:TPU:0, one launch (start us, length us, event | category | flops | bytes accessed | tf_op | source)
XLA Modules:
  0.0 217.6 jit_solution(17746880358356910649)
XLA Ops:
  0.6 3.9 %shard_map.102 = bf16[8,4,400,128]{3,2,1,0:T(8,128)(2,1)} custom-call(s32[8,8,8]{2,1,0:T(8,128)} %refs_0_.2, s32[3,8,8]{2,1,0:T(8,128)} %bitcast.28, bf16[128,4096]{1,0:T(8,128)(2,1)} %refs_2_.1, bf16[128,4096]{1,0:T(8,128)(2,1)} %refs_3_.1, bf16[128,4096]{1,0:T(8,128)(2,1)} %refs_0_.3, bf16[128,4096]{1,0:T(8,128)(2,1)} %refs_1_.1), custom_call_target="tpu_custom_call" | custom-call | bytes 6553600 | tf_op jit(solution)/shard_map/pallas_call | solution.py:125
  4.5 7.3 %all-to-all-start = ((bf16[32,400,128]{2,1,0:T(8,128)(2,1)}), bf16[32,400,128]{2,1,0:T(8,128)(2,1)S(1)}, u32[]{:S(2)}, u32[]{:S(2)}) async-start(bf16[32,400,128]{2,1,0:T(8,128)(2,1)} %bitcast.24), calls=%async_computation | async-start | bytes 6553600 | tf_op jit(solution)/shard_map/all_to_all | solution.py:490
  11.8 0.0 copy-start.1
  11.8 2.1 shard_map.103
  14.0 72.1 %all-to-all-done = bf16[32,400,128]{2,1,0:T(8,128)(2,1)S(1)} async-done(((bf16[32,400,128]{2,1,0:T(8,128)(2,1)}), bf16[32,400,128]{2,1,0:T(8,128)(2,1)S(1)}, u32[]{:S(2)}, u32[]{:S(2)}) %all-to-all-start) | async-done | bytes 3276832 | tf_op jit(solution)/shard_map/all_to_all | solution.py:490
  86.1 4.1 %all-to-all-start.1 = ((bf16[32,128,128]{2,1,0:T(8,128)(2,1)}), bf16[32,128,128]{2,1,0:T(8,128)(2,1)}, u32[]{:S(2)}, u32[]{:S(2)}) async-start(bf16[32,128,128]{2,1,0:T(8,128)(2,1)} %bitcast.25), calls=%async_computation.1 | async-start | bytes 2097152 | tf_op jit(solution)/shard_map/all_to_all | solution.py:490
  90.2 0.1 reshape.76
  90.3 0.0 copy-done.1
  90.3 0.1 broadcast_in_dim.2
  90.4 0.1 copy.17
  90.5 0.1 min.12.ids_ref
  90.6 0.6 slice_bitcast_fusion.drop_ref
  91.2 12.6 %shard_map.104 = (bf16[512,128]{1,0:T(8,128)(2,1)}, bf16[512,128]{1,0:T(8,128)(2,1)}, bf16[512,128]{1,0:T(8,128)(2,1)}, bf16[512,128]{1,0:T(8,128)(2,1)}, bf16[5...) custom-call(s32[512]{0:T(512)S(1)} %min.12.ids_ref, ...), custom_call_target="tpu_custom_call" | custom-call | flops 17179869184 | bytes 10747904 | tf_op jit(solution)/shard_map/pallas_call | solution.py:432
  103.8 2.7 %collective-permute-start = (bf16[512,128]{1,0:T(8,128)(2,1)}, bf16[512,128]{1,0:T(8,128)(2,1)S(1)}, u32[]{:S(2)}, u32[]{:S(2)}) collective-permute-start(bf16[512,128]{1,0:T(8,128)(2,1)} %get-tuple-element.25), channel_id=1, source_target_pairs={{0,16},{4,20},{8,24},{12,28},{16,0},{20,4},{24,8},{28,12},{1,17},{... | collective-permute-start | bytes 393224 | tf_op jit(solution)/shard_map/ppermute | solution.py:503
  106.5 1.4 collective-permute-start.1
  108.0 3.4 %collective-permute-start.2 = (bf16[512,128]{1,0:T(8,128)(2,1)}, bf16[512,128]{1,0:T(8,128)(2,1)}, u32[]{:S(2)}, u32[]{:S(2)}) collective-permute-start(bf16[512,128]{1,0:T(8,128)(2,1)} %get-tuple-element.27), channel_id=1, source_target_pairs={{0,24},{4,28},{8,16},{12,20},{16,8},{20,12},{24,0},{28,4},{1,25},{... | collective-permute-start | bytes 393224 | tf_op jit(solution)/shard_map/ppermute | solution.py:503
  111.3 0.2 collective-permute-start.3
  111.5 16.5 %all-to-all-done.1 = bf16[32,128,128]{2,1,0:T(8,128)(2,1)} async-done(((bf16[32,128,128]{2,1,0:T(8,128)(2,1)}), bf16[32,128,128]{2,1,0:T(8,128)(2,1)}, u32[]{:S(2)}, u32[]{:S(2)}) %all-to-all-start.1) | async-done | bytes 1048608 | tf_op jit(solution)/shard_map/all_to_all | solution.py:490
  128.1 13.5 %shard_map.105 = bf16[8,1536,128]{2,1,0:T(8,128)(2,1)} custom-call(s32[512]{0:T(512)S(1)} %min.12.ids_ref, s32[512]{0:T(512)S(1)} %fusion.1.starts_ref, s32[1]{0:T(128)} %bitcast.5.first_ref, s32[1]{0:T(128)} %bitcast.6.member_ref, s32[64,8]{1,0:T(8,128)} %slice_bitcast_fusion.drop_ref, bf16[12800,128]{1,0:T(8,128)(2,1)S(1)} %bitcast.23, ...), custom_call_target="tpu_custom_call" | custom-call | flops 17179869184 | bytes 8519680 | tf_op jit(solution)/shard_map/pallas_call | solution.py:432
  141.6 0.0 copy-start
  141.6 0.0 collective-permute-done.refs_4_
  141.6 0.0 collective-permute-done.1.refs_3_
  141.6 0.0 collective-permute-done.2.refs_2_
  141.6 0.0 collective-permute-done.3.refs_1_
  141.6 3.7 %all-to-all-start.2 = ((bf16[8,1536,128]{2,1,0:T(8,128)(2,1)}), bf16[8,1536,128]{2,1,0:T(8,128)(2,1)S(1)}, u32[]{:S(2)}, u32[]{:S(2)}) async-start(bf16[8,1536,128]{2,1,0:T(8,128)(2,1)} %shard_map.105), calls=%async_computation.2 | async-start | bytes 6291456 | tf_op jit(solution)/shard_map/all_to_all | solution.py:583
  145.3 2.8 %collective-permute-start.4 = (bf16[512,128]{1,0:T(8,128)(2,1)}, bf16[512,128]{1,0:T(8,128)(2,1)S(1)}, u32[]{:S(2)}, u32[]{:S(2)}) collective-permute-start(bf16[512,128]{1,0:T(8,128)(2,1)} %get-tuple-element.35), channel_id=1, source_target_pairs={{0,12},{4,8},{8,4},{12,0},{16,28},{20,24},{24,20},{28,16},{1,13},{... | collective-permute-start | bytes 393224 | tf_op jit(solution)/shard_map/ppermute | solution.py:503
  148.1 0.5 collective-permute-start.5
  148.7 0.2 collective-permute-start.6
  148.8 52.2 %collective-permute-done.4.refs_5_ = bf16[512,128]{1,0:T(8,128)(2,1)S(1)} collective-permute-done((bf16[512,128]{1,0:T(8,128)(2,1)}, bf16[512,128]{1,0:T(8,128)(2,1)S(1)}, u32[]{:S(2)}, u32[]{:S(2)}) %collective-permute-start.4) | collective-permute-done | bytes 131104 | tf_op jit(solution)/shard_map/ppermute | solution.py:503
  201.1 1.5 collective-permute-done.5.refs_6_
  202.5 0.0 collective-permute-done.6.refs_7_
  202.6 0.0 copy-done
  202.6 2.2 %shard_map.106 = (bf16[4,2,64,1024]{3,2,1,0:T(8,128)(2,1)}, bf16[4,2,64,1024]{3,2,1,0:T(8,128)(2,1)}) custom-call(s32[1]{0:T(128)} %bitcast.6.member_ref, bf16[512,128]{1,0:T(8,128)(2,1)S(1)} %copy-done, bf16[512,128]{1,0:T(8,128)(2,1)} %collective-permute-done.3.refs_1_, bf16[512,128]{1,0:T(8,128)(2,1)} %collective-permute-done.2.refs_2_, ...), custom_call_target="tpu_custom_call" | custom-call | bytes 2097152 | tf_op jit(solution)/shard_map/pallas_call | solution.py:168
  204.8 11.0 %all-to-all-done.2.piece_ref = bf16[8,1536,128]{2,1,0:T(8,128)(2,1)S(1)} async-done(((bf16[8,1536,128]{2,1,0:T(8,128)(2,1)}), bf16[8,1536,128]{2,1,0:T(8,128)(2,1)S(1)}, u32[]{:S(2)}, u32[]{:S(2)}) %all-to-all-start.2) | async-done | bytes 3145760 | tf_op jit(solution)/shard_map/all_to_all | solution.py:583
  215.8 1.8 shard_map.107
  (9 shorter events, 0.1 us)
Async XLA Ops:
  4.5 81.6 %all-to-all-start = ((bf16[32,400,128]{2,1,0:T(8,128)(2,1)}), bf16[32,400,128]{2,1,0:T(8,128)(2,1)S(1)}, u32[]{:S(2)}, u32[]{:S(2)}) async-start(bf16[32,400,128]{2,1,0:T(8,128)(2,1)} %bitcast.24), calls=%async_computation | async-start | bytes 6553600 | tf_op jit(solution)/shard_map/all_to_all | solution.py:490
  11.8 78.5 %copy-start.1 = (s32[2]{0:T(128)S(1)}, s32[2]{0:T(128)}, u32[]{:S(2)}) copy-start(s32[2]{0:T(128)} %param.12) | copy-start | bytes 28
  86.1 42.0 %all-to-all-start.1 = ((bf16[32,128,128]{2,1,0:T(8,128)(2,1)}), bf16[32,128,128]{2,1,0:T(8,128)(2,1)}, u32[]{:S(2)}, u32[]{:S(2)}) async-start(bf16[32,128,128]{2,1,0:T(8,128)(2,1)} %bitcast.25), calls=%async_computation.1 | async-start | bytes 2097152 | tf_op jit(solution)/shard_map/all_to_all | solution.py:490
  103.8 37.7 %collective-permute-start = (bf16[512,128]{1,0:T(8,128)(2,1)}, bf16[512,128]{1,0:T(8,128)(2,1)S(1)}, u32[]{:S(2)}, u32[]{:S(2)}) collective-permute-start(bf16[512,128]{1,0:T(8,128)(2,1)} %get-tuple-element.25), channel_id=1, source_target_pairs={{0,16},{4,20},{8,24},{12,28},{16,0},{20,4},{24,8},{28,12},{1,17},{... | collective-permute-start | bytes 393224 | tf_op jit(solution)/shard_map/ppermute | solution.py:503
  106.5 35.1 %collective-permute-start.1 = (bf16[512,128]{1,0:T(8,128)(2,1)}, bf16[512,128]{1,0:T(8,128)(2,1)S(1)}, u32[]{:S(2)}, u32[]{:S(2)}) collective-permute-start(bf16[512,128]{1,0:T(8,128)(2,1)} %get-tuple-element.26), channel_id=1, source_target_pairs={{0,20},{4,16},{8,28},{12,24},{16,4},{20,0},{24,12},{28,8},{1,21},{... | collective-permute-start | bytes 393224 | tf_op jit(solution)/shard_map/ppermute | solution.py:503
  108.0 33.6 %collective-permute-start.2 = (bf16[512,128]{1,0:T(8,128)(2,1)}, bf16[512,128]{1,0:T(8,128)(2,1)}, u32[]{:S(2)}, u32[]{:S(2)}) collective-permute-start(bf16[512,128]{1,0:T(8,128)(2,1)} %get-tuple-element.27), channel_id=1, source_target_pairs={{0,24},{4,28},{8,16},{12,20},{16,8},{20,12},{24,0},{28,4},{1,25},{... | collective-permute-start | bytes 393224 | tf_op jit(solution)/shard_map/ppermute | solution.py:503
  111.3 30.3 %collective-permute-start.3 = (bf16[512,128]{1,0:T(8,128)(2,1)}, bf16[512,128]{1,0:T(8,128)(2,1)}, u32[]{:S(2)}, u32[]{:S(2)}) collective-permute-start(bf16[512,128]{1,0:T(8,128)(2,1)} %get-tuple-element.28), channel_id=1, source_target_pairs={{0,28},{4,24},{8,20},{12,16},{16,12},{20,8},{24,4},{28,0},{1,29},{... | collective-permute-start | bytes 393224 | tf_op jit(solution)/shard_map/ppermute | solution.py:503
  141.6 61.0 %copy-start = (bf16[512,128]{1,0:T(8,128)(2,1)S(1)}, bf16[512,128]{1,0:T(8,128)(2,1)}, u32[]{:S(2)}) copy-start(bf16[512,128]{1,0:T(8,128)(2,1)} %get-tuple-element.30.refs_0_) | copy-start | bytes 393220
  141.6 74.2 %all-to-all-start.2 = ((bf16[8,1536,128]{2,1,0:T(8,128)(2,1)}), bf16[8,1536,128]{2,1,0:T(8,128)(2,1)S(1)}, u32[]{:S(2)}, u32[]{:S(2)}) async-start(bf16[8,1536,128]{2,1,0:T(8,128)(2,1)} %shard_map.105), calls=%async_computation.2 | async-start | bytes 6291456 | tf_op jit(solution)/shard_map/all_to_all | solution.py:583
  145.3 55.8 %collective-permute-start.4 = (bf16[512,128]{1,0:T(8,128)(2,1)}, bf16[512,128]{1,0:T(8,128)(2,1)S(1)}, u32[]{:S(2)}, u32[]{:S(2)}) collective-permute-start(bf16[512,128]{1,0:T(8,128)(2,1)} %get-tuple-element.35), channel_id=1, source_target_pairs={{0,12},{4,8},{8,4},{12,0},{16,28},{20,24},{24,20},{28,16},{1,13},{... | collective-permute-start | bytes 393224 | tf_op jit(solution)/shard_map/ppermute | solution.py:503
  148.1 54.4 %collective-permute-start.5 = (bf16[512,128]{1,0:T(8,128)(2,1)}, bf16[512,128]{1,0:T(8,128)(2,1)S(1)}, u32[]{:S(2)}, u32[]{:S(2)}) collective-permute-start(bf16[512,128]{1,0:T(8,128)(2,1)} %get-tuple-element.36), channel_id=1, source_target_pairs={{0,8},{4,12},{8,0},{12,4},{16,24},{20,28},{24,16},{28,20},{1,9},{5... | collective-permute-start | bytes 393224 | tf_op jit(solution)/shard_map/ppermute | solution.py:503
  148.7 53.9 %collective-permute-start.6 = (bf16[512,128]{1,0:T(8,128)(2,1)}, bf16[512,128]{1,0:T(8,128)(2,1)S(1)}, u32[]{:S(2)}, u32[]{:S(2)}) collective-permute-start(bf16[512,128]{1,0:T(8,128)(2,1)} %get-tuple-element.37), channel_id=1, source_target_pairs={{0,4},{4,0},{8,12},{12,8},{16,20},{20,16},{24,28},{28,24},{1,5},{5... | collective-permute-start | bytes 393224 | tf_op jit(solution)/shard_map/ppermute | solution.py:503

commit v13 on v11

--- a/solution.py
+++ b/solution.py
@@ -13,6 +13,7 @@
 R = 3
 G = 2
 SLOTS = 3 + G + R
+OWN = 3 + R
 WIDE = SLOTS * BLOCK_TOKENS
 UNROLL = 8
 STRIP = 16
@@ -332,19 +333,30 @@
         pair = jnp.concatenate(
             [jnp.concatenate([q, none], axis=1), jnp.concatenate([none, do], axis=1)], axis=0
         )
-        terms = lax.dot_general(factors, pair, tn, preferred_element_type=jnp.float32)
-        for s in range(SLOTS):
+        terms = lax.dot_general(
+            factors[:, : OWN * BLOCK_TOKENS], pair, tn, preferred_element_type=jnp.float32
+        )
+        for s in range(OWN):
             acc[block_rows(ids_ref[j * SLOTS + s]), :] += terms[
                 s * BLOCK_TOKENS : (s + 1) * BLOCK_TOKENS
             ]
         target, pos = lax.div(i, out_steps), lax.rem(i, out_steps)
         near[target, block_rows(pos), :] = att.astype(jnp.bfloat16)
         near[target, block_rows(out_steps + pos), :] = dq.astype(jnp.bfloat16)
+        return factors[:, OWN * BLOCK_TOKENS :], pair
+
+    def finish_all(first):
+        done_blocks = [finish(first + u, u) for u in range(UNROLL)]
+        factors, pairs = [jnp.concatenate(each, axis=0) for each in zip(*done_blocks)]
+        terms = lax.dot_general(factors, pairs, tn, preferred_element_type=jnp.float32)
+        for n in range(G):
+            acc[block_rows(ids_ref[OWN + n]), :] += terms[
+                n * BLOCK_TOKENS : (n + 1) * BLOCK_TOKENS
+            ]
 
     def step(t, carry):
         scores = [score(t * UNROLL + u) for u in range(UNROLL)]
-        for u in range(UNROLL):
-            finish((t - 1) * UNROLL + u, u)
+        finish_all((t - 1) * UNROLL)
         for u in range(UNROLL):
             factor(t * UNROLL + u, u, *scores[u])
         return carry
@@ -352,8 +364,7 @@
     for u in range(UNROLL):
         factor(u, u, *score(u))
     lax.fori_loop(1, steps // UNROLL, step, 0)
-    for u in range(UNROLL):
-        finish(steps - UNROLL + u, u)
+    finish_all(steps - UNROLL)
     if has_start:
         fetch.wait()
     if joined:
@@ -524,6 +535,7 @@
         keepdims=False,
     ).astype(jnp.int32)
     drops = tables[:, :shard_blocks, :SLOTS].reshape(team_blocks, SLOTS)
+    drops = jnp.concatenate([drops[:, :3], drops[:, 3 + G :], drops[:, 3 : 3 + G]], axis=1)
     randoms = tables[:, shard_blocks : shard_blocks + R, :shard_blocks].transpose(0, 2, 1)
     randoms = randoms.reshape(team_blocks, R)
     qd = [None] + later
@@ -533,7 +545,7 @@
     blocks = first_block + jnp.arange(team_blocks, dtype=jnp.int32)
     window = jnp.stack([blocks - 1, blocks, blocks + 1], axis=1)
     listed = jnp.concatenate(
-        [window, jnp.broadcast_to(global_ids[None], (team_blocks, G)), randoms], axis=1
+        [window, randoms, jnp.broadcast_to(global_ids[None], (team_blocks, G))], axis=1
     )
     listed = jnp.clip(listed, 0, total_blocks - 1).reshape(-1)
     starts = listed // device_blocks * kv.shape[1] + listed % device_blocks * BLOCK_TOKENS

time: 217 us -> 216 us (level)
  transfers between devices with their start and end apart: 10 -> 10, of which waited for: 5 -> 5; matrix products, arithmetic and copies ran while one was open for 0% -> 1% of each run, Pallas kernels for 13% -> 13%
where the time goes in v13:
time: 216 us
  waiting for transfers between devices  153 us (71%)
  Pallas kernels  33.7 us (16%)
  starting transfers between devices  26.3 us (12%)
    all_to_all x2, waiting for transfers between devices, to_heads(): lax.all_to_all(packed, ('seq', 'head'), split_axis=0, concat_axis=0, tile...  88.5 us
    ppermute x7, waiting for transfers between devices, to_shards(): received[k] = lax.ppermute(results[k], 'seq', pairs)  53.7 us
    pallas_call x2, Pallas kernels, attend(): pl.pallas_call(functools.partial(attention_kernel, total_blocks - 1, devi...  23.6 us
    all_to_all x2, starting transfers between devices, to_heads(): lax.all_to_all(packed, ('seq', 'head'), split_axis=0, concat_axis=0, tile...  11.4 us
    ppermute x7, starting transfers between devices, to_shards(): received[k] = lax.ppermute(results[k], 'seq', pairs)  11.3 us
    all_to_all x1, waiting for transfers between devices, per_device(): rest = lax.all_to_all(rest, 'seq', split_axis=0, concat_axis=0, tiled=True)  11 us
    pallas_call x2, Pallas kernels, pack(): pl.pallas_call(functools.partial(pack_kernel, heads, groups, tuple(((at,...  6.01 us
  transfers between devices with their start and end apart: 10, of which 5 were waited for; matrix products, arithmetic and copies ran while one was open for 1% of the time, Pallas kernels for 13%

profile of v13, /device:TPU:0, one launch (start us, length us, event | category | flops | bytes accessed | tf_op | source)
XLA Modules:
  0.0 215.5 jit_solution(6107462888334382790)
XLA Ops:
  0.6 3.9 %shard_map.102 = bf16[8,4,400,128]{3,2,1,0:T(8,128)(2,1)} custom-call(s32[8,8,8]{2,1,0:T(8,128)} %refs_0_.2, s32[3,8,8]{2,1,0:T(8,128)} %bitcast.28, bf16[128,4096]{1,0:T(8,128)(2,1)} %refs_2_.1, bf16[128,4096]{1,0:T(8,128)(2,1)} %refs_3_.1, bf16[128,4096]{1,0:T(8,128)(2,1)} %refs_0_.3, bf16[128,4096]{1,0:T(8,128)(2,1)} %refs_1_.1), custom_call_target="tpu_custom_call" | custom-call | bytes 6553600 | tf_op jit(solution)/shard_map/pallas_call | solution.py:126
  4.5 7.3 %all-to-all-start = ((bf16[32,400,128]{2,1,0:T(8,128)(2,1)}), bf16[32,400,128]{2,1,0:T(8,128)(2,1)S(1)}, u32[]{:S(2)}, u32[]{:S(2)}) async-start(bf16[32,400,128]{2,1,0:T(8,128)(2,1)} %bitcast.24), calls=%async_computation | async-start | bytes 6553600 | tf_op jit(solution)/shard_map/all_to_all | solution.py:501
  11.8 0.0 copy-start.1
  11.8 2.1 shard_map.103
  14.0 72.1 %all-to-all-done = bf16[32,400,128]{2,1,0:T(8,128)(2,1)S(1)} async-done(((bf16[32,400,128]{2,1,0:T(8,128)(2,1)}), bf16[32,400,128]{2,1,0:T(8,128)(2,1)S(1)}, u32[]{:S(2)}, u32[]{:S(2)}) %all-to-all-start) | async-done | bytes 3276832 | tf_op jit(solution)/shard_map/all_to_all | solution.py:501
  86.1 4.1 %all-to-all-start.1 = ((bf16[32,128,128]{2,1,0:T(8,128)(2,1)}), bf16[32,128,128]{2,1,0:T(8,128)(2,1)}, u32[]{:S(2)}, u32[]{:S(2)}) async-start(bf16[32,128,128]{2,1,0:T(8,128)(2,1)} %bitcast.25), calls=%async_computation.1 | async-start | bytes 2097152 | tf_op jit(solution)/shard_map/all_to_all | solution.py:501
  90.2 0.1 reshape.76
  90.3 0.1 fusion.5
  90.4 0.0 copy-done.1
  90.4 0.1 broadcast_in_dim.2
  90.5 0.1 slice.29
  90.6 0.1 copy.19
  90.7 0.1 min.12.ids_ref
  90.7 0.1 copy.27
  90.8 0.1 copy.25
  90.9 0.1 copy.26
  91.0 0.7 copy.24.drop_ref
  91.7 12.2 %shard_map.104 = (bf16[512,128]{1,0:T(8,128)(2,1)}, bf16[512,128]{1,0:T(8,128)(2,1)}, bf16[512,128]{1,0:T(8,128)(2,1)}, bf16[512,128]{1,0:T(8,128)(2,1)}, bf16[5...) custom-call(s32[512]{0:T(512)S(1)} %min.12.ids_ref, ...), custom_call_target="tpu_custom_call" | custom-call | flops 17179869184 | bytes 10747904 | tf_op jit(solution)/shard_map/pallas_call | solution.py:443
  103.9 2.6 %collective-permute-start = (bf16[512,128]{1,0:T(8,128)(2,1)}, bf16[512,128]{1,0:T(8,128)(2,1)S(1)}, u32[]{:S(2)}, u32[]{:S(2)}) collective-permute-start(bf16[512,128]{1,0:T(8,128)(2,1)} %get-tuple-element.25), channel_id=1, source_target_pairs={{0,16},{4,20},{8,24},{12,28},{16,0},{20,4},{24,8},{28,12},{1,17},{... | collective-permute-start | bytes 393224 | tf_op jit(solution)/shard_map/ppermute | solution.py:514
  106.5 1.5 collective-permute-start.1
  108.0 3.3 %collective-permute-start.2 = (bf16[512,128]{1,0:T(8,128)(2,1)}, bf16[512,128]{1,0:T(8,128)(2,1)}, u32[]{:S(2)}, u32[]{:S(2)}) collective-permute-start(bf16[512,128]{1,0:T(8,128)(2,1)} %get-tuple-element.27), channel_id=1, source_target_pairs={{0,24},{4,28},{8,16},{12,20},{16,8},{20,12},{24,0},{28,4},{1,25},{... | collective-permute-start | bytes 393224 | tf_op jit(solution)/shard_map/ppermute | solution.py:514
  111.4 0.3 collective-permute-start.3
  111.6 16.5 %all-to-all-done.1 = bf16[32,128,128]{2,1,0:T(8,128)(2,1)} async-done(((bf16[32,128,128]{2,1,0:T(8,128)(2,1)}), bf16[32,128,128]{2,1,0:T(8,128)(2,1)}, u32[]{:S(2)}, u32[]{:S(2)}) %all-to-all-start.1) | async-done | bytes 1048608 | tf_op jit(solution)/shard_map/all_to_all | solution.py:501
  128.1 11.4 %shard_map.105 = bf16[8,1536,128]{2,1,0:T(8,128)(2,1)} custom-call(s32[512]{0:T(512)S(1)} %min.12.ids_ref, s32[512]{0:T(512)S(1)} %fusion.1.starts_ref, s32[1]{0:T(128)} %bitcast.5.first_ref, s32[1]{0:T(128)} %bitcast.6.member_ref, s32[64,8]{1,0:T(8,128)} %copy.24.drop_ref, bf16[12800,128]{1,0:T(8,128)(2,1)S(1)} %bitcast.23, ...), custom_call_target="tpu_custom_call" | custom-call | flops 17179869184 | bytes 8519680 | tf_op jit(solution)/shard_map/pallas_call | solution.py:443
  139.5 0.0 copy-start
  139.5 0.0 collective-permute-done.refs_4_
  139.5 0.0 collective-permute-done.1.refs_3_
  139.6 0.0 collective-permute-done.2.refs_2_
  139.6 0.0 collective-permute-done.3.refs_1_
  139.6 3.7 %all-to-all-start.2 = ((bf16[8,1536,128]{2,1,0:T(8,128)(2,1)}), bf16[8,1536,128]{2,1,0:T(8,128)(2,1)S(1)}, u32[]{:S(2)}, u32[]{:S(2)}) async-start(bf16[8,1536,128]{2,1,0:T(8,128)(2,1)} %shard_map.105), calls=%async_computation.2 | async-start | bytes 6291456 | tf_op jit(solution)/shard_map/all_to_all | solution.py:595
  143.2 2.8 %collective-permute-start.4 = (bf16[512,128]{1,0:T(8,128)(2,1)}, bf16[512,128]{1,0:T(8,128)(2,1)S(1)}, u32[]{:S(2)}, u32[]{:S(2)}) collective-permute-start(bf16[512,128]{1,0:T(8,128)(2,1)} %get-tuple-element.35), channel_id=1, source_target_pairs={{0,12},{4,8},{8,4},{12,0},{16,28},{20,24},{24,20},{28,16},{1,13},{... | collective-permute-start | bytes 393224 | tf_op jit(solution)/shard_map/ppermute | solution.py:514
  146.1 0.5 collective-permute-start.5
  146.6 0.2 collective-permute-start.6
  146.8 52.2 %collective-permute-done.4.refs_5_ = bf16[512,128]{1,0:T(8,128)(2,1)S(1)} collective-permute-done((bf16[512,128]{1,0:T(8,128)(2,1)}, bf16[512,128]{1,0:T(8,128)(2,1)S(1)}, u32[]{:S(2)}, u32[]{:S(2)}) %collective-permute-start.4) | collective-permute-done | bytes 131104 | tf_op jit(solution)/shard_map/ppermute | solution.py:514
  199.0 1.4 collective-permute-done.5.refs_6_
  200.5 0.0 collective-permute-done.6.refs_7_
  200.5 0.0 copy-done
  200.5 2.2 %shard_map.106 = (bf16[4,2,64,1024]{3,2,1,0:T(8,128)(2,1)}, bf16[4,2,64,1024]{3,2,1,0:T(8,128)(2,1)}) custom-call(s32[1]{0:T(128)} %bitcast.6.member_ref, bf16[512,128]{1,0:T(8,128)(2,1)S(1)} %copy-done, bf16[512,128]{1,0:T(8,128)(2,1)} %collective-permute-done.3.refs_1_, bf16[512,128]{1,0:T(8,128)(2,1)} %collective-permute-done.2.refs_2_, ...), custom_call_target="tpu_custom_call" | custom-call | bytes 2097152 | tf_op jit(solution)/shard_map/pallas_call | solution.py:169
  202.7 11.0 %all-to-all-done.2.piece_ref = bf16[8,1536,128]{2,1,0:T(8,128)(2,1)S(1)} async-done(((bf16[8,1536,128]{2,1,0:T(8,128)(2,1)}), bf16[8,1536,128]{2,1,0:T(8,128)(2,1)S(1)}, u32[]{:S(2)}, u32[]{:S(2)}) %all-to-all-start.2) | async-done | bytes 3145760 | tf_op jit(solution)/shard_map/all_to_all | solution.py:595
  213.7 1.8 shard_map.107
  (11 shorter events, 0.1 us)
Async XLA Ops:
  4.5 81.6 %all-to-all-start = ((bf16[32,400,128]{2,1,0:T(8,128)(2,1)}), bf16[32,400,128]{2,1,0:T(8,128)(2,1)S(1)}, u32[]{:S(2)}, u32[]{:S(2)}) async-start(bf16[32,400,128]{2,1,0:T(8,128)(2,1)} %bitcast.24), calls=%async_computation | async-start | bytes 6553600 | tf_op jit(solution)/shard_map/all_to_all | solution.py:501
  11.8 78.6 %copy-start.1 = (s32[2]{0:T(128)S(1)}, s32[2]{0:T(128)}, u32[]{:S(2)}) copy-start(s32[2]{0:T(128)} %param.12) | copy-start | bytes 28
  86.1 42.0 %all-to-all-start.1 = ((bf16[32,128,128]{2,1,0:T(8,128)(2,1)}), bf16[32,128,128]{2,1,0:T(8,128)(2,1)}, u32[]{:S(2)}, u32[]{:S(2)}) async-start(bf16[32,128,128]{2,1,0:T(8,128)(2,1)} %bitcast.25), calls=%async_computation.1 | async-start | bytes 2097152 | tf_op jit(solution)/shard_map/all_to_all | solution.py:501
  103.9 35.6 %collective-permute-start = (bf16[512,128]{1,0:T(8,128)(2,1)}, bf16[512,128]{1,0:T(8,128)(2,1)S(1)}, u32[]{:S(2)}, u32[]{:S(2)}) collective-permute-start(bf16[512,128]{1,0:T(8,128)(2,1)} %get-tuple-element.25), channel_id=1, source_target_pairs={{0,16},{4,20},{8,24},{12,28},{16,0},{20,4},{24,8},{28,12},{1,17},{... | collective-permute-start | bytes 393224 | tf_op jit(solution)/shard_map/ppermute | solution.py:514
  106.5 33.0 %collective-permute-start.1 = (bf16[512,128]{1,0:T(8,128)(2,1)}, bf16[512,128]{1,0:T(8,128)(2,1)S(1)}, u32[]{:S(2)}, u32[]{:S(2)}) collective-permute-start(bf16[512,128]{1,0:T(8,128)(2,1)} %get-tuple-element.26), channel_id=1, source_target_pairs={{0,20},{4,16},{8,28},{12,24},{16,4},{20,0},{24,12},{28,8},{1,21},{... | collective-permute-start | bytes 393224 | tf_op jit(solution)/shard_map/ppermute | solution.py:514
  108.0 31.6 %collective-permute-start.2 = (bf16[512,128]{1,0:T(8,128)(2,1)}, bf16[512,128]{1,0:T(8,128)(2,1)}, u32[]{:S(2)}, u32[]{:S(2)}) collective-permute-start(bf16[512,128]{1,0:T(8,128)(2,1)} %get-tuple-element.27), channel_id=1, source_target_pairs={{0,24},{4,28},{8,16},{12,20},{16,8},{20,12},{24,0},{28,4},{1,25},{... | collective-permute-start | bytes 393224 | tf_op jit(solution)/shard_map/ppermute | solution.py:514
  111.4 28.2 %collective-permute-start.3 = (bf16[512,128]{1,0:T(8,128)(2,1)}, bf16[512,128]{1,0:T(8,128)(2,1)}, u32[]{:S(2)}, u32[]{:S(2)}) collective-permute-start(bf16[512,128]{1,0:T(8,128)(2,1)} %get-tuple-element.28), channel_id=1, source_target_pairs={{0,28},{4,24},{8,20},{12,16},{16,12},{20,8},{24,4},{28,0},{1,29},{... | collective-permute-start | bytes 393224 | tf_op jit(solution)/shard_map/ppermute | solution.py:514
  139.5 60.9 %copy-start = (bf16[512,128]{1,0:T(8,128)(2,1)S(1)}, bf16[512,128]{1,0:T(8,128)(2,1)}, u32[]{:S(2)}) copy-start(bf16[512,128]{1,0:T(8,128)(2,1)} %get-tuple-element.30.refs_0_) | copy-start | bytes 393220
  139.6 74.1 %all-to-all-start.2 = ((bf16[8,1536,128]{2,1,0:T(8,128)(2,1)}), bf16[8,1536,128]{2,1,0:T(8,128)(2,1)S(1)}, u32[]{:S(2)}, u32[]{:S(2)}) async-start(bf16[8,1536,128]{2,1,0:T(8,128)(2,1)} %shard_map.105), calls=%async_computation.2 | async-start | bytes 6291456 | tf_op jit(solution)/shard_map/all_to_all | solution.py:595
  143.2 55.8 %collective-permute-start.4 = (bf16[512,128]{1,0:T(8,128)(2,1)}, bf16[512,128]{1,0:T(8,128)(2,1)S(1)}, u32[]{:S(2)}, u32[]{:S(2)}) collective-permute-start(bf16[512,128]{1,0:T(8,128)(2,1)} %get-tuple-element.35), channel_id=1, source_target_pairs={{0,12},{4,8},{8,4},{12,0},{16,28},{20,24},{24,20},{28,16},{1,13},{... | collective-permute-start | bytes 393224 | tf_op jit(solution)/shard_map/ppermute | solution.py:514
  146.1 54.4 %collective-permute-start.5 = (bf16[512,128]{1,0:T(8,128)(2,1)}, bf16[512,128]{1,0:T(8,128)(2,1)S(1)}, u32[]{:S(2)}, u32[]{:S(2)}) collective-permute-start(bf16[512,128]{1,0:T(8,128)(2,1)} %get-tuple-element.36), channel_id=1, source_target_pairs={{0,8},{4,12},{8,0},{12,4},{16,24},{20,28},{24,16},{28,20},{1,9},{5... | collective-permute-start | bytes 393224 | tf_op jit(solution)/shard_map/ppermute | solution.py:514
  146.6 53.8 %collective-permute-start.6 = (bf16[512,128]{1,0:T(8,128)(2,1)}, bf16[512,128]{1,0:T(8,128)(2,1)S(1)}, u32[]{:S(2)}, u32[]{:S(2)}) collective-permute-start(bf16[512,128]{1,0:T(8,128)(2,1)} %get-tuple-element.37), channel_id=1, source_target_pairs={{0,4},{4,0},{8,12},{12,8},{16,20},{20,16},{24,28},{28,24},{1,5},{5... | collective-permute-start | bytes 393224 | tf_op jit(solution)/shard_map/ppermute | solution.py:514

commit v14 on v13

--- a/solution.py
+++ b/solution.py
@@ -15,6 +15,7 @@
 SLOTS = 3 + G + R
 OWN = 3 + R
 WIDE = SLOTS * BLOCK_TOKENS
+NEAR = 4 * BLOCK_TOKENS
 UNROLL = 8
 STRIP = 16
 VMEM_LIMIT = 16 * 1024 * 1024
@@ -263,7 +264,7 @@
     if has_start:
         fetch = pltpu.make_async_copy(start_ref, earlier, start_sem)
         fetch.start()
-    lane = lax.broadcasted_iota(jnp.int32, (1, WIDE), 1)
+    lane = lax.broadcasted_iota(jnp.int32, (1, NEAR), 1)
     nt = (((1,), (1,)), ((), ()))
     tn = (((0,), (0,)), ((), ()))
     out_steps = steps // targets
@@ -313,7 +314,10 @@
         )
         keep = retain[pl.ds(j, 1), :]
         for r in range(0, BLOCK_TOKENS, STRIP):
-            part = jnp.where(absent, -jnp.inf, logits[r : r + STRIP])
+            part = logits[r : r + STRIP]
+            part = jnp.concatenate(
+                [jnp.where(absent, -jnp.inf, part[:, :NEAR]), part[:, NEAR:]], axis=1
+            )
             top = jnp.max(part, axis=-1, keepdims=True)
             expd = jnp.exp2((part - top) * (scale / math.log(2.0)))
             probs = expd * (1.0 / jnp.sum(expd, axis=-1, keepdims=True))

time: 216 us -> 216 us (level)
  no operation moved by 1% of the time
where the time goes in v14:
time: 216 us
  waiting for transfers between devices  153 us (71%)
  Pallas kernels  33.7 us (16%)
  starting transfers between devices  26.3 us (12%)
    all_to_all x2, waiting for transfers between devices, to_heads(): lax.all_to_all(packed, ('seq', 'head'), split_axis=0, concat_axis=0, tile...  88.5 us
    ppermute x7, waiting for transfers between devices, to_shards(): received[k] = lax.ppermute(results[k], 'seq', pairs)  53.7 us
    pallas_call x2, Pallas kernels, attend(): pl.pallas_call(functools.partial(attention_kernel, total_blocks - 1, devi...  23.7 us
    all_to_all x2, starting transfers between devices, to_heads(): lax.all_to_all(packed, ('seq', 'head'), split_axis=0, concat_axis=0, tile...  11.4 us
    ppermute x7, starting transfers between devices, to_shards(): received[k] = lax.ppermute(results[k], 'seq', pairs)  11.3 us
    all_to_all x1, waiting for transfers between devices, per_device(): rest = lax.all_to_all(rest, 'seq', split_axis=0, concat_axis=0, tiled=True)  11 us
    pallas_call x2, Pallas kernels, pack(): pl.pallas_call(functools.partial(pack_kernel, heads, groups, tuple(((at,...  6.01 us
  transfers between devices with their start and end apart: 10, of which 5 were waited for; matrix products, arithmetic and copies ran while one was open for 1% of the time, Pallas kernels for 13%

profile of v14, /device:TPU:0, one launch (start us, length us, event | category | flops | bytes accessed | tf_op | source)
XLA Modules:
  0.0 215.6 jit_solution(6107462888334382790)
XLA Ops:
  0.6 3.9 %shard_map.102 = bf16[8,4,400,128]{3,2,1,0:T(8,128)(2,1)} custom-call(s32[8,8,8]{2,1,0:T(8,128)} %refs_0_.2, s32[3,8,8]{2,1,0:T(8,128)} %bitcast.28, bf16[128,4096]{1,0:T(8,128)(2,1)} %refs_2_.1, bf16[128,4096]{1,0:T(8,128)(2,1)} %refs_3_.1, bf16[128,4096]{1,0:T(8,128)(2,1)} %refs_0_.3, bf16[128,4096]{1,0:T(8,128)(2,1)} %refs_1_.1), custom_call_target="tpu_custom_call" | custom-call | bytes 6553600 | tf_op jit(solution)/shard_map/pallas_call | solution.py:127
  4.5 7.3 %all-to-all-start = ((bf16[32,400,128]{2,1,0:T(8,128)(2,1)}), bf16[32,400,128]{2,1,0:T(8,128)(2,1)S(1)}, u32[]{:S(2)}, u32[]{:S(2)}) async-start(bf16[32,400,128]{2,1,0:T(8,128)(2,1)} %bitcast.24), calls=%async_computation | async-start | bytes 6553600 | tf_op jit(solution)/shard_map/all_to_all | solution.py:505
  11.8 0.0 copy-start.1
  11.8 2.1 shard_map.103
  14.0 72.1 %all-to-all-done = bf16[32,400,128]{2,1,0:T(8,128)(2,1)S(1)} async-done(((bf16[32,400,128]{2,1,0:T(8,128)(2,1)}), bf16[32,400,128]{2,1,0:T(8,128)(2,1)S(1)}, u32[]{:S(2)}, u32[]{:S(2)}) %all-to-all-start) | async-done | bytes 3276832 | tf_op jit(solution)/shard_map/all_to_all | solution.py:505
  86.1 4.1 %all-to-all-start.1 = ((bf16[32,128,128]{2,1,0:T(8,128)(2,1)}), bf16[32,128,128]{2,1,0:T(8,128)(2,1)}, u32[]{:S(2)}, u32[]{:S(2)}) async-start(bf16[32,128,128]{2,1,0:T(8,128)(2,1)} %bitcast.25), calls=%async_computation.1 | async-start | bytes 2097152 | tf_op jit(solution)/shard_map/all_to_all | solution.py:505
  90.2 0.1 reshape.76
  90.3 0.1 fusion.5
  90.4 0.0 copy-done.1
  90.4 0.1 broadcast_in_dim.2
  90.5 0.1 slice.29
  90.6 0.1 copy.19
  90.7 0.1 min.12.ids_ref
  90.7 0.1 copy.27
  90.8 0.1 copy.25
  90.9 0.1 copy.26
  91.0 0.7 copy.24.drop_ref
  91.7 12.2 %shard_map.104 = (bf16[512,128]{1,0:T(8,128)(2,1)}, bf16[512,128]{1,0:T(8,128)(2,1)}, bf16[512,128]{1,0:T(8,128)(2,1)}, bf16[512,128]{1,0:T(8,128)(2,1)}, bf16[5...) custom-call(s32[512]{0:T(512)S(1)} %min.12.ids_ref, ...), custom_call_target="tpu_custom_call" | custom-call | flops 17179869184 | bytes 10747904 | tf_op jit(solution)/shard_map/pallas_call | solution.py:447
  103.9 2.7 %collective-permute-start = (bf16[512,128]{1,0:T(8,128)(2,1)}, bf16[512,128]{1,0:T(8,128)(2,1)S(1)}, u32[]{:S(2)}, u32[]{:S(2)}) collective-permute-start(bf16[512,128]{1,0:T(8,128)(2,1)} %get-tuple-element.25), channel_id=1, source_target_pairs={{0,16},{4,20},{8,24},{12,28},{16,0},{20,4},{24,8},{28,12},{1,17},{... | collective-permute-start | bytes 393224 | tf_op jit(solution)/shard_map/ppermute | solution.py:518
  106.6 1.5 collective-permute-start.1
  108.1 3.3 %collective-permute-start.2 = (bf16[512,128]{1,0:T(8,128)(2,1)}, bf16[512,128]{1,0:T(8,128)(2,1)}, u32[]{:S(2)}, u32[]{:S(2)}) collective-permute-start(bf16[512,128]{1,0:T(8,128)(2,1)} %get-tuple-element.27), channel_id=1, source_target_pairs={{0,24},{4,28},{8,16},{12,20},{16,8},{20,12},{24,0},{28,4},{1,25},{... | collective-permute-start | bytes 393224 | tf_op jit(solution)/shard_map/ppermute | solution.py:518
  111.4 0.2 collective-permute-start.3
  111.6 16.5 %all-to-all-done.1 = bf16[32,128,128]{2,1,0:T(8,128)(2,1)} async-done(((bf16[32,128,128]{2,1,0:T(8,128)(2,1)}), bf16[32,128,128]{2,1,0:T(8,128)(2,1)}, u32[]{:S(2)}, u32[]{:S(2)}) %all-to-all-start.1) | async-done | bytes 1048608 | tf_op jit(solution)/shard_map/all_to_all | solution.py:505
  128.1 11.5 %shard_map.105 = bf16[8,1536,128]{2,1,0:T(8,128)(2,1)} custom-call(s32[512]{0:T(512)S(1)} %min.12.ids_ref, s32[512]{0:T(512)S(1)} %fusion.1.starts_ref, s32[1]{0:T(128)} %bitcast.5.first_ref, s32[1]{0:T(128)} %bitcast.6.member_ref, s32[64,8]{1,0:T(8,128)} %copy.24.drop_ref, bf16[12800,128]{1,0:T(8,128)(2,1)S(1)} %bitcast.23, ...), custom_call_target="tpu_custom_call" | custom-call | flops 17179869184 | bytes 8519680 | tf_op jit(solution)/shard_map/pallas_call | solution.py:447
  139.5 0.0 copy-start
  139.6 0.0 collective-permute-done.refs_4_
  139.6 0.0 collective-permute-done.1.refs_3_
  139.6 0.0 collective-permute-done.2.refs_2_
  139.6 0.0 collective-permute-done.3.refs_1_
  139.6 3.7 %all-to-all-start.2 = ((bf16[8,1536,128]{2,1,0:T(8,128)(2,1)}), bf16[8,1536,128]{2,1,0:T(8,128)(2,1)S(1)}, u32[]{:S(2)}, u32[]{:S(2)}) async-start(bf16[8,1536,128]{2,1,0:T(8,128)(2,1)} %shard_map.105), calls=%async_computation.2 | async-start | bytes 6291456 | tf_op jit(solution)/shard_map/all_to_all | solution.py:599
  143.3 2.8 %collective-permute-start.4 = (bf16[512,128]{1,0:T(8,128)(2,1)}, bf16[512,128]{1,0:T(8,128)(2,1)S(1)}, u32[]{:S(2)}, u32[]{:S(2)}) collective-permute-start(bf16[512,128]{1,0:T(8,128)(2,1)} %get-tuple-element.35), channel_id=1, source_target_pairs={{0,12},{4,8},{8,4},{12,0},{16,28},{20,24},{24,20},{28,16},{1,13},{... | collective-permute-start | bytes 393224 | tf_op jit(solution)/shard_map/ppermute | solution.py:518
  146.1 0.5 collective-permute-start.5
  146.7 0.2 collective-permute-start.6
  146.8 52.2 %collective-permute-done.4.refs_5_ = bf16[512,128]{1,0:T(8,128)(2,1)S(1)} collective-permute-done((bf16[512,128]{1,0:T(8,128)(2,1)}, bf16[512,128]{1,0:T(8,128)(2,1)S(1)}, u32[]{:S(2)}, u32[]{:S(2)}) %collective-permute-start.4) | collective-permute-done | bytes 131104 | tf_op jit(solution)/shard_map/ppermute | solution.py:518
  199.1 1.5 collective-permute-done.5.refs_6_
  200.5 0.0 collective-permute-done.6.refs_7_
  200.5 0.0 copy-done
  200.5 2.2 %shard_map.106 = (bf16[4,2,64,1024]{3,2,1,0:T(8,128)(2,1)}, bf16[4,2,64,1024]{3,2,1,0:T(8,128)(2,1)}) custom-call(s32[1]{0:T(128)} %bitcast.6.member_ref, bf16[512,128]{1,0:T(8,128)(2,1)S(1)} %copy-done, bf16[512,128]{1,0:T(8,128)(2,1)} %collective-permute-done.3.refs_1_, bf16[512,128]{1,0:T(8,128)(2,1)} %collective-permute-done.2.refs_2_, ...), custom_call_target="tpu_custom_call" | custom-call | bytes 2097152 | tf_op jit(solution)/shard_map/pallas_call | solution.py:170
  202.8 11.0 %all-to-all-done.2.piece_ref = bf16[8,1536,128]{2,1,0:T(8,128)(2,1)S(1)} async-done(((bf16[8,1536,128]{2,1,0:T(8,128)(2,1)}), bf16[8,1536,128]{2,1,0:T(8,128)(2,1)S(1)}, u32[]{:S(2)}, u32[]{:S(2)}) %all-to-all-start.2) | async-done | bytes 3145760 | tf_op jit(solution)/shard_map/all_to_all | solution.py:599
  213.8 1.8 shard_map.107
  (11 shorter events, 0.1 us)
Async XLA Ops:
  4.5 81.6 %all-to-all-start = ((bf16[32,400,128]{2,1,0:T(8,128)(2,1)}), bf16[32,400,128]{2,1,0:T(8,128)(2,1)S(1)}, u32[]{:S(2)}, u32[]{:S(2)}) async-start(bf16[32,400,128]{2,1,0:T(8,128)(2,1)} %bitcast.24), calls=%async_computation | async-start | bytes 6553600 | tf_op jit(solution)/shard_map/all_to_all | solution.py:505
  11.8 78.6 %copy-start.1 = (s32[2]{0:T(128)S(1)}, s32[2]{0:T(128)}, u32[]{:S(2)}) copy-start(s32[2]{0:T(128)} %param.12) | copy-start | bytes 28
  86.1 42.0 %all-to-all-start.1 = ((bf16[32,128,128]{2,1,0:T(8,128)(2,1)}), bf16[32,128,128]{2,1,0:T(8,128)(2,1)}, u32[]{:S(2)}, u32[]{:S(2)}) async-start(bf16[32,128,128]{2,1,0:T(8,128)(2,1)} %bitcast.25), calls=%async_computation.1 | async-start | bytes 2097152 | tf_op jit(solution)/shard_map/all_to_all | solution.py:505
  103.9 35.7 %collective-permute-start = (bf16[512,128]{1,0:T(8,128)(2,1)}, bf16[512,128]{1,0:T(8,128)(2,1)S(1)}, u32[]{:S(2)}, u32[]{:S(2)}) collective-permute-start(bf16[512,128]{1,0:T(8,128)(2,1)} %get-tuple-element.25), channel_id=1, source_target_pairs={{0,16},{4,20},{8,24},{12,28},{16,0},{20,4},{24,8},{28,12},{1,17},{... | collective-permute-start | bytes 393224 | tf_op jit(solution)/shard_map/ppermute | solution.py:518
  106.6 33.0 %collective-permute-start.1 = (bf16[512,128]{1,0:T(8,128)(2,1)}, bf16[512,128]{1,0:T(8,128)(2,1)S(1)}, u32[]{:S(2)}, u32[]{:S(2)}) collective-permute-start(bf16[512,128]{1,0:T(8,128)(2,1)} %get-tuple-element.26), channel_id=1, source_target_pairs={{0,20},{4,16},{8,28},{12,24},{16,4},{20,0},{24,12},{28,8},{1,21},{... | collective-permute-start | bytes 393224 | tf_op jit(solution)/shard_map/ppermute | solution.py:518
  108.1 31.5 %collective-permute-start.2 = (bf16[512,128]{1,0:T(8,128)(2,1)}, bf16[512,128]{1,0:T(8,128)(2,1)}, u32[]{:S(2)}, u32[]{:S(2)}) collective-permute-start(bf16[512,128]{1,0:T(8,128)(2,1)} %get-tuple-element.27), channel_id=1, source_target_pairs={{0,24},{4,28},{8,16},{12,20},{16,8},{20,12},{24,0},{28,4},{1,25},{... | collective-permute-start | bytes 393224 | tf_op jit(solution)/shard_map/ppermute | solution.py:518
  111.4 28.2 %collective-permute-start.3 = (bf16[512,128]{1,0:T(8,128)(2,1)}, bf16[512,128]{1,0:T(8,128)(2,1)}, u32[]{:S(2)}, u32[]{:S(2)}) collective-permute-start(bf16[512,128]{1,0:T(8,128)(2,1)} %get-tuple-element.28), channel_id=1, source_target_pairs={{0,28},{4,24},{8,20},{12,16},{16,12},{20,8},{24,4},{28,0},{1,29},{... | collective-permute-start | bytes 393224 | tf_op jit(solution)/shard_map/ppermute | solution.py:518
  139.5 61.0 %copy-start = (bf16[512,128]{1,0:T(8,128)(2,1)S(1)}, bf16[512,128]{1,0:T(8,128)(2,1)}, u32[]{:S(2)}) copy-start(bf16[512,128]{1,0:T(8,128)(2,1)} %get-tuple-element.30.refs_0_) | copy-start | bytes 393220
  139.6 74.2 %all-to-all-start.2 = ((bf16[8,1536,128]{2,1,0:T(8,128)(2,1)}), bf16[8,1536,128]{2,1,0:T(8,128)(2,1)S(1)}, u32[]{:S(2)}, u32[]{:S(2)}) async-start(bf16[8,1536,128]{2,1,0:T(8,128)(2,1)} %shard_map.105), calls=%async_computation.2 | async-start | bytes 6291456 | tf_op jit(solution)/shard_map/all_to_all | solution.py:599
  143.3 55.8 %collective-permute-start.4 = (bf16[512,128]{1,0:T(8,128)(2,1)}, bf16[512,128]{1,0:T(8,128)(2,1)S(1)}, u32[]{:S(2)}, u32[]{:S(2)}) collective-permute-start(bf16[512,128]{1,0:T(8,128)(2,1)} %get-tuple-element.35), channel_id=1, source_target_pairs={{0,12},{4,8},{8,4},{12,0},{16,28},{20,24},{24,20},{28,16},{1,13},{... | collective-permute-start | bytes 393224 | tf_op jit(solution)/shard_map/ppermute | solution.py:518
  146.1 54.4 %collective-permute-start.5 = (bf16[512,128]{1,0:T(8,128)(2,1)}, bf16[512,128]{1,0:T(8,128)(2,1)S(1)}, u32[]{:S(2)}, u32[]{:S(2)}) collective-permute-start(bf16[512,128]{1,0:T(8,128)(2,1)} %get-tuple-element.36), channel_id=1, source_target_pairs={{0,8},{4,12},{8,0},{12,4},{16,24},{20,28},{24,16},{28,20},{1,9},{5... | collective-permute-start | bytes 393224 | tf_op jit(solution)/shard_map/ppermute | solution.py:518
  146.7 53.9 %collective-permute-start.6 = (bf16[512,128]{1,0:T(8,128)(2,1)}, bf16[512,128]{1,0:T(8,128)(2,1)S(1)}, u32[]{:S(2)}, u32[]{:S(2)}) collective-permute-start(bf16[512,128]{1,0:T(8,128)(2,1)} %get-tuple-element.37), channel_id=1, source_target_pairs={{0,4},{4,0},{8,12},{12,8},{16,20},{20,16},{24,28},{28,24},{1,5},{5... | collective-permute-start | bytes 393224 | tf_op jit(solution)/shard_map/ppermute | solution.py:518
